TPU v7x, 32 devices: a whole 2x2x4 slice. The times are simulated.
32 devices in a mesh: dp: 16 (over z, y, core), rows: 2 (over x).
Axes of the slice: x: 2, y: 2, z: 4, core: 2. Of those that a mesh axis runs over, the one named last changes fastest.
Arguments:
- features: bfloat16 [16, 32, 32, 768], P('dp', 'rows'), may hold values from -6 to 6
- bucket: int32 [16], P('dp'), may hold values from 0 to 16, as said below
- kernel: float32 [7, 7, 768], replicated, may hold values from -0.875 to 0.875
- up_weight: bfloat16 [768, 2816], P('dp'), may hold values from -0.21875 to 0.21875
- down_weight: bfloat16 [2816, 768], P('dp'), may hold values from -0.109375 to 0.109375
- cotangent: bfloat16 [16, 32, 32, 768], P('dp', 'rows'), may hold values from -6 to 6
Outputs:
- block_out: bfloat16 [16, 32, 32, 768], P('dp', 'rows')
- feature_grad: bfloat16 [16, 32, 32, 768], P('dp', 'rows')
- up_grad: float32 [768, 2816], P('dp')
- down_grad: float32 [2816, 768], P('dp')
- kernel_grad: float32 [7, 7, 768], replicated
Inputs may be any that keep to these rules, and one draw needn't show every extreme that they name: `bucket`: both ends of the range occur in every draw.
All inputs are finite; a program needn't handle non-finite values.
Results may differ from a plain program's by a relative error of at most 0.0075.
Values may be sent and summed in bfloat16 or wider, within the bound.
A program may use at most 128 MiB of HBM per device.

v0:
```python
import jax
import jax.numpy as jnp
from jax import lax
from jax.sharding import PartitionSpec as P

INV_ROOT_TWO = 0.7071067811865476
INV_ROOT_TAU = 0.3989422804014327
EPSILON = 1e-06


def padded_2(block, sides, width):
    for axis, dim in sides:
        count = lax.axis_size(axis)
        forward = [(i, i + 1) for i in range(count - 1)]
        backward = [(target, source) for source, target in forward]
        low = lax.ppermute(
            lax.slice_in_dim(block, block.shape[dim] - width, None, axis=dim), axis, forward
        )
        high = lax.ppermute(lax.slice_in_dim(block, 0, width, axis=dim), axis, backward)
        block = jnp.concatenate([low, block, high], axis=dim)
    return block


def gelu_parts(pre_act):
    normal_cdf = 0.5 * (1.0 + lax.erf(pre_act * INV_ROOT_TWO))
    density = jnp.exp(-0.5 * pre_act * pre_act) * INV_ROOT_TAU
    return (pre_act * normal_cdf, normal_cdf + pre_act * density)


def depthwise(padded, kernel, out_rows, out_cols, flipped):
    span = kernel.shape[0]
    result = jnp.zeros(padded.shape[:-3] + (out_rows, out_cols, padded.shape[-1]), jnp.float32)
    for offset_row in range(span):
        for offset_col in range(span):
            start_row = span - 1 - offset_row if flipped else offset_row
            start_col = span - 1 - offset_col if flipped else offset_col
            result = (
                result
                + kernel[offset_row, offset_col]
                * padded[..., start_row : start_row + out_rows, start_col : start_col + out_cols, :]
            )
    return result


def kernel_terms(grad_conv, padded, span):
    reduce_axes = tuple(range(grad_conv.ndim - 1))
    rows_out = grad_conv.shape[-3]
    cols_out = grad_conv.shape[-2]
    kernel_rows = []
    for offset_row in range(span):
        kernel_row = []
        for offset_col in range(span):
            window = padded[
                ..., offset_row : offset_row + rows_out, offset_col : offset_col + cols_out, :
            ]
            kernel_row.append(jnp.sum(grad_conv * window, axis=reduce_axes))
        kernel_rows.append(jnp.stack(kernel_row))
    return jnp.stack(kernel_rows)


def layer_norm(convolved):
    centered = convolved - jnp.mean(convolved, axis=-1, keepdims=True)
    inv_std = lax.rsqrt(jnp.mean(centered * centered, axis=-1, keepdims=True) + EPSILON)
    return (centered * inv_std, inv_std)


def norm_backward(grad_norm, unit_norm, inv_std):
    first_mean = jnp.mean(grad_norm, axis=-1, keepdims=True)
    second_mean = jnp.mean(grad_norm * unit_norm, axis=-1, keepdims=True)
    return inv_std * (grad_norm - first_mean - unit_norm * second_mean)


def pointwise(tokens, cot_rows, up_full, down_full):
    pre_act = jnp.dot(tokens, up_full, preferred_element_type=jnp.float32)
    hidden, derivative = gelu_parts(pre_act)
    activation = hidden.astype(jnp.bfloat16)
    branch = jnp.dot(activation, down_full, preferred_element_type=jnp.float32)
    grad_act = lax.dot_general(
        cot_rows, down_full, (((1,), (1,)), ((), ())), preferred_element_type=jnp.float32
    )
    grad_pre = (grad_act * derivative).astype(jnp.bfloat16)
    grad_norm = lax.dot_general(
        grad_pre, up_full, (((1,), (1,)), ((), ())), preferred_element_type=jnp.float32
    )
    return (activation, branch, grad_pre, grad_norm)


def on_device(features, bucket, kernel, up_weight, down_weight, cotangent):
    images, strip_rows, canvas_cols, channels = features.shape
    rows_count = lax.axis_size("rows")
    row_index = lax.axis_index("rows")
    canvas_rows = strip_rows * rows_count
    area_cells = canvas_rows * canvas_cols // 2
    reach = kernel.shape[0] // 2
    grad_scale = 1.0 / (images * lax.axis_size("dp"))
    heights = canvas_rows // 2 + bucket
    widths = jnp.minimum(canvas_cols, area_cells // heights)
    row_ids = row_index * strip_rows + lax.iota(jnp.int32, strip_rows)
    col_ids = lax.iota(jnp.int32, canvas_cols)
    inside = (row_ids[None, :, None] < heights[:, None, None]) & (
        col_ids[None, None, :] < widths[:, None, None]
    )
    inside_cells = inside[..., None]
    masked = jnp.where(inside_cells, features, jnp.zeros((), features.dtype))
    masked_cot = jnp.where(inside_cells, cotangent, jnp.zeros((), cotangent.dtype))
    up_full, down_full = (
        lax.all_gather(up_weight, "dp", axis=0, tiled=True),
        lax.all_gather(down_weight, "dp", axis=0, tiled=True),
    )
    rimmed = padded_2(masked, (("rows", 1),), reach)
    padded = jnp.pad(rimmed, ((0, 0), (0, 0), (reach, reach), (0, 0)))
    convolved = jnp.where(
        inside_cells, depthwise(padded, kernel, strip_rows, canvas_cols, False), 0.0
    )
    unit_norm, inv_std = layer_norm(convolved)
    normed = unit_norm.astype(jnp.bfloat16)
    tokens = normed.reshape(images * strip_rows * canvas_cols, channels)
    cot_rows = masked_cot.reshape(images * strip_rows * canvas_cols, channels)
    activation, branch_rows, grad_pre, grad_rows = pointwise(tokens, cot_rows, up_full, down_full)
    branch = branch_rows.reshape(features.shape)
    grad_norm = grad_rows.reshape(features.shape)
    block_out = (masked + branch).astype(jnp.bfloat16)
    grad_conv = jnp.where(inside_cells, norm_backward(grad_norm, unit_norm, inv_std), 0.0)
    kernel_grad = lax.psum(
        kernel_terms(grad_conv, padded, kernel.shape[0]) * grad_scale, ("dp", "rows")
    )
    grad_rimmed = padded_2(grad_conv.astype(jnp.bfloat16), (("rows", 1),), reach).astype(
        grad_conv.dtype
    )
    grad_padded = jnp.pad(grad_rimmed, ((0, 0), (0, 0), (reach, reach), (0, 0)))
    feature_grad = jnp.where(
        inside_cells,
        masked_cot + depthwise(grad_padded, kernel, strip_rows, canvas_cols, True),
        0.0,
    ).astype(jnp.bfloat16)
    columns = tokens
    up_part = lax.psum_scatter(
        lax.dot_general(
            columns, grad_pre, (((0,), (0,)), ((), ())), preferred_element_type=jnp.float32
        )
        * grad_scale,
        "dp",
        scatter_dimension=0,
        tiled=True,
    )
    columns = activation
    down_part = lax.psum_scatter(
        lax.dot_general(
            columns, cot_rows, (((0,), (0,)), ((), ())), preferred_element_type=jnp.float32
        )
        * grad_scale,
        "dp",
        scatter_dimension=0,
        tiled=True,
    )
    up_half, down_half = (
        lax.psum_scatter(
            up_part.astype(jnp.bfloat16), "rows", scatter_dimension=0, tiled=True
        ).astype(jnp.float32),
        lax.psum_scatter(
            down_part.astype(jnp.bfloat16), "rows", scatter_dimension=0, tiled=True
        ).astype(jnp.float32),
    )
    up_grad, down_grad = (
        lax.all_gather(up_half.astype(jnp.bfloat16), "rows", axis=0, tiled=True).astype(
            up_half.dtype
        ),
        lax.all_gather(down_half.astype(jnp.bfloat16), "rows", axis=0, tiled=True).astype(
            down_half.dtype
        ),
    )
    return (block_out, feature_grad, up_grad, down_grad, kernel_grad)


def solution(mesh):
    placed = (
        P("dp", "rows", None, None),
        P("dp"),
        P(),
        P("dp", None),
        P("dp", None),
        P("dp", "rows", None, None),
    )
    return jax.shard_map(
        on_device,
        mesh=mesh,
        in_specs=placed,
        out_specs=(
            P("dp", "rows", None, None),
            P("dp", "rows", None, None),
            P("dp", None),
            P("dp", None),
            P(),
        ),
        check_vma=False,
    )
```

profile of v0, /device:TPU:0, one launch (start us, length us, event | category | flops | bytes accessed | tf_op | source)
XLA Modules:
  0.0 502.4 jit_solution(509236760290077369)
XLA Ops:
  9.5 2.5 broadcast_select_fusion
  12.0 4.9 collective-permute-start
  19.9 4.1 collective-permute-done.1
  24.6 15.5 %fusion.209 = (f32[16,32]{1,0:T(8,128)S(1)}, f32[1,16,32,768]{3,2,1,0:T(8,128)S(1)}) fusion(bf16[1,22,38,768]{3,2,1,0:T(8,128)(2,1)S(1)} %fusion.203, f32[768]{0:T(1024)S(1)} %get-tuple-element.104, f32[768]{0:T(1024)S(1)} %get-tuple-element.105, f32[768]{0:T(1024)S(1)} %get-tuple-element.58, bf16[1,3,32,768]{3,2,1,0:T(8,128)(2,1)S(1)} %collective-permute-done.1, ...), kind=kLoop, calls=%fused_computation.445 | loop fusion | flops 60554752 | bytes 35837440 | tf_op jit(solution)/shard_map/reduce_sum | solution.py:62
  41.6 22.7 %all-gather.3.cloned.1.call-done = bf16[768,2816]{1,0:T(8,128)(2,1)} async-done(((bf16[48,2816]{1,0:T(8,128)(2,1)}), bf16[768,2816]{1,0:T(8,128)(2,1)}) %all-gather.3.cloned.1.call-update) | async-done | bytes 4325392 | tf_op jit(solution)/shard_map/all_gather | solution.py:107
  64.3 6.4 %multiply_convert_fusion = (bf16[512,2816]{1,0:T(8,128)(2,1)S(1)}, f32[512,2816]{1,0:T(8,128)}) fusion(bf16[512,768]{1,0:T(8,128)(2,1)} %bitcast.42, bf16[768,2816]{1,0:T(8,128)(2,1)} %all-gather.3.cloned.1.call-done), kind=kOutput, calls=%fused_computation.51 | convolution fusion | flops 2221801472 | bytes 13762560 | tf_op jit(solution)/shard_map/dot_general | solution.py:74
  72.3 5.8 %convolution_multiply_fusion = f32[2816,768]{1,0:T(8,128)} fusion(bf16[512,2816]{1,0:T(8,128)(2,1)S(1)} %get-tuple-element.119, bf16[512,768]{1,0:T(8,128)(2,1)S(1)} %bitcast.41), kind=kOutput, calls=%fused_computation.43 | convolution fusion | flops 2216755200 | bytes 12320768 | tf_op jit(solution)/shard_map/dot_general | solution.py:148
  78.3 38.1 %all-gather.5.cloned.1.call-done = bf16[2816,768]{1,0:T(8,128)(2,1)} async-done(((bf16[176,768]{1,0:T(8,128)(2,1)}), bf16[2816,768]{1,0:T(8,128)(2,1)}) %all-gather.5.cloned.1.call-update) | async-done | bytes 4325392 | tf_op jit(solution)/shard_map/all_gather | solution.py:108
  116.4 7.7 %fusion.5 = bf16[512,2816]{1,0:T(8,128)(2,1)} fusion(f32[512,2816]{1,0:T(8,128)} %get-tuple-element.120, bf16[512,768]{1,0:T(8,128)(2,1)} %bitcast.40, bf16[2816,768]{1,0:T(8,128)(2,1)} %all-gather.5.cloned.1.call-done), kind=kOutput, calls=%fused_computation.50 | convolution fusion | flops 2229010432 | bytes 13762560 | tf_op jit(solution)/shard_map/dot_general | solution.py:78
  124.1 8.1 %convolution_multiply_fusion.1 = f32[768,2816]{1,0:T(8,128)} fusion(bf16[512,768]{1,0:T(8,128)(2,1)S(1)} %bitcast.43, bf16[512,2816]{1,0:T(8,128)(2,1)} %fusion.5), kind=kOutput, calls=%fused_computation.44 | convolution fusion | flops 2216755200 | bytes 12320768 | tf_op jit(solution)/shard_map/dot_general | solution.py:138
  132.3 7.4 %fusion.213 = (f32[512]{0:T(512)S(1)}, f32[512,768]{1,0:T(8,128)}) fusion(bf16[512,2816]{1,0:T(8,128)(2,1)} %fusion.5, bf16[768,2816]{1,0:T(8,128)(2,1)} %all-gather.3.cloned.1.call-done), kind=kOutput, calls=%fused_computation.448 | convolution fusion | flops 2214985216 | bytes 8783872 | tf_op jit(solution)/shard_map/dot_general | solution.py:82
  139.8 2.1 multiply_reduce_fusion
  141.9 4.7 fusion.102
  146.7 4.1 fusion.99
  152.2 4.0 fusion.81
  156.4 3.4 collective-permute-start.2
  161.3 64.9 %reduce-scatter.9.cloned.1.call-done = f32[176,768]{1,0:T(8,128)} async-done(((f32[2816,768]{1,0:T(8,128)}), f32[176,768]{1,0:T(8,128)}) %reduce-scatter.9.cloned.1.call-update) | async-done | bytes 540688 | tf_op jit(solution)/shard_map/reduce_scatter | solution.py:147
  228.5 108.7 %reduce-scatter.5.cloned.1.call-done = f32[48,2816]{1,0:T(8,128)} async-done(((f32[768,2816]{1,0:T(8,128)}), f32[48,2816]{1,0:T(8,128)}) %reduce-scatter.5.cloned.1.call-update) | async-done | bytes 540688 | tf_op jit(solution)/shard_map/reduce_scatter | solution.py:137
  337.2 1.8 convert_element_type.306
  341.2 12.5 %fusion.194 = bf16[1,16,32,768]{3,2,1,0:T(8,128)(2,1)} fusion(f32[1,22,32,768]{3,2,1,0:T(8,128)S(1)} %maximum_convert_fusion, f32[768]{0:T(1024)S(1)} %get-tuple-element.104, f32[768]{0:T(1024)S(1)} %get-tuple-element.105, f32[768]{0:T(1024)S(1)} %get-tuple-element.58, f32[768]{0:T(1024)S(1)} %get-tuple-element.59, f32[768]{0:T(1024)S(1)} %get-tuple-element.60, ...), kind=kLoop, calls=%fused_computation.342 | loop fusion | flops 40108032 | bytes 14948352 | tf_op jit(solution)/shard_map/convert_element_type | solution.py:135
  353.7 6.2 %all_gather.15 = bf16[176,768]{1,0:T(8,128)(2,1)S(1)} all-gather(bf16[88,768]{1,0:T(8,128)(2,1)} %reduce-scatter.11.cloned.1.call-done), channel_id=1, replica_groups=mesh['dp'=16,'rows'=2] {'rows'}, dimensions={0}, use_global_device_ids=true | all-gather | bytes 405504 | tf_op jit(solution)/shard_map/all_gather | solution.py:168
  360.8 5.1 %reduce-scatter.7.cloned.1.call-done = bf16[24,2816]{1,0:T(8,128)(2,1)} async-done(((bf16[48,2816]{1,0:T(8,128)(2,1)}), bf16[24,2816]{1,0:T(8,128)(2,1)}) %reduce-scatter.7.cloned.1.call-update) | async-done | bytes 135184 | tf_op jit(solution)/shard_map/reduce_scatter | solution.py:157
  365.9 6.2 %all_gather.14 = bf16[48,2816]{1,0:T(8,128)(2,1)S(1)} all-gather(bf16[24,2816]{1,0:T(8,128)(2,1)} %reduce-scatter.7.cloned.1.call-done), channel_id=1, replica_groups=mesh['dp'=16,'rows'=2] {'rows'}, dimensions={0}, use_global_device_ids=true | all-gather | bytes 405504 | tf_op jit(solution)/shard_map/all_gather | solution.py:165
  372.9 121.0 %all-reduce.4.cloned.1.call-done = f32[7,7,768]{2,1,0:T(8,128)} async-done(((f32[7,7,768]{2,1,0:T(8,128)}), f32[7,7,768]{2,1,0:T(8,128)}) %all-reduce.4.cloned.1.call-update) | async-done | bytes 150544 | tf_op jit(solution)/shard_map/psum | solution.py:124
  (129 shorter events, 19.0 us)
Async XLA Ops:
  7.2 57.1 %all-gather.3.cloned.1.call-start = ((), (), s32[]{:S(2)}) async-start(), calls=%async_computation.4 | async-start | bytes 4595712 | tf_op jit(solution)/shard_map/all_gather | solution.py:107
  7.9 108.5 %all-gather.5.cloned.1.call-start = ((), (), s32[]{:S(2)}) async-start(), calls=%async_computation.5 | async-start | bytes 4595712 | tf_op jit(solution)/shard_map/all_gather | solution.py:108
  8.6 217.6 %reduce-scatter.9.cloned.1.call-start = ((), (), s32[]{:S(2)}) async-start(), calls=%async_computation.8 | async-start | bytes 9191424 | tf_op jit(solution)/shard_map/reduce_scatter | solution.py:147
  9.5 8.7 %copy-start.8 = (f32[7,7,768]{2,1,0:T(8,128)S(1)}, f32[7,7,768]{2,1,0:T(8,128)}, u32[]{:S(2)}) copy-start(f32[7,7,768]{2,1,0:T(8,128)} %param.8) | copy-start | bytes 451588
  11.9 12.7 %copy-start = (bf16[1,16,32,768]{3,2,1,0:T(8,128)(2,1)}, bf16[1,16,32,768]{3,2,1,0:T(8,128)(2,1)S(1)}, u32[]{:S(2)}) copy-start(bf16[1,16,32,768]{3,2,1,0:T(8,128)(2,1)S(1)} %get-tuple-element.116) | copy-start | bytes 2359300
  12.0 7.9 %collective-permute-start = (bf16[1,3,32,768]{3,2,1,0:T(8,128)(2,1)S(1)}, bf16[1,3,32,768]{3,2,1,0:T(8,128)(2,1)S(1)}, u32[]{:S(2)}, u32[]{:S(2)}) collective-permute-start(bf16[1,3,32,768]{3,2,1,0:T(8,128)(2,1)S(1)} %get-tuple-element.113), channel_id=1, source_target_pairs={{0,1},{2,3},{4,5},{6,7},{8,9},{10,11},{12,13},{14,15},{16,17},{18,... | collective-permute-start | bytes 442376 | tf_op jit(solution)/shard_map/ppermute | solution.py:16
  16.8 7.2 %collective-permute-start.1 = (bf16[1,3,32,768]{3,2,1,0:T(8,128)(2,1)S(1)}, bf16[1,3,32,768]{3,2,1,0:T(8,128)(2,1)S(1)}, u32[]{:S(2)}, u32[]{:S(2)}) collective-permute-start(bf16[1,3,32,768]{3,2,1,0:T(8,128)(2,1)S(1)} %get-tuple-element.114), channel_id=1, source_target_pairs={{1,0},{3,2},{5,4},{7,6},{9,8},{11,10},{13,12},{15,14},{17,16},{19,... | collective-permute-start | bytes 442376 | tf_op jit(solution)/shard_map/ppermute | solution.py:19
  64.3 8.0 %copy-start.4 = (bf16[1,16,32,768]{3,2,1,0:T(8,128)(2,1)S(1)}, bf16[1,16,32,768]{3,2,1,0:T(8,128)(2,1)}, u32[]{:S(2)}) copy-start(bf16[1,16,32,768]{3,2,1,0:T(8,128)(2,1)} %get-tuple-element.115) | copy-start | bytes 2359300
  70.7 1.6 copy-start.6
  78.1 259.1 %reduce-scatter.5.cloned.1.call-start = ((), (), s32[]{:S(2)}) async-start(), calls=%async_computation.6 | async-start | bytes 9191424 | tf_op jit(solution)/shard_map/reduce_scatter | solution.py:137
  116.4 7.7 %copy-start.5 = (bf16[1,16,32,768]{3,2,1,0:T(8,128)(2,1)S(1)}, bf16[1,16,32,768]{3,2,1,0:T(8,128)(2,1)}, u32[]{:S(2)}) copy-start(bf16[1,16,32,768]{3,2,1,0:T(8,128)(2,1)} %fusion.204) | copy-start | bytes 2359300
  132.3 221.5 %reduce-scatter.11.cloned.1.call-start = ((), (), s32[]{:S(2)}) async-start(), calls=%async_computation.9 | async-start | bytes 405504 | tf_op jit(solution)/shard_map/reduce_scatter | solution.py:160
  139.8 2.1 copy-start.2
  139.8 6.9 %slice-start = ((s8[4325376]{0:T(1024)(128)(4,1)}), s8[4194304]{0:T(1024)(128)(4,1)S(1)}, s32[]{:S(2)}) async-start(s8[4325376]{0:T(1024)(128)(4,1)} %bitcast.44), calls=%async_computation.11 | async-start | bytes 8388608
  141.9 4.8 copy-start.1
  141.9 4.8 copy-start.7
  141.9 4.8 slice-start.1
  156.4 183.7 %collective-permute-start.2 = (bf16[1,3,32,768]{3,2,1,0:T(8,128)(2,1)S(1)}, bf16[1,3,32,768]{3,2,1,0:T(8,128)(2,1)S(1)}, u32[]{:S(2)}, u32[]{:S(2)}) collective-permute-start(bf16[1,3,32,768]{3,2,1,0:T(8,128)(2,1)S(1)} %get-tuple-element.111), channel_id=1, source_target_pairs={{0,1},{2,3},{4,5},{6,7},{8,9},{10,11},{12,13},{14,15},{16,17},{18,... | collective-permute-start | bytes 442376 | tf_op jit(solution)/shard_map/ppermute | solution.py:16
  159.9 180.3 %collective-permute-start.3 = (bf16[1,3,32,768]{3,2,1,0:T(8,128)(2,1)S(1)}, bf16[1,3,32,768]{3,2,1,0:T(8,128)(2,1)S(1)}, u32[]{:S(2)}, u32[]{:S(2)}) collective-permute-start(bf16[1,3,32,768]{3,2,1,0:T(8,128)(2,1)S(1)} %get-tuple-element.112), channel_id=1, source_target_pairs={{1,0},{3,2},{5,4},{7,6},{9,8},{11,10},{13,12},{15,14},{17,16},{19,... | collective-permute-start | bytes 442376 | tf_op jit(solution)/shard_map/ppermute | solution.py:19
  228.0 137.9 %reduce-scatter.7.cloned.1.call-start = ((), (), s32[]{:S(2)}) async-start(), calls=%async_computation.7 | async-start | bytes 405504 | tf_op jit(solution)/shard_map/reduce_scatter | solution.py:157
  339.0 155.0 %all-reduce.4.cloned.1.call-start = ((), (), s32[]{:S(2)}) async-start(), calls=%async_computation.10 | async-start | bytes 344064 | tf_op jit(solution)/shard_map/psum | solution.py:124
  340.1 1.1 copy-start.3
Sparse Core Ops, SparseCore 0:
  10.3 53.9 all-gather.2
  66.6 49.7 all-gather.4
  120.4 105.7 reduce-scatter.8
  230.1 106.9 reduce-scatter.4
  339.8 11.4 reduce-scatter.10
  354.1 11.7 reduce-scatter.6
  372.0 121.9 all-reduce.3
where the time goes:
time: 504 us; the launch traced here: 502 us
  waiting for transfers between devices  367 us (73%)
  other arithmetic  50.8 us (10%)
  matrix products  39.5 us (8%)
  between operations  15.5 us (3%)
  blocking collectives  12.4 us (2%)
  starting transfers between devices  11.6 us (2%)
  local copies, waits for them, and re-layouts  5.23 us (1%)
    psum x1, waiting for transfers between devices, on_device(): lax.psum(kernel_terms(grad_conv, padded, kernel.shape[0]) * grad_scale, (...  121 us
    reduce_scatter x1, waiting for transfers between devices, on_device(): lax.psum_scatter(lax.dot_general(columns, grad_pre, (((0,), (0,)), ((), (...  109 us
    reduce_scatter x1, waiting for transfers between devices, on_device(): lax.psum_scatter(lax.dot_general(columns, cot_rows, (((0,), (0,)), ((), (...  64.9 us
    all_gather x1, waiting for transfers between devices, on_device(): lax.all_gather(down_weight, 'dp', axis=0, tiled=True)  38.1 us
    all_gather x1, waiting for transfers between devices, on_device(): lax.all_gather(up_weight, 'dp', axis=0, tiled=True)  22.7 us
    reduce_sum x1, other arithmetic, layer_norm(): centered = convolved - jnp.mean(convolved, axis=-1, keepdims=True)  15.5 us
    convert_element_type x1, other arithmetic, on_device(): feature_grad = jnp.where(inside_cells, masked_cot + depthwise(grad_padded...  12.5 us
  transfers between devices with their start and end apart: 11, of which 8 were waited for; matrix products, arithmetic and copies ran while one was open for 18% of the time, Pallas kernels for 0%

commit v1 on v0

--- a/solution.py
+++ b/solution.py
@@ -70,6 +70,67 @@
     return inv_std * (grad_norm - first_mean - unit_norm * second_mean)
 
 
+def partner(values, bit):
+    count = lax.axis_size("dp")
+    return lax.ppermute(values, "dp", [(i, i ^ bit) for i in range(count)])
+
+
+def other_row(values):
+    return lax.ppermute(values, "rows", [(0, 1), (1, 0)])
+
+
+def pick(values, which, axis):
+    return lax.dynamic_index_in_dim(values, which, axis, keepdims=False)
+
+
+def halved_dp(slices, bits, bit):
+    at = bits.index(bit)
+    low = 1 << (len(bits) - 1 - at)
+    grouped = slices.reshape((slices.shape[0] // (2 * low), 2, low) + slices.shape[1:])
+    mine = (lax.axis_index("dp") // bit) % 2
+    sent = pick(grouped, 1 - mine, 1).astype(jnp.bfloat16)
+    total = pick(grouped, mine, 1) + partner(sent, bit).astype(jnp.float32)
+    return total.reshape((slices.shape[0] // 2,) + slices.shape[1:]), [b for b in bits if b != bit]
+
+
+def halved_rows(slices):
+    half = slices.shape[-1] // 2
+    mine = lax.axis_index("rows")
+    sent = lax.dynamic_slice_in_dim(slices, (1 - mine) * half, half, axis=2).astype(jnp.bfloat16)
+    kept = lax.dynamic_slice_in_dim(slices, mine * half, half, axis=2)
+    return kept + other_row(sent).astype(jnp.float32)
+
+
+def joined_rows(half):
+    sent = half.astype(jnp.bfloat16)
+    other = other_row(sent)
+    first = lax.axis_index("rows") == 0
+    return jnp.concatenate(
+        [jnp.where(first, sent, other), jnp.where(first, other, sent)], axis=-1
+    ).astype(jnp.float32)
+
+
+def scattered(partial, order):
+    count = lax.axis_size("dp")
+    slices = partial.reshape(count, partial.shape[0] // count, partial.shape[1])
+    bits = [1 << k for k in reversed(range(count.bit_length() - 1))]
+    for stage in order:
+        if stage == "rows":
+            slices = halved_rows(slices)
+        else:
+            slices, bits = halved_dp(slices, bits, stage)
+    return joined_rows(slices[0])
+
+
+def summed_everywhere(values):
+    count = lax.axis_size("dp")
+    bit = 1
+    while bit < count:
+        values = values + partner(values, bit)
+        bit *= 2
+    return values + other_row(values)
+
+
 def pointwise(tokens, cot_rows, up_full, down_full):
     pre_act = jnp.dot(tokens, up_full, preferred_element_type=jnp.float32)
     hidden, derivative = gelu_parts(pre_act)
@@ -121,8 +182,8 @@
     grad_norm = grad_rows.reshape(features.shape)
     block_out = (masked + branch).astype(jnp.bfloat16)
     grad_conv = jnp.where(inside_cells, norm_backward(grad_norm, unit_norm, inv_std), 0.0)
-    kernel_grad = lax.psum(
-        kernel_terms(grad_conv, padded, kernel.shape[0]) * grad_scale, ("dp", "rows")
+    kernel_grad = summed_everywhere(
+        kernel_terms(grad_conv, padded, kernel.shape[0]) * grad_scale
     )
     grad_rimmed = padded_2(grad_conv.astype(jnp.bfloat16), (("rows", 1),), reach).astype(
         grad_conv.dtype
@@ -133,41 +194,20 @@
         masked_cot + depthwise(grad_padded, kernel, strip_rows, canvas_cols, True),
         0.0,
     ).astype(jnp.bfloat16)
-    columns = tokens
-    up_part = lax.psum_scatter(
+    dp_bits = [1 << k for k in range(lax.axis_size("dp").bit_length() - 1)]
+    down_grad = scattered(
         lax.dot_general(
-            columns, grad_pre, (((0,), (0,)), ((), ())), preferred_element_type=jnp.float32
+            activation, cot_rows, (((0,), (0,)), ((), ())), preferred_element_type=jnp.float32
         )
         * grad_scale,
-        "dp",
-        scatter_dimension=0,
-        tiled=True,
-    )
-    columns = activation
-    down_part = lax.psum_scatter(
+        dp_bits + ["rows"],
+    )
+    up_grad = scattered(
         lax.dot_general(
-            columns, cot_rows, (((0,), (0,)), ((), ())), preferred_element_type=jnp.float32
+            tokens, grad_pre, (((0,), (0,)), ((), ())), preferred_element_type=jnp.float32
         )
         * grad_scale,
-        "dp",
-        scatter_dimension=0,
-        tiled=True,
-    )
-    up_half, down_half = (
-        lax.psum_scatter(
-            up_part.astype(jnp.bfloat16), "rows", scatter_dimension=0, tiled=True
-        ).astype(jnp.float32),
-        lax.psum_scatter(
-            down_part.astype(jnp.bfloat16), "rows", scatter_dimension=0, tiled=True
-        ).astype(jnp.float32),
-    )
-    up_grad, down_grad = (
-        lax.all_gather(up_half.astype(jnp.bfloat16), "rows", axis=0, tiled=True).astype(
-            up_half.dtype
-        ),
-        lax.all_gather(down_half.astype(jnp.bfloat16), "rows", axis=0, tiled=True).astype(
-            down_half.dtype
-        ),
+        dp_bits[:1] + ["rows"] + dp_bits[2:] + dp_bits[1:2],
     )
     return (block_out, feature_grad, up_grad, down_grad, kernel_grad)
 

time: 504 us -> 266 us (0.53)
  waiting for transfers between devices: 367 us -> 122 us
  starting transfers between devices: 11.6 us -> 27 us
  matrix products: 39.5 us -> 25.3 us
  blocking collectives: 12.4 us -> 0 us
  other arithmetic: 50.8 us -> 60.8 us
  local copies, waits for them, and re-layouts: 5.23 us -> 13.1 us
    reduce_scatter x4 -> x0, waiting for transfers between devices: 179 us -> none  [the longest x1 109 us: on_device(): lax.psum_scatter(lax.dot_general(columns, grad_pre, (((0,), (0,)), ((), (...]
    psum x1 -> x0, waiting for transfers between devices: 121 us -> none  [on_device(): lax.psum(kernel_terms(grad_conv, padded, kernel.shape[0]) * grad_scale, (...]
    ppermute x0 -> x17, waiting for transfers between devices: none -> 29.2 us  [the longest x12 25.7 us: partner(): return lax.ppermute(values, 'dp', [(i, i ^ bit) for i in range(count)])]
    ppermute x2, waiting for transfers between devices: 1.33 us -> 18.9 us  [padded_2(): lax.ppermute(lax.slice_in_dim(block, block.shape[dim] - width, None, axis...]
    ppermute x0 -> x17, starting transfers between devices: none -> 17.1 us  [the longest x12 12 us: partner(): return lax.ppermute(values, 'dp', [(i, i ^ bit) for i in range(count)])]
    add x0 -> x13, other arithmetic: none -> 13.5 us  [the longest x7 10.3 us: halved_dp(): total = pick(grouped, mine, 1) + partner(sent, bit).astype(jnp.float32)]
    all_gather x2 -> x0, blocking collectives: 12.4 us -> none  [the longest x1 6.23 us: on_device(): lax.all_gather(down_half.astype(jnp.bfloat16), 'rows', axis=0, tiled=True)]
    dot_general x2, matrix products: 13.9 us -> 4.96 us  [the longest x1 2.49 us: on_device(): lax.dot_general(activation, cot_rows, (((0,), (0,)), ((), ())), preferred...]
  transfers between devices with their start and end apart: 11 -> 23, of which waited for: 8 -> 13; matrix products, arithmetic and copies ran while one was open for 18% -> 23% of each run, Pallas kernels for 0% -> 0%
where the time goes in v1:
time: 266 us; the launch traced here: 265 us
  waiting for transfers between devices  122 us (46%)
  other arithmetic  60.8 us (23%)
  starting transfers between devices  27 us (10%)
  matrix products  25.3 us (10%)
  between operations  16.4 us (6%)
  local copies, waits for them, and re-layouts  13.1 us (5%)
    all_gather x1, waiting for transfers between devices, on_device(): lax.all_gather(down_weight, 'dp', axis=0, tiled=True)  45.4 us
    ppermute x12, waiting for transfers between devices, partner(): return lax.ppermute(values, 'dp', [(i, i ^ bit) for i in range(count)])  25.7 us
    all_gather x1, waiting for transfers between devices, on_device(): lax.all_gather(up_weight, 'dp', axis=0, tiled=True)  22.5 us
    ppermute x2, waiting for transfers between devices, padded_2(): lax.ppermute(lax.slice_in_dim(block, block.shape[dim] - width, None, axis...  18.9 us
    reduce_sum x1, other arithmetic, layer_norm(): centered = convolved - jnp.mean(convolved, axis=-1, keepdims=True)  15.4 us
    convert_element_type x1, other arithmetic, on_device(): feature_grad = jnp.where(inside_cells, masked_cot + depthwise(grad_padded...  12.9 us
    ppermute x12, starting transfers between devices, partner(): return lax.ppermute(values, 'dp', [(i, i ^ bit) for i in range(count)])  12 us
    reduce_sum x3, other arithmetic, kernel_terms(): kernel_row.append(jnp.sum(grad_conv * window, axis=reduce_axes))  11.2 us
  transfers between devices with their start and end apart: 23, of which 13 were waited for; matrix products, arithmetic and copies ran while one was open for 23% of the time, Pallas kernels for 0%

profile of v1, /device:TPU:0, one launch (start us, length us, event | category | flops | bytes accessed | tf_op | source)
XLA Modules:
  0.0 265.1 jit_solution(2824931682859398757)
XLA Ops:
  9.4 2.5 broadcast_select_fusion
  11.9 4.9 %collective-permute-start = (bf16[1,3,32,768]{3,2,1,0:T(8,128)(2,1)S(1)}, bf16[1,3,32,768]{3,2,1,0:T(8,128)(2,1)S(1)}, u32[]{:S(2)}, u32[]{:S(2)}) collective-permute-start(bf16[1,3,32,768]{3,2,1,0:T(8,128)(2,1)S(1)} %get-tuple-element.113), channel_id=1, source_target_pairs={{0,1},{2,3},{4,5},{6,7},{8,9},{10,11},{12,13},{14,15},{16,17},{18,... | collective-permute-start | bytes 442376 | tf_op jit(solution)/shard_map/ppermute | solution.py:16
  19.9 4.1 %collective-permute-done.1 = bf16[1,3,32,768]{3,2,1,0:T(8,128)(2,1)S(1)} collective-permute-done((bf16[1,3,32,768]{3,2,1,0:T(8,128)(2,1)S(1)}, bf16[1,3,32,768]{3,2,1,0:T(8,128)(2,1)S(1)}, u32[]{:S(2)}, u32[]{:S(2)}) %collective-permute-start.1) | collective-permute-done | bytes 147488 | tf_op jit(solution)/shard_map/ppermute | solution.py:19
  24.6 15.4 %fusion.220 = (f32[16,32]{1,0:T(8,128)S(1)}, f32[1,16,32,768]{3,2,1,0:T(8,128)S(1)}) fusion(bf16[1,22,38,768]{3,2,1,0:T(8,128)(2,1)S(1)} %fusion.205, f32[768]{0:T(1024)S(1)} %get-tuple-element.104, f32[768]{0:T(1024)S(1)} %get-tuple-element.105, f32[768]{0:T(1024)S(1)} %get-tuple-element.58, bf16[1,3,32,768]{3,2,1,0:T(8,128)(2,1)S(1)} %collective-permute-done.1, ...), kind=kLoop, calls=%fused_computation.482 | loop fusion | flops 60554752 | bytes 35837440 | tf_op jit(solution)/shard_map/reduce_sum | solution.py:62
  41.8 22.5 %all-gather.3.cloned.1.call-done = bf16[768,2816]{1,0:T(8,128)(2,1)} async-done(((bf16[48,2816]{1,0:T(8,128)(2,1)}), bf16[768,2816]{1,0:T(8,128)(2,1)}) %all-gather.3.cloned.1.call-update) | async-done | bytes 4325392 | tf_op jit(solution)/shard_map/all_gather | solution.py:168
  64.3 6.7 %multiply_convert_fusion = (bf16[512,2816]{1,0:T(8,128)(2,1)}, f32[512,2816]{1,0:T(8,128)}) fusion(bf16[512,768]{1,0:T(8,128)(2,1)} %bitcast.101, bf16[768,2816]{1,0:T(8,128)(2,1)} %all-gather.3.cloned.1.call-done), kind=kOutput, calls=%fused_computation.51 | convolution fusion | flops 2221801472 | bytes 13762560 | tf_op jit(solution)/shard_map/dot_general | solution.py:135
  71.0 45.4 %all-gather.5.cloned.1.call-done = bf16[2816,768]{1,0:T(8,128)(2,1)} async-done(((bf16[176,768]{1,0:T(8,128)(2,1)}), bf16[2816,768]{1,0:T(8,128)(2,1)}) %all-gather.5.cloned.1.call-update) | async-done | bytes 4325392 | tf_op jit(solution)/shard_map/all_gather | solution.py:169
  116.3 6.6 %fusion.5 = bf16[512,2816]{1,0:T(8,128)(2,1)S(1)} fusion(f32[512,2816]{1,0:T(8,128)} %get-tuple-element.124, bf16[512,768]{1,0:T(8,128)(2,1)} %bitcast.99, bf16[2816,768]{1,0:T(8,128)(2,1)} %all-gather.5.cloned.1.call-done), kind=kOutput, calls=%fused_computation.50 | convolution fusion | flops 2229010432 | bytes 13762560 | tf_op jit(solution)/shard_map/dot_general | solution.py:139
  123.0 2.5 fusion.224
  126.8 5.7 %fusion.104 = (f32[768]{0:T(1024)S(1)}, f32[768]{0:T(1024)S(1)}, f32[768]{0:T(1024)S(1)}, f32[768]{0:T(1024)S(1)}, f32[768]{0:T(1024)S(1)}, /*index=5*/f32[768]{...) fusion(bf16[1,22,38,768]{3,2,1,0:T(8,128)(2,1)S(1)} %fusion.205, ...), kind=kLoop, calls=%fused_computation.260 | loop fusion | flops 23972352 | bytes 18938368 | tf_op jit(solution)/shard_map/reduce_sum | solution.py:56
  132.4 4.2 %fusion.83 = (f32[768]{0:T(1024)S(1)}, f32[768]{0:T(1024)S(1)}, f32[768]{0:T(1024)S(1)}, f32[768]{0:T(1024)S(1)}, f32[768]{0:T(1024)S(1)}, /*index=5*/f32[768]{0...) fusion(f32[1,16,32,768]{3,2,1,0:T(8,128)S(1)} %get-tuple-elemen, ...), kind=kLoop, calls=%fused_computation.239 | loop fusion | flops 21613056 | bytes 16570368 | tf_op jit(solution)/shard_map/reduce_sum | solution.py:56
  138.7 2.5 convolution_multiply_fusion.1
  141.3 2.5 convolution_multiply_fusion
  143.8 4.5 %fusion.101 = (f32[768]{0:T(1024)S(1)}, f32[768]{0:T(1024)S(1)}, f32[768]{0:T(1024)S(1)}, f32[768]{0:T(1024)S(1)}, f32[768]{0:T(1024)S(1)}, /*index=5*/f32[768]{...) fusion(f32[1,16,32,768]{3,2,1,0:T(8,128)S(1)} %get-tuple-element.106, ...), kind=kOutput, calls=%fused_computation.257 | convolution fusion | flops 2225990400 | bytes 10671104 | tf_op jit(solution)/shard_map/dot_general | solution.py:138
  156.0 3.4 %bitcast_add_fusion = f32[8,1,176,768]{3,2,0,1:T(8,128)S(1)} fusion(bf16[8,1,176,768]{3,2,0,1:T(8,128)(2,1)} %collective-permute-done.10, f32[8,2,1,176,768]{4,3,1,0,2:T(8,128)} %bitcast.91, s32[]{:T(128)S(6)} %select_n.148), kind=kLoop, calls=%fused_computation.55 | loop fusion | flops 2162688 | bytes 10813444 | tf_op jit(solution)/shard_map/add | solution.py:92
  170.8 2.5 collective-permute-start.2
  176.4 18.6 %collective-permute-done.2 = bf16[1,3,32,768]{3,2,1,0:T(8,128)(2,1)S(1)} collective-permute-done((bf16[1,3,32,768]{3,2,1,0:T(8,128)(2,1)}, bf16[1,3,32,768]{3,2,1,0:T(8,128)(2,1)S(1)}, u32[]{:S(2)}, u32[]{:S(2)}) %collective-permute-start.2) | collective-permute-done | bytes 147488 | tf_op jit(solution)/shard_map/ppermute | solution.py:16
  198.5 2.3 bitcast_add_fusion.2
  206.3 12.9 %fusion.196 = bf16[1,16,32,768]{3,2,1,0:T(8,128)(2,1)} fusion(f32[1,22,32,768]{3,2,1,0:T(8,128)S(1)} %maximum_convert_fusion, f32[768]{0:T(1024)} %copy-done.52, f32[768]{0:T(1024)} %copy-done.53, f32[768]{0:T(1024)S(1)} %get-tuple-element.58, f32[768]{0:T(1024)S(1)} %get-tuple-element.59, f32[768]{0:T(1024)S(1)} %copy-done.16, f32[768]{0:T(1024)S(1)} %copy-done.18, ...), kind=kLoop, calls=%fused_computation.352 | loop fusion | flops 40108032 | bytes 14913536 | tf_op jit(solution)/shard_map/convert_element_type | solution.py:196
  224.0 6.9 %collective-permute-done.6 = bf16[2,2,48,1408]{3,2,1,0:T(8,128)(2,1)} collective-permute-done((bf16[2,2,48,1408]{3,2,1,0:T(8,128)(2,1)}, bf16[2,2,48,1408]{3,2,1,0:T(8,128)(2,1)}, u32[]{:S(2)}, u32[]{:S(2)}) %collective-permute-start.6) | collective-permute-done | bytes 540704 | tf_op jit(solution)/shard_map/ppermute | solution.py:75
  232.3 10.7 %collective-permute-done.13 = bf16[1,1,176,768]{3,2,0,1:T(8,128)(2,1)S(1)} collective-permute-done((bf16[1,1,176,768]{3,2,0,1:T(8,128)(2,1)S(1)}, bf16[1,1,176,768]{3,2,0,1:T(8,128)(2,1)S(1)}, u32[]{:S(2)}, u32[]{:S(2)}) %collective-permute-start.13) | collective-permute-done | bytes 270368 | tf_op jit(solution)/shard_map/ppermute | solution.py:75
  243.8 3.3 %collective-permute-done.7 = bf16[1,2,48,1408]{3,2,1,0:T(8,128)(2,1)S(1)} collective-permute-done((bf16[1,2,48,1408]{3,2,1,0:T(8,128)(2,1)S(1)}, bf16[1,2,48,1408]{3,2,1,0:T(8,128)(2,1)S(1)}, u32[]{:S(2)}, u32[]{:S(2)}) %collective-permute-start.7) | collective-permute-done | bytes 270368 | tf_op jit(solution)/shard_map/ppermute | solution.py:75
  249.5 2.8 %collective-permute-done.8 = bf16[1,1,48,1408]{3,2,1,0:T(8,128)(2,1)S(1)} collective-permute-done((bf16[1,1,48,1408]{3,2,1,0:T(8,128)(2,1)S(1)}, bf16[1,1,48,1408]{3,2,1,0:T(8,128)(2,1)S(1)}, u32[]{:S(2)}, u32[]{:S(2)}) %collective-permute-start.8) | collective-permute-done | bytes 135200 | tf_op jit(solution)/shard_map/ppermute | solution.py:75
  253.1 2.1 collective-permute-done.15
  (284 shorter events, 53.3 us)
Async XLA Ops:
  7.2 57.1 %all-gather.3.cloned.1.call-start = ((), (), s32[]{:S(2)}) async-start(), calls=%async_computation | async-start | bytes 4595712 | tf_op jit(solution)/shard_map/all_gather | solution.py:168
  7.9 108.4 %all-gather.5.cloned.1.call-start = ((), (), s32[]{:S(2)}) async-start(), calls=%async_computation.1 | async-start | bytes 4595712 | tf_op jit(solution)/shard_map/all_gather | solution.py:169
  11.9 7.9 %collective-permute-start = (bf16[1,3,32,768]{3,2,1,0:T(8,128)(2,1)S(1)}, bf16[1,3,32,768]{3,2,1,0:T(8,128)(2,1)S(1)}, u32[]{:S(2)}, u32[]{:S(2)}) collective-permute-start(bf16[1,3,32,768]{3,2,1,0:T(8,128)(2,1)S(1)} %get-tuple-element.113), channel_id=1, source_target_pairs={{0,1},{2,3},{4,5},{6,7},{8,9},{10,11},{12,13},{14,15},{16,17},{18,... | collective-permute-start | bytes 442376 | tf_op jit(solution)/shard_map/ppermute | solution.py:16
  16.8 7.2 %collective-permute-start.1 = (bf16[1,3,32,768]{3,2,1,0:T(8,128)(2,1)S(1)}, bf16[1,3,32,768]{3,2,1,0:T(8,128)(2,1)S(1)}, u32[]{:S(2)}, u32[]{:S(2)}) collective-permute-start(bf16[1,3,32,768]{3,2,1,0:T(8,128)(2,1)S(1)} %get-tuple-element.114), channel_id=1, source_target_pairs={{1,0},{3,2},{5,4},{7,6},{9,8},{11,10},{13,12},{15,14},{17,16},{19,... | collective-permute-start | bytes 442376 | tf_op jit(solution)/shard_map/ppermute | solution.py:19
  18.3 21.7 %copy-start.15 = (f32[768]{0:T(1024)}, f32[768]{0:T(1024)S(1)}, u32[]{:S(2)}) copy-start(f32[768]{0:T(1024)S(1)} %get-tuple-element.60) | copy-start | bytes 9220
  150.6 5.4 %collective-permute-start.10 = (bf16[8,1,176,768]{3,2,0,1:T(8,128)(2,1)}, bf16[8,1,176,768]{3,2,0,1:T(8,128)(2,1)}, u32[]{:S(2)}, u32[]{:S(2)}) collective-permute-start(bf16[8,1,176,768]{3,2,0,1:T(8,128)(2,1)} %fusion.8), channel_id=1, source_target_pairs={{0,2},{2,0},{4,6},{6,4},{8,10},{10,8},{12,14},{14,12},{16,18},{18,... | collective-permute-start | bytes 6488072 | tf_op jit(solution)/shard_map/ppermute | solution.py:75
  152.4 8.7 %collective-permute-start.4 = (bf16[8,1,48,2816]{3,2,0,1:T(8,128)(2,1)}, bf16[8,1,48,2816]{3,2,0,1:T(8,128)(2,1)}, u32[]{:S(2)}, u32[]{:S(2)}) collective-permute-start(bf16[8,1,48,2816]{3,2,0,1:T(8,128)(2,1)} %fusion.7), channel_id=1, source_target_pairs={{0,2},{2,0},{4,6},{6,4},{8,10},{10,8},{12,14},{14,12},{16,18},{18,... | collective-permute-start | bytes 6488072 | tf_op jit(solution)/shard_map/ppermute | solution.py:75
  153.1 2.2 collective-permute-start.16
  155.3 13.1 %collective-permute-start.17 = (f32[7,7,768]{2,1,0:T(8,128)S(1)}, f32[7,7,768]{2,1,0:T(8,128)S(1)}, u32[]{:S(2)}, u32[]{:S(2)}) collective-permute-start(f32[7,7,768]{2,1,0:T(8,128)S(1)} %fusion.219), channel_id=1, source_target_pairs={{0,4},{2,6},{4,0},{6,2},{8,12},{10,14},{12,8},{14,10},{16,20},{18,... | collective-permute-start | bytes 451592 | tf_op jit(solution)/shard_map/ppermute | solution.py:75
  159.6 39.0 %collective-permute-start.11 = (bf16[4,1,176,768]{3,2,0,1:T(8,128)(2,1)S(1)}, bf16[4,1,176,768]{3,2,0,1:T(8,128)(2,1)}, u32[]{:S(2)}, u32[]{:S(2)}) collective-permute-start(bf16[4,1,176,768]{3,2,0,1:T(8,128)(2,1)S(1)} %fusion.208), channel_id=1, source_target_pairs={{0,4},{2,6},{4,0},{6,2},{8,12},{10,14},{12,8},{14,10},{16,20},{18,... | collective-permute-start | bytes 3244040 | tf_op jit(solution)/shard_map/ppermute | solution.py:75
  167.0 36.4 %collective-permute-start.5 = (bf16[8,48,1408]{2,1,0:T(8,128)(2,1)S(1)}, bf16[8,48,1408]{2,1,0:T(8,128)(2,1)}, u32[]{:S(2)}, u32[]{:S(2)}) collective-permute-start(bf16[8,48,1408]{2,1,0:T(8,128)(2,1)S(1)} %fusion.207), channel_id=1, source_target_pairs={{0,1},{1,0},{2,3},{3,2},{4,5},{5,4},{6,7},{7,6},{8,9},{9,8},{10,11... | collective-permute-start | bytes 3244040 | tf_op jit(solution)/shard_map/ppermute | solution.py:79
  168.5 6.2 %collective-permute-start.18 = (f32[7,7,768]{2,1,0:T(8,128)S(1)}, f32[7,7,768]{2,1,0:T(8,128)S(1)}, u32[]{:S(2)}, u32[]{:S(2)}) collective-permute-start(f32[7,7,768]{2,1,0:T(8,128)S(1)} %add.587), channel_id=1, source_target_pairs={{0,8},{2,10},{4,12},{6,14},{8,0},{10,2},{12,4},{14,6},{16,24},{18,... | collective-permute-start | bytes 451592 | tf_op jit(solution)/shard_map/ppermute | solution.py:75
  170.8 24.2 %collective-permute-start.2 = (bf16[1,3,32,768]{3,2,1,0:T(8,128)(2,1)}, bf16[1,3,32,768]{3,2,1,0:T(8,128)(2,1)S(1)}, u32[]{:S(2)}, u32[]{:S(2)}) collective-permute-start(bf16[1,3,32,768]{3,2,1,0:T(8,128)(2,1)} %get-tuple-element.111), channel_id=1, source_target_pairs={{0,1},{2,3},{4,5},{6,7},{8,9},{10,11},{12,13},{14,15},{16,17},{18,... | collective-permute-start | bytes 442376 | tf_op jit(solution)/shard_map/ppermute | solution.py:16
  173.2 22.8 %collective-permute-start.3 = (bf16[1,3,32,768]{3,2,1,0:T(8,128)(2,1)}, bf16[1,3,32,768]{3,2,1,0:T(8,128)(2,1)}, u32[]{:S(2)}, u32[]{:S(2)}) collective-permute-start(bf16[1,3,32,768]{3,2,1,0:T(8,128)(2,1)} %get-tuple-element.112), channel_id=1, source_target_pairs={{1,0},{3,2},{5,4},{7,6},{9,8},{11,10},{13,12},{15,14},{17,16},{19,... | collective-permute-start | bytes 442376 | tf_op jit(solution)/shard_map/ppermute | solution.py:19
  174.6 22.4 %collective-permute-start.19 = (f32[7,7,768]{2,1,0:T(8,128)S(1)}, f32[7,7,768]{2,1,0:T(8,128)S(1)}, u32[]{:S(2)}, u32[]{:S(2)}) collective-permute-start(f32[7,7,768]{2,1,0:T(8,128)S(1)} %add.588), channel_id=1, source_target_pairs={{0,16},{2,18},{4,20},{6,22},{8,24},{10,26},{12,28},{14,30},{16,0},... | collective-permute-start | bytes 451592 | tf_op jit(solution)/shard_map/ppermute | solution.py:75
  197.1 22.1 %collective-permute-start.20 = (f32[7,7,768]{2,1,0:T(8,128)S(1)}, f32[7,7,768]{2,1,0:T(8,128)}, u32[]{:S(2)}, u32[]{:S(2)}) collective-permute-start(f32[7,7,768]{2,1,0:T(8,128)S(1)} %add.589), channel_id=1, source_target_pairs={{0,1},{1,0},{2,3},{3,2},{4,5},{5,4},{6,7},{7,6},{8,9},{9,8},{10,11... | collective-permute-start | bytes 451592 | tf_op jit(solution)/shard_map/ppermute | solution.py:79
  201.8 19.1 %collective-permute-start.12 = (bf16[2,1,176,768]{3,2,0,1:T(8,128)(2,1)}, bf16[2,1,176,768]{3,2,0,1:T(8,128)(2,1)}, u32[]{:S(2)}, u32[]{:S(2)}) collective-permute-start(bf16[2,1,176,768]{3,2,0,1:T(8,128)(2,1)} %fusion.214), channel_id=1, source_target_pairs={{0,8},{2,10},{4,12},{6,14},{8,0},{10,2},{12,4},{14,6},{16,24},{18,... | collective-permute-start | bytes 1622024 | tf_op jit(solution)/shard_map/ppermute | solution.py:75
  205.7 25.1 %collective-permute-start.6 = (bf16[2,2,48,1408]{3,2,1,0:T(8,128)(2,1)}, bf16[2,2,48,1408]{3,2,1,0:T(8,128)(2,1)}, u32[]{:S(2)}, u32[]{:S(2)}) collective-permute-start(bf16[2,2,48,1408]{3,2,1,0:T(8,128)(2,1)} %fusion.213), channel_id=1, source_target_pairs={{0,8},{2,10},{4,12},{6,14},{8,0},{10,2},{12,4},{14,6},{16,24},{18,... | collective-permute-start | bytes 1622024 | tf_op jit(solution)/shard_map/ppermute | solution.py:75
  222.1 21.0 %collective-permute-start.13 = (bf16[1,1,176,768]{3,2,0,1:T(8,128)(2,1)S(1)}, bf16[1,1,176,768]{3,2,0,1:T(8,128)(2,1)S(1)}, u32[]{:S(2)}, u32[]{:S(2)}) collective-permute-start(bf16[1,1,176,768]{3,2,0,1:T(8,128)(2,1)S(1)} %dynamic-slice_convert_fusion.4), channel_id=1, source_target_pairs={{0,16},{2,18},{4,20},{6,22},{8,24},{10,26},{12,28},{14,30},{16,0},... | collective-permute-start | bytes 811016 | tf_op jit(solution)/shard_map/ppermute | solution.py:75
  232.1 15.1 %collective-permute-start.7 = (bf16[1,2,48,1408]{3,2,1,0:T(8,128)(2,1)S(1)}, bf16[1,2,48,1408]{3,2,1,0:T(8,128)(2,1)S(1)}, u32[]{:S(2)}, u32[]{:S(2)}) collective-permute-start(bf16[1,2,48,1408]{3,2,1,0:T(8,128)(2,1)S(1)} %dynamic-slice_convert_fusion.5), channel_id=1, source_target_pairs={{0,16},{2,18},{4,20},{6,22},{8,24},{10,26},{12,28},{14,30},{16,0},... | collective-permute-start | bytes 811016 | tf_op jit(solution)/shard_map/ppermute | solution.py:75
  243.1 5.6 %collective-permute-start.14 = (bf16[1,176,384]{2,1,0:T(8,128)(2,1)S(1)}, bf16[1,176,384]{2,1,0:T(8,128)(2,1)S(1)}, u32[]{:S(2)}, u32[]{:S(2)}) collective-permute-start(bf16[1,176,384]{2,1,0:T(8,128)(2,1)S(1)} %fusion.217), channel_id=1, source_target_pairs={{0,1},{1,0},{2,3},{3,2},{4,5},{5,4},{6,7},{7,6},{8,9},{9,8},{10,11... | collective-permute-start | bytes 405512 | tf_op jit(solution)/shard_map/ppermute | solution.py:79
  247.3 5.1 %collective-permute-start.8 = (bf16[1,1,48,1408]{3,2,1,0:T(8,128)(2,1)S(1)}, bf16[1,1,48,1408]{3,2,1,0:T(8,128)(2,1)S(1)}, u32[]{:S(2)}, u32[]{:S(2)}) collective-permute-start(bf16[1,1,48,1408]{3,2,1,0:T(8,128)(2,1)S(1)} %dynamic-slice_convert_fusion.7), channel_id=1, source_target_pairs={{0,4},{2,6},{4,0},{6,2},{8,12},{10,14},{12,8},{14,10},{16,20},{18,... | collective-permute-start | bytes 405512 | tf_op jit(solution)/shard_map/ppermute | solution.py:75
  248.8 6.4 %collective-permute-start.15 = (bf16[176,384]{1,0:T(8,128)(2,1)S(1)}, bf16[176,384]{1,0:T(8,128)(2,1)S(1)}, u32[]{:S(2)}, u32[]{:S(2)}) collective-permute-start(bf16[176,384]{1,0:T(8,128)(2,1)S(1)} %fusion.218), channel_id=1, source_target_pairs={{0,1},{1,0},{2,3},{3,2},{4,5},{5,4},{6,7},{7,6},{8,9},{9,8},{10,11... | collective-permute-start | bytes 405512 | tf_op jit(solution)/shard_map/ppermute | solution.py:79
  252.4 5.1 %collective-permute-start.9 = (bf16[48,1408]{1,0:T(8,128)(2,1)S(1)}, bf16[48,1408]{1,0:T(8,128)(2,1)S(1)}, u32[]{:S(2)}, u32[]{:S(2)}) collective-permute-start(bf16[48,1408]{1,0:T(8,128)(2,1)S(1)} %fusion.216), channel_id=1, source_target_pairs={{0,1},{1,0},{2,3},{3,2},{4,5},{5,4},{6,7},{7,6},{8,9},{9,8},{10,11... | collective-permute-start | bytes 405512 | tf_op jit(solution)/shard_map/ppermute | solution.py:79
  (67 other events, 931.4 us)
Sparse Core Ops, SparseCore 0:
  10.3 53.9 all-gather.2
  66.5 49.7 all-gather.4

commit v2 on v1

--- a/solution.py
+++ b/solution.py
@@ -83,43 +83,82 @@
     return lax.dynamic_index_in_dim(values, which, axis, keepdims=False)
 
 
-def halved_dp(slices, bits, bit):
-    at = bits.index(bit)
-    low = 1 << (len(bits) - 1 - at)
-    grouped = slices.reshape((slices.shape[0] // (2 * low), 2, low) + slices.shape[1:])
-    mine = (lax.axis_index("dp") // bit) % 2
-    sent = pick(grouped, 1 - mine, 1).astype(jnp.bfloat16)
-    total = pick(grouped, mine, 1) + partner(sent, bit).astype(jnp.float32)
-    return total.reshape((slices.shape[0] // 2,) + slices.shape[1:]), [b for b in bits if b != bit]
+def place():
+    index = lax.axis_index("dp")
+    return index // 4, (index // 2) % 2, index % 2
+
+
+def halved_dp(slices, axis, mine, bit):
+    sent = pick(slices, 1 - mine, axis).astype(jnp.bfloat16)
+    return pick(slices, mine, axis) + partner(sent, bit).astype(jnp.float32)
 
 
 def halved_rows(slices):
     half = slices.shape[-1] // 2
+    axis = slices.ndim - 1
     mine = lax.axis_index("rows")
-    sent = lax.dynamic_slice_in_dim(slices, (1 - mine) * half, half, axis=2).astype(jnp.bfloat16)
-    kept = lax.dynamic_slice_in_dim(slices, mine * half, half, axis=2)
-    return kept + other_row(sent).astype(jnp.float32)
-
-
-def joined_rows(half):
-    sent = half.astype(jnp.bfloat16)
-    other = other_row(sent)
-    first = lax.axis_index("rows") == 0
-    return jnp.concatenate(
-        [jnp.where(first, sent, other), jnp.where(first, other, sent)], axis=-1
-    ).astype(jnp.float32)
-
-
-def scattered(partial, order):
-    count = lax.axis_size("dp")
-    slices = partial.reshape(count, partial.shape[0] // count, partial.shape[1])
-    bits = [1 << k for k in reversed(range(count.bit_length() - 1))]
-    for stage in order:
-        if stage == "rows":
-            slices = halved_rows(slices)
-        else:
-            slices, bits = halved_dp(slices, bits, stage)
-    return joined_rows(slices[0])
+    sent = lax.dynamic_slice_in_dim(slices, (1 - mine) * half, half, axis=axis)
+    kept = lax.dynamic_slice_in_dim(slices, mine * half, half, axis=axis)
+    return kept + other_row(sent.astype(jnp.bfloat16)).astype(jnp.float32)
+
+
+def in_order(mine, own, other, axis, stacked):
+    first = mine == 0
+    pair = [jnp.where(first, own, other), jnp.where(first, other, own)]
+    return jnp.stack(pair, axis=axis) if stacked else jnp.concatenate(pair, axis=axis)
+
+
+def both_rows(half):
+    return in_order(lax.axis_index("rows"), half, other_row(half), half.ndim - 1, False)
+
+
+def scatter_core(partial):
+    line = lax.axis_size("dp") // 4
+    slices = partial.reshape(line, 2, 2, partial.shape[0] // (4 * line), partial.shape[1])
+    return halved_dp(slices, 2, place()[2], 1)
+
+
+def scatter_first(slices):
+    cut = slices.shape[0] // 2
+    return halved_rows(slices[:cut]), halved_dp(slices[cut:], 1, place()[1], 2)
+
+
+def scatter_second(low, high):
+    return jnp.concatenate([halved_dp(low, 1, place()[1], 2), halved_rows(high)], axis=0)
+
+
+def scatter_line(slices):
+    at = place()[0]
+    total = pick(slices, at, 0)
+    for step in range(1, slices.shape[0]):
+        sent = pick(slices, at ^ step, 0).astype(jnp.bfloat16)
+        total = total + partner(sent, 4 * step).astype(jnp.float32)
+    return total
+
+
+def scatter_last(half):
+    return both_rows(half.astype(jnp.bfloat16)).astype(jnp.float32)
+
+
+def gathered(weight):
+    line = lax.axis_size("dp") // 4
+    at, middle, core = place()
+    half = weight.shape[1] // 2
+    own = lax.dynamic_slice_in_dim(weight, lax.axis_index("rows") * half, half, axis=1)
+    pieces = [own] + [partner(own, 4 * step) for step in range(1, line)]
+    bit = 1
+    while bit < line:
+        swap = (at // bit) % 2 == 1
+        pieces = [jnp.where(swap, pieces[j ^ bit], pieces[j]) for j in range(line)]
+        bit *= 2
+    low, high = jnp.stack(pieces[: line // 2]), jnp.stack(pieces[line // 2 :])
+    low = in_order(middle, low, partner(low, 2), 1, True)
+    high = both_rows(high)
+    low = both_rows(low)
+    high = in_order(middle, high, partner(high, 2), 1, True)
+    slices = jnp.concatenate([low, high], axis=0)
+    slices = in_order(core, slices, partner(slices, 1), 2, True)
+    return slices.reshape(weight.shape[0] * 4 * line, weight.shape[1])
 
 
 def summed_everywhere(values):
@@ -129,21 +168,6 @@
         values = values + partner(values, bit)
         bit *= 2
     return values + other_row(values)
-
-
-def pointwise(tokens, cot_rows, up_full, down_full):
-    pre_act = jnp.dot(tokens, up_full, preferred_element_type=jnp.float32)
-    hidden, derivative = gelu_parts(pre_act)
-    activation = hidden.astype(jnp.bfloat16)
-    branch = jnp.dot(activation, down_full, preferred_element_type=jnp.float32)
-    grad_act = lax.dot_general(
-        cot_rows, down_full, (((1,), (1,)), ((), ())), preferred_element_type=jnp.float32
-    )
-    grad_pre = (grad_act * derivative).astype(jnp.bfloat16)
-    grad_norm = lax.dot_general(
-        grad_pre, up_full, (((1,), (1,)), ((), ())), preferred_element_type=jnp.float32
-    )
-    return (activation, branch, grad_pre, grad_norm)
 
 
 def on_device(features, bucket, kernel, up_weight, down_weight, cotangent):
@@ -165,7 +189,7 @@
     masked = jnp.where(inside_cells, features, jnp.zeros((), features.dtype))
     masked_cot = jnp.where(inside_cells, cotangent, jnp.zeros((), cotangent.dtype))
     up_full, down_full = (
-        lax.all_gather(up_weight, "dp", axis=0, tiled=True),
+        gathered(up_weight),
         lax.all_gather(down_weight, "dp", axis=0, tiled=True),
     )
     rimmed = padded_2(masked, (("rows", 1),), reach)
@@ -177,38 +201,63 @@
     normed = unit_norm.astype(jnp.bfloat16)
     tokens = normed.reshape(images * strip_rows * canvas_cols, channels)
     cot_rows = masked_cot.reshape(images * strip_rows * canvas_cols, channels)
-    activation, branch_rows, grad_pre, grad_rows = pointwise(tokens, cot_rows, up_full, down_full)
-    branch = branch_rows.reshape(features.shape)
+    pre_act = jnp.dot(tokens, up_full, preferred_element_type=jnp.float32)
+    hidden, derivative = gelu_parts(pre_act)
+    activation = hidden.astype(jnp.bfloat16)
+    down_part = (
+        lax.dot_general(
+            activation, cot_rows, (((0,), (0,)), ((), ())), preferred_element_type=jnp.float32
+        )
+        * grad_scale
+    )
+    down_part = scatter_core(down_part)
+    down_full, down_part = lax.optimization_barrier((down_full, down_part))
+    down_low, down_high = scatter_first(down_part)
+    grad_act = lax.dot_general(
+        cot_rows, down_full, (((1,), (1,)), ((), ())), preferred_element_type=jnp.float32
+    )
+    grad_pre = (grad_act * derivative).astype(jnp.bfloat16)
+    up_part = (
+        lax.dot_general(
+            tokens, grad_pre, (((0,), (0,)), ((), ())), preferred_element_type=jnp.float32
+        )
+        * grad_scale
+    )
+    up_part = scatter_core(up_part)
+    grad_rows = lax.dot_general(
+        grad_pre, up_full, (((1,), (1,)), ((), ())), preferred_element_type=jnp.float32
+    )
     grad_norm = grad_rows.reshape(features.shape)
-    block_out = (masked + branch).astype(jnp.bfloat16)
     grad_conv = jnp.where(inside_cells, norm_backward(grad_norm, unit_norm, inv_std), 0.0)
-    kernel_grad = summed_everywhere(
-        kernel_terms(grad_conv, padded, kernel.shape[0]) * grad_scale
-    )
+    grad_conv, up_part, down_low, down_high = lax.optimization_barrier(
+        (grad_conv, up_part, down_low, down_high)
+    )
+    down_part = scatter_second(down_low, down_high)
+    up_low, up_high = scatter_first(up_part)
     grad_rimmed = padded_2(grad_conv.astype(jnp.bfloat16), (("rows", 1),), reach).astype(
         grad_conv.dtype
     )
+    kernel_part = kernel_terms(grad_conv, padded, kernel.shape[0]) * grad_scale
+    kernel_part, grad_rimmed, down_part, up_low, up_high = lax.optimization_barrier(
+        (kernel_part, grad_rimmed, down_part, up_low, up_high)
+    )
+    kernel_grad = summed_everywhere(kernel_part)
+    down_half = scatter_line(down_part)
+    up_part = scatter_second(up_low, up_high)
     grad_padded = jnp.pad(grad_rimmed, ((0, 0), (0, 0), (reach, reach), (0, 0)))
     feature_grad = jnp.where(
         inside_cells,
         masked_cot + depthwise(grad_padded, kernel, strip_rows, canvas_cols, True),
         0.0,
     ).astype(jnp.bfloat16)
-    dp_bits = [1 << k for k in range(lax.axis_size("dp").bit_length() - 1)]
-    down_grad = scattered(
-        lax.dot_general(
-            activation, cot_rows, (((0,), (0,)), ((), ())), preferred_element_type=jnp.float32
-        )
-        * grad_scale,
-        dp_bits + ["rows"],
-    )
-    up_grad = scattered(
-        lax.dot_general(
-            tokens, grad_pre, (((0,), (0,)), ((), ())), preferred_element_type=jnp.float32
-        )
-        * grad_scale,
-        dp_bits[:1] + ["rows"] + dp_bits[2:] + dp_bits[1:2],
-    )
+    feature_grad, activation, down_half, up_part = lax.optimization_barrier(
+        (feature_grad, activation, down_half, up_part)
+    )
+    up_half = scatter_line(up_part)
+    branch = jnp.dot(activation, down_full, preferred_element_type=jnp.float32)
+    block_out = (masked + branch.reshape(features.shape)).astype(jnp.bfloat16)
+    down_grad = scatter_last(down_half)
+    up_grad = scatter_last(up_half)
     return (block_out, feature_grad, up_grad, down_grad, kernel_grad)
 
 

time: 266 us -> 243 us (0.914)
  waiting for transfers between devices: 122 us -> 48.1 us
  local copies, waits for them, and re-layouts: 13.1 us -> 36.5 us
  starting transfers between devices: 27 us -> 45.7 us
  other arithmetic: 60.8 us -> 71.3 us
    all_gather x1, waiting for transfers between devices: 45.4 us -> 0.01 us  [on_device(): lax.all_gather(down_weight, 'dp', axis=0, tiled=True)]
    all_gather x1 -> x0, waiting for transfers between devices: 22.5 us -> none  [on_device(): lax.all_gather(up_weight, 'dp', axis=0, tiled=True)]
    ppermute x5 -> x9, waiting for transfers between devices: 3.51 us -> 24 us  [other_row(): return lax.ppermute(values, 'rows', [(0, 1), (1, 0)])]
    ppermute x2, waiting for transfers between devices: 18.9 us -> 0.01 us  [padded_2(): lax.ppermute(lax.slice_in_dim(block, block.shape[dim] - width, None, axis...]
    another operation x56, local copies, waits for them, and re-layouts: 0.52 us -> 13.2 us  [kernel_terms(): kernel_rows.append(jnp.stack(kernel_row))]
    ppermute x12 -> x22, starting transfers between devices: 12 us -> 23.2 us  [partner(): return lax.ppermute(values, 'dp', [(i, i ^ bit) for i in range(count)])]
    ppermute x5 -> x9, starting transfers between devices: 5.03 us -> 12.8 us  [other_row(): return lax.ppermute(values, 'rows', [(0, 1), (1, 0)])]
    ppermute x2, waiting for transfers between devices: 5.13 us -> 0.01 us  [padded_2(): lax.ppermute(lax.slice_in_dim(block, 0, width, axis=dim), axis, backward)]
  transfers between devices with their start and end apart: 23 -> 36, of which waited for: 13 -> 13; matrix products, arithmetic and copies ran while one was open for 23% -> 43% of each run, Pallas kernels for 0% -> 0%
where the time goes in v2:
time: 243 us; the launch traced here: 242 us
  other arithmetic  71.3 us (29%)
  waiting for transfers between devices  48.1 us (20%)
  starting transfers between devices  45.7 us (19%)
  local copies, waits for them, and re-layouts  36.5 us (15%)
  matrix products  23.6 us (10%)
  between operations  17 us (7%)
    ppermute x9, waiting for transfers between devices, other_row(): return lax.ppermute(values, 'rows', [(0, 1), (1, 0)])  24 us
    ppermute x22, waiting for transfers between devices, partner(): return lax.ppermute(values, 'dp', [(i, i ^ bit) for i in range(count)])  24 us
    ppermute x22, starting transfers between devices, partner(): return lax.ppermute(values, 'dp', [(i, i ^ bit) for i in range(count)])  23.2 us
    reduce_sum x1, other arithmetic, layer_norm(): centered = convolved - jnp.mean(convolved, axis=-1, keepdims=True)  15.8 us
    convert_element_type x1, other arithmetic, on_device(): feature_grad = jnp.where(inside_cells, masked_cot + depthwise(grad_padded...  13.4 us
    add x6, other arithmetic, halved_dp(): return pick(slices, mine, axis) + partner(sent, bit).astype(jnp.float32)  13.2 us
    another operation x56, local copies, waits for them, and re-layouts, kernel_terms(): kernel_rows.append(jnp.stack(kernel_row))  13.2 us
    ppermute x9, starting transfers between devices, other_row(): return lax.ppermute(values, 'rows', [(0, 1), (1, 0)])  12.8 us
  transfers between devices with their start and end apart: 36, of which 13 were waited for; matrix products, arithmetic and copies ran while one was open for 43% of the time, Pallas kernels for 0%

profile of v2, /device:TPU:0, one launch (start us, length us, event | category | flops | bytes accessed | tf_op | source)
XLA Modules:
  0.0 242.2 jit_solution(14382764177913027385)
XLA Ops:
  8.1 5.1 %collective-permute-start.2 = (bf16[48,1408]{1,0:T(8,128)(2,1)S(1)}, bf16[48,1408]{1,0:T(8,128)(2,1)S(1)}, u32[]{:S(2)}, u32[]{:S(2)}) collective-permute-start(bf16[48,1408]{1,0:T(8,128)(2,1)S(1)} %constant_dynamic-slice_fusion.4), channel_id=1, source_target_pairs={{0,24},{2,26},{4,28},{6,30},{8,16},{10,18},{12,20},{14,22},{16,8},... | collective-permute-start | bytes 405512 | tf_op jit(solution)/shard_map/ppermute | solution.py:75
  17.2 3.5 %collective-permute-start = (bf16[1,3,32,768]{3,2,1,0:T(8,128)(2,1)S(1)}, bf16[1,3,32,768]{3,2,1,0:T(8,128)(2,1)S(1)}, u32[]{:S(2)}, u32[]{:S(2)}) collective-permute-start(bf16[1,3,32,768]{3,2,1,0:T(8,128)(2,1)S(1)} %get-tuple-element.157), channel_id=1, source_target_pairs={{0,1},{2,3},{4,5},{6,7},{8,9},{10,11},{12,13},{14,15},{16,17},{18,... | collective-permute-start | bytes 442376 | tf_op jit(solution)/shard_map/ppermute | solution.py:16
  28.8 3.6 %collective-permute-done.5 = bf16[2,48,1408]{2,1,0:T(8,128)(2,1)S(1)} collective-permute-done((bf16[2,48,1408]{2,1,0:T(8,128)(2,1)S(1)}, bf16[2,48,1408]{2,1,0:T(8,128)(2,1)S(1)}, u32[]{:S(2)}, u32[]{:S(2)}) %collective-permute-start.5) | collective-permute-done | bytes 270368 | tf_op jit(solution)/shard_map/ppermute | solution.py:75
  36.5 9.7 %collective-permute-done.6 = bf16[2,2,48,1408]{3,2,0,1:T(8,128)(2,1)S(1)} collective-permute-done((bf16[2,2,48,1408]{3,2,0,1:T(8,128)(2,1)S(1)}, bf16[2,2,48,1408]{3,2,0,1:T(8,128)(2,1)S(1)}, u32[]{:S(2)}, u32[]{:S(2)}) %collective-permute-start.6) | collective-permute-done | bytes 540704 | tf_op jit(solution)/shard_map/ppermute | solution.py:79
  46.3 3.5 %collective-permute-done.8 = bf16[2,48,2816]{2,1,0:T(8,128)(2,1)S(1)} collective-permute-done((bf16[2,48,2816]{2,1,0:T(8,128)(2,1)S(1)}, bf16[2,48,2816]{2,1,0:T(8,128)(2,1)S(1)}, u32[]{:S(2)}, u32[]{:S(2)}) %collective-permute-start.8) | collective-permute-done | bytes 540704 | tf_op jit(solution)/shard_map/ppermute | solution.py:75
  51.1 15.8 %fusion.225 = (f32[16,32]{1,0:T(8,128)S(1)}, f32[1,16,32,768]{3,2,1,0:T(8,128)S(1)}) fusion(bf16[1,22,38,768]{3,2,1,0:T(8,128)(2,1)S(1)} %fusion.204, f32[768]{0:T(1024)} %get-tuple-element.134, f32[768]{0:T(1024)} %get-tuple-element.135, f32[768]{0:T(1024)S(1)} %get-tuple-element.88, bf16[1,3,32,768]{3,2,1,0:T(8,128)(2,1)S(1)} %collective-permute-done.1, ...), kind=kLoop, calls=%fused_computation.520 | loop fusion | flops 60554752 | bytes 35837440 | tf_op jit(solution)/shard_map/reduce_sum | solution.py:62
  68.7 4.6 %multiply_convert_fusion = (bf16[512,2816]{1,0:T(8,128)(2,1)S(1)}, f32[512,2816]{1,0:T(8,128)}) fusion(bf16[512,768]{1,0:T(8,128)(2,1)S(1)} %bitcast.121, bf16[768,2816]{1,0:T(8,128)(2,1)S(1)} %bitcast.115), kind=kOutput, calls=%fused_computation.51 | convolution fusion | flops 2221801472 | bytes 13762560 | tf_op jit(solution)/shard_map/dot_general | solution.py:204
  75.8 3.3 %copy-done = f32[2816,768]{1,0:T(8,128)} copy-done((f32[2816,768]{1,0:T(8,128)}, f32[2816,768]{1,0:T(8,128)S(1)}, u32[]{:S(2)}) %copy-start) | copy-done | bytes 8650776
  81.0 4.3 %collective-permute-done.10 = bf16[4,2,176,768]{3,2,0,1:T(8,128)(2,1)} collective-permute-done((bf16[4,2,176,768]{3,2,0,1:T(8,128)(2,1)}, bf16[4,2,176,768]{3,2,0,1:T(8,128)(2,1)}, u32[]{:S(2)}, u32[]{:S(2)}) %collective-permute-start.10) | collective-permute-done | bytes 2162720 | tf_op jit(solution)/shard_map/ppermute | solution.py:75
  85.3 5.3 %bitcast_add_fusion.1 = f32[4,2,176,768]{3,2,0,1:T(8,128)} fusion(bf16[4,2,176,768]{3,2,0,1:T(8,128)(2,1)} %collective-permute-done.10, f32[4,2,2,176,768]{4,3,2,1,0:T(8,128)} %bitcast.111, s32[]{:T(128)S(6)} %select_n.286), kind=kLoop, calls=%fused_computation.57 | loop fusion | flops 2162688 | bytes 10813444 | tf_op jit(solution)/shard_map/add | solution.py:93
  97.4 5.9 %fusion.5 = bf16[512,2816]{1,0:T(8,128)(2,1)S(1)} fusion(f32[512,2816]{1,0:T(8,128)} %get-tuple-element.174, bf16[512,768]{1,0:T(8,128)(2,1)S(1)} %bitcast.120, bf16[2816,768]{1,0:T(8,128)(2,1)S(1)} %copy-done.106), kind=kOutput, calls=%fused_computation.50 | convolution fusion | flops 2229010432 | bytes 13762560 | tf_op jit(solution)/shard_map/dot_general | solution.py:216
  105.8 3.4 %copy-done.1 = f32[768,2816]{1,0:T(8,128)} copy-done((f32[768,2816]{1,0:T(8,128)}, f32[768,2816]{1,0:T(8,128)S(1)}, u32[]{:S(2)}) %copy-start.1) | copy-done | bytes 8650776
  110.6 3.7 %fusion.231 = (f32[512]{0:T(512)S(1)}, f32[512,768]{1,0:T(8,128)}) fusion(bf16[512,2816]{1,0:T(8,128)(2,1)S(1)} %fusion.5, bf16[768,2816]{1,0:T(8,128)(2,1)S(1)} %bitcast.118), kind=kOutput, calls=%fused_computation.525 | convolution fusion | flops 2214985216 | bytes 8783872 | tf_op jit(solution)/shard_map/dot_general | solution.py:227
  124.8 4.0 %fusion.104 = (f32[768]{0:T(1024)S(1)}, f32[768]{0:T(1024)S(1)}, f32[768]{0:T(1024)S(1)}, f32[768]{0:T(1024)S(1)}, f32[768]{0:T(1024)S(1)}, /*index=5*/f32[768]{...) fusion(f32[1,16,32,768]{3,2,1,0:T(8,128)S(1)} %multiply_select_, ...), kind=kLoop, calls=%fused_computation.260 | loop fusion | flops 21219840 | bytes 15783936 | tf_op jit(solution)/shard_map/reduce_sum | solution.py:56
  128.8 4.0 %fusion.83 = (f32[768]{0:T(1024)S(1)}, f32[768]{0:T(1024)S(1)}, f32[768]{0:T(1024)S(1)}, f32[768]{0:T(1024)S(1)}, f32[768]{0:T(1024)S(1)}, /*index=5*/f32[768]{0...) fusion(f32[1,16,32,768]{3,2,1,0:T(8,128)S(1)} %multiply_select_, ...), kind=kLoop, calls=%fused_computation.239 | loop fusion | flops 21219840 | bytes 15783936 | tf_op jit(solution)/shard_map/reduce_sum | solution.py:56
  143.1 3.2 %collective-permute-start.14 = (bf16[1,3,32,768]{3,2,1,0:T(8,128)(2,1)}, bf16[1,3,32,768]{3,2,1,0:T(8,128)(2,1)}, u32[]{:S(2)}, u32[]{:S(2)}) collective-permute-start(bf16[1,3,32,768]{3,2,1,0:T(8,128)(2,1)} %get-tuple-element.155), channel_id=1, source_target_pairs={{0,1},{2,3},{4,5},{6,7},{8,9},{10,11},{12,13},{14,15},{16,17},{18,... | collective-permute-start | bytes 442376 | tf_op jit(solution)/shard_map/ppermute | solution.py:16
  162.5 3.1 %collective-permute-start.17 = (bf16[2,176,384]{2,1,0:T(8,128)(2,1)S(1)}, bf16[2,176,384]{2,1,0:T(8,128)(2,1)S(1)}, u32[]{:S(2)}, u32[]{:S(2)}) collective-permute-start(bf16[2,176,384]{2,1,0:T(8,128)(2,1)S(1)} %dynamic-slice_convert_fusion.6), channel_id=1, source_target_pairs={{0,1},{1,0},{2,3},{3,2},{4,5},{5,4},{6,7},{7,6},{8,9},{9,8},{10,11... | collective-permute-start | bytes 811016 | tf_op jit(solution)/shard_map/ppermute | solution.py:79
  167.1 4.3 %collective-permute-done.17 = bf16[2,176,384]{2,1,0:T(8,128)(2,1)S(1)} collective-permute-done((bf16[2,176,384]{2,1,0:T(8,128)(2,1)S(1)}, bf16[2,176,384]{2,1,0:T(8,128)(2,1)S(1)}, u32[]{:S(2)}, u32[]{:S(2)}) %collective-permute-start.17) | collective-permute-done | bytes 270368 | tf_op jit(solution)/shard_map/ppermute | solution.py:79
  182.1 13.4 %fusion.196 = bf16[1,16,32,768]{3,2,1,0:T(8,128)(2,1)} fusion(f32[1,22,32,768]{3,2,1,0:T(8,128)S(1)} %maximum_convert_fusion, f32[768]{0:T(1024)} %get-tuple-element.134, f32[768]{0:T(1024)} %get-tuple-element.135, f32[768]{0:T(1024)S(1)} %get-tuple-element.88, f32[768]{0:T(1024)S(1)} %get-tuple-element.89, f32[768]{0:T(1024)S(1)} %get-tuple-element.90, ...), kind=kLoop, calls=%fused_computation.352 | loop fusion | flops 40108032 | bytes 14946304 | tf_op jit(solution)/shard_map/convert_element_type | solution.py:252
  199.2 4.1 %collective-permute-done.24 = bf16[2,48,1408]{2,1,0:T(8,128)(2,1)S(1)} collective-permute-done((bf16[2,48,1408]{2,1,0:T(8,128)(2,1)S(1)}, bf16[2,48,1408]{2,1,0:T(8,128)(2,1)S(1)}, u32[]{:S(2)}, u32[]{:S(2)}) %collective-permute-start.24) | collective-permute-done | bytes 270368 | tf_op jit(solution)/shard_map/ppermute | solution.py:79
  205.4 3.1 %collective-permute-start.26 = (bf16[48,1408]{1,0:T(8,128)(2,1)S(1)}, bf16[48,1408]{1,0:T(8,128)(2,1)S(1)}, u32[]{:S(2)}, u32[]{:S(2)}) collective-permute-start(bf16[48,1408]{1,0:T(8,128)(2,1)S(1)} %get-tuple-element.147), channel_id=1, source_target_pairs={{0,16},{2,18},{4,20},{6,22},{8,24},{10,26},{12,28},{14,30},{16,0},... | collective-permute-start | bytes 405512 | tf_op jit(solution)/shard_map/ppermute | solution.py:75
  209.8 4.6 %fusion.232 = f32[512,768]{1,0:T(8,128)S(1)} fusion(bf16[512,2816]{1,0:T(8,128)(2,1)S(1)} %copy-done.26, bf16[2816,768]{1,0:T(8,128)(2,1)} %all-gather.2.cloned.1.call-done), kind=kOutput, calls=%fused_computation.526 | convolution fusion | flops 2214592512 | bytes 8781824 | tf_op jit(solution)/shard_map/dot_general | solution.py:257
  222.6 6.6 %collective-permute-done.33 = f32[7,7,768]{2,1,0:T(8,128)S(1)} collective-permute-done((f32[7,7,768]{2,1,0:T(8,128)S(1)}, f32[7,7,768]{2,1,0:T(8,128)S(1)}, u32[]{:S(2)}, u32[]{:S(2)}) %collective-permute-start.33) | collective-permute-done | bytes 150560 | tf_op jit(solution)/shard_map/ppermute | solution.py:75
  230.5 4.1 %collective-permute-done.34 = f32[7,7,768]{2,1,0:T(8,128)S(1)} collective-permute-done((f32[7,7,768]{2,1,0:T(8,128)S(1)}, f32[7,7,768]{2,1,0:T(8,128)S(1)}, u32[]{:S(2)}, u32[]{:S(2)}) %collective-permute-start.34) | collective-permute-done | bytes 150560 | tf_op jit(solution)/shard_map/ppermute | solution.py:79
  (415 shorter events, 99.1 us)
Async XLA Ops:
  7.2 83.5 %all-gather.2.cloned.1.call-start = ((), (), s32[]{:S(2)}) async-start(), calls=%async_computation | async-start | bytes 4595712 | tf_op jit(solution)/shard_map/all_gather | solution.py:193
  8.1 14.6 %collective-permute-start.2 = (bf16[48,1408]{1,0:T(8,128)(2,1)S(1)}, bf16[48,1408]{1,0:T(8,128)(2,1)S(1)}, u32[]{:S(2)}, u32[]{:S(2)}) collective-permute-start(bf16[48,1408]{1,0:T(8,128)(2,1)S(1)} %constant_dynamic-slice_fusion.4), channel_id=1, source_target_pairs={{0,24},{2,26},{4,28},{6,30},{8,16},{10,18},{12,20},{14,22},{16,8},... | collective-permute-start | bytes 405512 | tf_op jit(solution)/shard_map/ppermute | solution.py:75
  13.3 11.4 %collective-permute-start.3 = (bf16[48,1408]{1,0:T(8,128)(2,1)S(1)}, bf16[48,1408]{1,0:T(8,128)(2,1)S(1)}, u32[]{:S(2)}, u32[]{:S(2)}) collective-permute-start(bf16[48,1408]{1,0:T(8,128)(2,1)S(1)} %constant_dynamic-slice_fusion.4), channel_id=1, source_target_pairs={{0,16},{2,18},{4,20},{6,22},{8,24},{10,26},{12,28},{14,30},{16,0},... | collective-permute-start | bytes 405512 | tf_op jit(solution)/shard_map/ppermute | solution.py:75
  17.2 18.7 %collective-permute-start = (bf16[1,3,32,768]{3,2,1,0:T(8,128)(2,1)S(1)}, bf16[1,3,32,768]{3,2,1,0:T(8,128)(2,1)S(1)}, u32[]{:S(2)}, u32[]{:S(2)}) collective-permute-start(bf16[1,3,32,768]{3,2,1,0:T(8,128)(2,1)S(1)} %get-tuple-element.157), channel_id=1, source_target_pairs={{0,1},{2,3},{4,5},{6,7},{8,9},{10,11},{12,13},{14,15},{16,17},{18,... | collective-permute-start | bytes 442376 | tf_op jit(solution)/shard_map/ppermute | solution.py:16
  20.7 15.1 %collective-permute-start.1 = (bf16[1,3,32,768]{3,2,1,0:T(8,128)(2,1)S(1)}, bf16[1,3,32,768]{3,2,1,0:T(8,128)(2,1)S(1)}, u32[]{:S(2)}, u32[]{:S(2)}) collective-permute-start(bf16[1,3,32,768]{3,2,1,0:T(8,128)(2,1)S(1)} %get-tuple-element.158), channel_id=1, source_target_pairs={{1,0},{3,2},{5,4},{7,6},{9,8},{11,10},{13,12},{15,14},{17,16},{19,... | collective-permute-start | bytes 442376 | tf_op jit(solution)/shard_map/ppermute | solution.py:19
  32.6 13.6 %collective-permute-start.6 = (bf16[2,2,48,1408]{3,2,0,1:T(8,128)(2,1)S(1)}, bf16[2,2,48,1408]{3,2,0,1:T(8,128)(2,1)S(1)}, u32[]{:S(2)}, u32[]{:S(2)}) collective-permute-start(bf16[2,2,48,1408]{3,2,0,1:T(8,128)(2,1)S(1)} %pad_maximum_fusion.6), channel_id=1, source_target_pairs={{0,1},{1,0},{2,3},{3,2},{4,5},{5,4},{6,7},{7,6},{8,9},{9,8},{10,11... | collective-permute-start | bytes 1622024 | tf_op jit(solution)/shard_map/ppermute | solution.py:79
  35.7 14.1 %collective-permute-start.8 = (bf16[2,48,2816]{2,1,0:T(8,128)(2,1)S(1)}, bf16[2,48,2816]{2,1,0:T(8,128)(2,1)S(1)}, u32[]{:S(2)}, u32[]{:S(2)}) collective-permute-start(bf16[2,48,2816]{2,1,0:T(8,128)(2,1)S(1)} %pad_maximum_fusion.7), channel_id=1, source_target_pairs={{0,4},{2,6},{4,0},{6,2},{8,12},{10,14},{12,8},{14,10},{16,20},{18,... | collective-permute-start | bytes 1622024 | tf_op jit(solution)/shard_map/ppermute | solution.py:75
  50.1 17.3 %collective-permute-start.9 = (bf16[4,2,48,2816]{3,2,1,0:T(8,128)(2,1)S(1)}, bf16[4,2,48,2816]{3,2,1,0:T(8,128)(2,1)S(1)}, u32[]{:S(2)}, u32[]{:S(2)}) collective-permute-start(bf16[4,2,48,2816]{3,2,1,0:T(8,128)(2,1)S(1)} %maximum_maximum_fusion), channel_id=1, source_target_pairs={{0,2},{2,0},{4,6},{6,4},{8,10},{10,8},{12,14},{14,12},{16,18},{18,... | collective-permute-start | bytes 6488072 | tf_op jit(solution)/shard_map/ppermute | solution.py:75
  94.4 24.0 %collective-permute-start.13 = (bf16[2,176,768]{2,1,0:T(8,128)(2,1)}, bf16[2,176,768]{2,1,0:T(8,128)(2,1)}, u32[]{:S(2)}, u32[]{:S(2)}) collective-permute-start(bf16[2,176,768]{2,1,0:T(8,128)(2,1)} %fusion.210), channel_id=1, source_target_pairs={{0,4},{2,6},{4,0},{6,2},{8,12},{10,14},{12,8},{14,10},{16,20},{18,... | collective-permute-start | bytes 1622024 | tf_op jit(solution)/shard_map/ppermute | solution.py:75
  95.9 25.2 %collective-permute-start.12 = (bf16[2,2,176,384]{3,2,0,1:T(8,128)(2,1)}, bf16[2,2,176,384]{3,2,0,1:T(8,128)(2,1)}, u32[]{:S(2)}, u32[]{:S(2)}) collective-permute-start(bf16[2,2,176,384]{3,2,0,1:T(8,128)(2,1)} %dynamic-slice_convert_fusion.3), channel_id=1, source_target_pairs={{0,1},{1,0},{2,3},{3,2},{4,5},{5,4},{6,7},{7,6},{8,9},{9,8},{10,11... | collective-permute-start | bytes 1622024 | tf_op jit(solution)/shard_map/ppermute | solution.py:79
  110.6 11.7 %collective-permute-start.11 = (bf16[4,2,48,2816]{3,2,0,1:T(8,128)(2,1)}, bf16[4,2,48,2816]{3,2,0,1:T(8,128)(2,1)}, u32[]{:S(2)}, u32[]{:S(2)}) collective-permute-start(bf16[4,2,48,2816]{3,2,0,1:T(8,128)(2,1)} %fusion.8), channel_id=1, source_target_pairs={{0,2},{2,0},{4,6},{6,4},{8,10},{10,8},{12,14},{14,12},{16,18},{18,... | collective-permute-start | bytes 6488072 | tf_op jit(solution)/shard_map/ppermute | solution.py:75
  135.2 36.3 %collective-permute-start.19 = (bf16[2,48,2816]{2,1,0:T(8,128)(2,1)}, bf16[2,48,2816]{2,1,0:T(8,128)(2,1)}, u32[]{:S(2)}, u32[]{:S(2)}) collective-permute-start(bf16[2,48,2816]{2,1,0:T(8,128)(2,1)} %fusion.211), channel_id=1, source_target_pairs={{0,4},{2,6},{4,0},{6,2},{8,12},{10,14},{12,8},{14,10},{16,20},{18,... | collective-permute-start | bytes 1622024 | tf_op jit(solution)/shard_map/ppermute | solution.py:75
  137.4 37.0 %collective-permute-start.18 = (bf16[2,2,48,1408]{3,2,0,1:T(8,128)(2,1)}, bf16[2,2,48,1408]{3,2,0,1:T(8,128)(2,1)}, u32[]{:S(2)}, u32[]{:S(2)}) collective-permute-start(bf16[2,2,48,1408]{3,2,0,1:T(8,128)(2,1)} %dynamic-slice_convert_fusion.1), channel_id=1, source_target_pairs={{0,1},{1,0},{2,3},{3,2},{4,5},{5,4},{6,7},{7,6},{8,9},{9,8},{10,11... | collective-permute-start | bytes 1622024 | tf_op jit(solution)/shard_map/ppermute | solution.py:79
  138.8 28.1 %collective-permute-start.16 = (bf16[2,176,384]{2,1,0:T(8,128)(2,1)}, bf16[2,176,384]{2,1,0:T(8,128)(2,1)S(1)}, u32[]{:S(2)}, u32[]{:S(2)}) collective-permute-start(bf16[2,176,384]{2,1,0:T(8,128)(2,1)} %fusion.212), channel_id=1, source_target_pairs={{0,4},{2,6},{4,0},{6,2},{8,12},{10,14},{12,8},{14,10},{16,20},{18,... | collective-permute-start | bytes 811016 | tf_op jit(solution)/shard_map/ppermute | solution.py:75
  143.1 19.4 %collective-permute-start.14 = (bf16[1,3,32,768]{3,2,1,0:T(8,128)(2,1)}, bf16[1,3,32,768]{3,2,1,0:T(8,128)(2,1)}, u32[]{:S(2)}, u32[]{:S(2)}) collective-permute-start(bf16[1,3,32,768]{3,2,1,0:T(8,128)(2,1)} %get-tuple-element.155), channel_id=1, source_target_pairs={{0,1},{2,3},{4,5},{6,7},{8,9},{10,11},{12,13},{14,15},{16,17},{18,... | collective-permute-start | bytes 442376 | tf_op jit(solution)/shard_map/ppermute | solution.py:16
  146.3 19.3 %collective-permute-start.15 = (bf16[1,3,32,768]{3,2,1,0:T(8,128)(2,1)}, bf16[1,3,32,768]{3,2,1,0:T(8,128)(2,1)}, u32[]{:S(2)}, u32[]{:S(2)}) collective-permute-start(bf16[1,3,32,768]{3,2,1,0:T(8,128)(2,1)} %get-tuple-element.156), channel_id=1, source_target_pairs={{1,0},{3,2},{5,4},{7,6},{9,8},{11,10},{13,12},{15,14},{17,16},{19,... | collective-permute-start | bytes 442376 | tf_op jit(solution)/shard_map/ppermute | solution.py:19
  175.6 22.7 %collective-permute-start.30 = (f32[7,7,768]{2,1,0:T(8,128)S(1)}, f32[7,7,768]{2,1,0:T(8,128)S(1)}, u32[]{:S(2)}, u32[]{:S(2)}) collective-permute-start(f32[7,7,768]{2,1,0:T(8,128)S(1)} %broadcast_multiply_fusion), channel_id=1, source_target_pairs={{0,2},{2,0},{4,6},{6,4},{8,10},{10,8},{12,14},{14,12},{16,18},{18,... | collective-permute-start | bytes 451592 | tf_op jit(solution)/shard_map/ppermute | solution.py:75
  175.8 23.4 %collective-permute-start.23 = (bf16[2,48,1408]{2,1,0:T(8,128)(2,1)S(1)}, bf16[2,48,1408]{2,1,0:T(8,128)(2,1)S(1)}, u32[]{:S(2)}, u32[]{:S(2)}) collective-permute-start(bf16[2,48,1408]{2,1,0:T(8,128)(2,1)S(1)} %fusion.213), channel_id=1, source_target_pairs={{0,4},{2,6},{4,0},{6,2},{8,12},{10,14},{12,8},{14,10},{16,20},{18,... | collective-permute-start | bytes 811016 | tf_op jit(solution)/shard_map/ppermute | solution.py:75
  177.2 18.2 %collective-permute-start.20 = (bf16[176,384]{1,0:T(8,128)(2,1)S(1)}, bf16[176,384]{1,0:T(8,128)(2,1)S(1)}, u32[]{:S(2)}, u32[]{:S(2)}) collective-permute-start(bf16[176,384]{1,0:T(8,128)(2,1)S(1)} %get-tuple-element.148), channel_id=1, source_target_pairs={{0,8},{2,10},{4,12},{6,14},{8,0},{10,2},{12,4},{14,6},{16,24},{18,... | collective-permute-start | bytes 405512 | tf_op jit(solution)/shard_map/ppermute | solution.py:75
  177.6 19.7 %collective-permute-start.21 = (bf16[176,384]{1,0:T(8,128)(2,1)S(1)}, bf16[176,384]{1,0:T(8,128)(2,1)S(1)}, u32[]{:S(2)}, u32[]{:S(2)}) collective-permute-start(bf16[176,384]{1,0:T(8,128)(2,1)S(1)} %get-tuple-element.150), channel_id=1, source_target_pairs={{0,16},{2,18},{4,20},{6,22},{8,24},{10,26},{12,28},{14,30},{16,0},... | collective-permute-start | bytes 405512 | tf_op jit(solution)/shard_map/ppermute | solution.py:75
  180.4 16.9 %collective-permute-start.22 = (bf16[176,384]{1,0:T(8,128)(2,1)S(1)}, bf16[176,384]{1,0:T(8,128)(2,1)S(1)}, u32[]{:S(2)}, u32[]{:S(2)}) collective-permute-start(bf16[176,384]{1,0:T(8,128)(2,1)S(1)} %get-tuple-element.149), channel_id=1, source_target_pairs={{0,24},{2,26},{4,28},{6,30},{8,16},{10,18},{12,20},{14,22},{16,8},... | collective-permute-start | bytes 405512 | tf_op jit(solution)/shard_map/ppermute | solution.py:75
  198.4 17.2 %collective-permute-start.31 = (f32[7,7,768]{2,1,0:T(8,128)S(1)}, f32[7,7,768]{2,1,0:T(8,128)S(1)}, u32[]{:S(2)}, u32[]{:S(2)}) collective-permute-start(f32[7,7,768]{2,1,0:T(8,128)S(1)} %add.619), channel_id=1, source_target_pairs={{0,4},{2,6},{4,0},{6,2},{8,12},{10,14},{12,8},{14,10},{16,20},{18,... | collective-permute-start | bytes 451592 | tf_op jit(solution)/shard_map/ppermute | solution.py:75
  203.5 14.4 %collective-permute-start.29 = (bf16[176,384]{1,0:T(8,128)(2,1)S(1)}, bf16[176,384]{1,0:T(8,128)(2,1)S(1)}, u32[]{:S(2)}, u32[]{:S(2)}) collective-permute-start(bf16[176,384]{1,0:T(8,128)(2,1)S(1)} %fusion.218), channel_id=1, source_target_pairs={{0,1},{1,0},{2,3},{3,2},{4,5},{5,4},{6,7},{7,6},{8,9},{9,8},{10,11... | collective-permute-start | bytes 405512 | tf_op jit(solution)/shard_map/ppermute | solution.py:79
  205.4 12.0 %collective-permute-start.26 = (bf16[48,1408]{1,0:T(8,128)(2,1)S(1)}, bf16[48,1408]{1,0:T(8,128)(2,1)S(1)}, u32[]{:S(2)}, u32[]{:S(2)}) collective-permute-start(bf16[48,1408]{1,0:T(8,128)(2,1)S(1)} %get-tuple-element.147), channel_id=1, source_target_pairs={{0,16},{2,18},{4,20},{6,22},{8,24},{10,26},{12,28},{14,30},{16,0},... | collective-permute-start | bytes 405512 | tf_op jit(solution)/shard_map/ppermute | solution.py:75
  (121 other events, 1612.7 us)
Sparse Core Ops, SparseCore 0:
  22.2 55.1 all-gather.1

commit v3 on v2

--- a/solution.py
+++ b/solution.py
@@ -1,6 +1,10 @@
+import functools
+
 import jax
 import jax.numpy as jnp
 from jax import lax
+from jax.experimental import pallas as pl
+from jax.experimental.pallas import tpu as pltpu
 from jax.sharding import PartitionSpec as P
 
 INV_ROOT_TWO = 0.7071067811865476
@@ -27,35 +31,89 @@
     return (pre_act * normal_cdf, normal_cdf + pre_act * density)
 
 
+LANES = 128
+SUBLANES = 8
+
+
+def depthwise_kernel(flipped, padded_ref, kernel_ref, out_ref):
+    span = kernel_ref.shape[0]
+    rows, cols = out_ref.shape[1], out_ref.shape[2]
+    for col in range(0, cols, SUBLANES):
+        sums = [jnp.zeros((SUBLANES, LANES), jnp.float32)] * rows
+        for start_col in range(span):
+            offset_col = span - 1 - start_col if flipped else start_col
+            taps = [
+                jnp.broadcast_to(
+                    kernel_ref[span - 1 - a if flipped else a, pl.ds(offset_col, 1), :],
+                    (SUBLANES, LANES),
+                )
+                for a in range(span)
+            ]
+            for source in range(rows + span - 1):
+                window = padded_ref[0, source, pl.ds(col + start_col, SUBLANES), :]
+                for a in range(span):
+                    if 0 <= source - a < rows:
+                        sums[source - a] = sums[source - a] + taps[a] * window
+        for row in range(rows):
+            out_ref[0, row, pl.ds(col, SUBLANES), :] = sums[row]
+
+
 def depthwise(padded, kernel, out_rows, out_cols, flipped):
+    images, channels = padded.shape[0], padded.shape[-1]
     span = kernel.shape[0]
-    result = jnp.zeros(padded.shape[:-3] + (out_rows, out_cols, padded.shape[-1]), jnp.float32)
-    for offset_row in range(span):
+    taps = span * span * out_rows * out_cols * channels * images
+    return pl.pallas_call(
+        functools.partial(depthwise_kernel, flipped),
+        grid=(images, channels // LANES),
+        in_specs=[
+            pl.BlockSpec((1,) + padded.shape[1:3] + (LANES,), lambda i, c: (i, 0, 0, c)),
+            pl.BlockSpec((span, span, LANES), lambda i, c: (0, 0, c)),
+        ],
+        out_specs=pl.BlockSpec((1, out_rows, out_cols, LANES), lambda i, c: (i, 0, 0, c)),
+        out_shape=jax.ShapeDtypeStruct((images, out_rows, out_cols, channels), jnp.float32),
+        cost_estimate=pl.CostEstimate(
+            flops=2 * taps, bytes_accessed=4 * padded.size, transcendentals=0
+        ),
+        compiler_params=pltpu.CompilerParams(vmem_limit_bytes=16 * 1024 * 1024),
+    )(padded.astype(jnp.float32), kernel)
+
+
+def kernel_terms_kernel(span, grad_ref, padded_ref, out_ref):
+    rows, cols = grad_ref.shape[1], grad_ref.shape[2]
+    for col in range(0, cols, SUBLANES):
+        grads = [grad_ref[0, row, pl.ds(col, SUBLANES), :] for row in range(rows)]
         for offset_col in range(span):
-            start_row = span - 1 - offset_row if flipped else offset_row
-            start_col = span - 1 - offset_col if flipped else offset_col
-            result = (
-                result
-                + kernel[offset_row, offset_col]
-                * padded[..., start_row : start_row + out_rows, start_col : start_col + out_cols, :]
-            )
-    return result
+            sums = [jnp.zeros((SUBLANES, LANES), jnp.float32)] * span
+            for source in range(rows + span - 1):
+                window = padded_ref[0, source, pl.ds(col + offset_col, SUBLANES), :]
+                for a in range(span):
+                    if 0 <= source - a < rows:
+                        sums[a] = sums[a] + grads[source - a] * window
+            for a in range(span):
+                if col == 0:
+                    out_ref[0, a * span + offset_col] = sums[a]
+                else:
+                    out_ref[0, a * span + offset_col] += sums[a]
 
 
 def kernel_terms(grad_conv, padded, span):
-    reduce_axes = tuple(range(grad_conv.ndim - 1))
-    rows_out = grad_conv.shape[-3]
-    cols_out = grad_conv.shape[-2]
-    kernel_rows = []
-    for offset_row in range(span):
-        kernel_row = []
-        for offset_col in range(span):
-            window = padded[
-                ..., offset_row : offset_row + rows_out, offset_col : offset_col + cols_out, :
-            ]
-            kernel_row.append(jnp.sum(grad_conv * window, axis=reduce_axes))
-        kernel_rows.append(jnp.stack(kernel_row))
-    return jnp.stack(kernel_rows)
+    images, rows, cols, channels = grad_conv.shape
+    taps = span * span * grad_conv.size
+    terms = pl.pallas_call(
+        functools.partial(kernel_terms_kernel, span),
+        grid=(images, channels // LANES),
+        in_specs=[
+            pl.BlockSpec((1, rows, cols, LANES), lambda i, c: (i, 0, 0, c)),
+            pl.BlockSpec((1,) + padded.shape[1:3] + (LANES,), lambda i, c: (i, 0, 0, c)),
+        ],
+        out_specs=pl.BlockSpec((1, span * span, SUBLANES, LANES), lambda i, c: (i, 0, 0, c)),
+        out_shape=jax.ShapeDtypeStruct((images, span * span, SUBLANES, channels), jnp.float32),
+        cost_estimate=pl.CostEstimate(
+            flops=2 * taps, bytes_accessed=4 * padded.size, transcendentals=0
+        ),
+        compiler_params=pltpu.CompilerParams(vmem_limit_bytes=16 * 1024 * 1024),
+    )(grad_conv, padded.astype(jnp.float32))
+    return jnp.sum(terms, axis=(0, 2)).reshape(span, span, channels)
 
 
 def layer_norm(convolved):
@@ -140,9 +198,9 @@
     return both_rows(half.astype(jnp.bfloat16)).astype(jnp.float32)
 
 
-def gathered(weight):
+def gather_line(weight):
     line = lax.axis_size("dp") // 4
-    at, middle, core = place()
+    at = place()[0]
     half = weight.shape[1] // 2
     own = lax.dynamic_slice_in_dim(weight, lax.axis_index("rows") * half, half, axis=1)
     pieces = [own] + [partner(own, 4 * step) for step in range(1, line)]
@@ -151,23 +209,29 @@
         swap = (at // bit) % 2 == 1
         pieces = [jnp.where(swap, pieces[j ^ bit], pieces[j]) for j in range(line)]
         bit *= 2
-    low, high = jnp.stack(pieces[: line // 2]), jnp.stack(pieces[line // 2 :])
-    low = in_order(middle, low, partner(low, 2), 1, True)
-    high = both_rows(high)
-    low = both_rows(low)
-    high = in_order(middle, high, partner(high, 2), 1, True)
+    return jnp.stack(pieces[: line // 2]), jnp.stack(pieces[line // 2 :])
+
+
+def gather_middle(slices):
+    return in_order(place()[1], slices, partner(slices, 2), 1, True)
+
+
+def gather_core(low, high):
     slices = jnp.concatenate([low, high], axis=0)
-    slices = in_order(core, slices, partner(slices, 1), 2, True)
-    return slices.reshape(weight.shape[0] * 4 * line, weight.shape[1])
-
-
-def summed_everywhere(values):
-    count = lax.axis_size("dp")
+    slices = in_order(place()[2], slices, partner(slices, 1), 2, True)
+    return slices.reshape(-1, slices.shape[-1])
+
+
+def summed_line(values):
+    line = lax.axis_size("dp") // 4
+    at = place()[0]
+    pieces = [values] + [partner(values, 4 * step) for step in range(1, line)]
     bit = 1
-    while bit < count:
-        values = values + partner(values, bit)
+    while bit < line:
+        swap = (at // bit) % 2 == 1
+        pieces = [jnp.where(swap, pieces[j ^ bit], pieces[j]) for j in range(line)]
         bit *= 2
-    return values + other_row(values)
+    return functools.reduce(jnp.add, pieces)
 
 
 def on_device(features, bucket, kernel, up_weight, down_weight, cotangent):
@@ -188,19 +252,21 @@
     inside_cells = inside[..., None]
     masked = jnp.where(inside_cells, features, jnp.zeros((), features.dtype))
     masked_cot = jnp.where(inside_cells, cotangent, jnp.zeros((), cotangent.dtype))
-    up_full, down_full = (
-        gathered(up_weight),
-        lax.all_gather(down_weight, "dp", axis=0, tiled=True),
-    )
+    down_full = lax.all_gather(down_weight, "dp", axis=0, tiled=True)
+    up_low, up_high = gather_line(up_weight)
     rimmed = padded_2(masked, (("rows", 1),), reach)
-    padded = jnp.pad(rimmed, ((0, 0), (0, 0), (reach, reach), (0, 0)))
-    convolved = jnp.where(
-        inside_cells, depthwise(padded, kernel, strip_rows, canvas_cols, False), 0.0
-    )
+    padded = jnp.pad(rimmed, ((0, 0), (0, 0), (reach, reach), (0, 0))).astype(jnp.float32)
+    padded, up_low, up_high = lax.optimization_barrier((padded, up_low, up_high))
+    up_low, up_high = gather_middle(up_low), both_rows(up_high)
+    convolved = depthwise(padded, kernel, strip_rows, canvas_cols, False)
+    convolved, up_low, up_high = lax.optimization_barrier((convolved, up_low, up_high))
+    up_low, up_high = both_rows(up_low), gather_middle(up_high)
+    convolved = jnp.where(inside_cells, convolved, 0.0)
     unit_norm, inv_std = layer_norm(convolved)
     normed = unit_norm.astype(jnp.bfloat16)
     tokens = normed.reshape(images * strip_rows * canvas_cols, channels)
     cot_rows = masked_cot.reshape(images * strip_rows * canvas_cols, channels)
+    up_full = gather_core(up_low, up_high)
     pre_act = jnp.dot(tokens, up_full, preferred_element_type=jnp.float32)
     hidden, derivative = gelu_parts(pre_act)
     activation = hidden.astype(jnp.bfloat16)
@@ -241,7 +307,7 @@
     kernel_part, grad_rimmed, down_part, up_low, up_high = lax.optimization_barrier(
         (kernel_part, grad_rimmed, down_part, up_low, up_high)
     )
-    kernel_grad = summed_everywhere(kernel_part)
+    kernel_part = kernel_part + partner(kernel_part, 1)
     down_half = scatter_line(down_part)
     up_part = scatter_second(up_low, up_high)
     grad_padded = jnp.pad(grad_rimmed, ((0, 0), (0, 0), (reach, reach), (0, 0)))
@@ -250,12 +316,14 @@
         masked_cot + depthwise(grad_padded, kernel, strip_rows, canvas_cols, True),
         0.0,
     ).astype(jnp.bfloat16)
-    feature_grad, activation, down_half, up_part = lax.optimization_barrier(
-        (feature_grad, activation, down_half, up_part)
-    )
+    feature_grad, activation, down_half, up_part, kernel_part = lax.optimization_barrier(
+        (feature_grad, activation, down_half, up_part, kernel_part)
+    )
+    kernel_part = kernel_part + partner(kernel_part, 2)
     up_half = scatter_line(up_part)
     branch = jnp.dot(activation, down_full, preferred_element_type=jnp.float32)
     block_out = (masked + branch.reshape(features.shape)).astype(jnp.bfloat16)
+    kernel_grad = summed_line(kernel_part + other_row(kernel_part))
     down_grad = scatter_last(down_half)
     up_grad = scatter_last(up_half)
     return (block_out, feature_grad, up_grad, down_grad, kernel_grad)

time: 243 us -> 231 us (0.951)
  other arithmetic: 71.3 us -> 38.4 us
  waiting for transfers between devices: 48.1 us -> 66.5 us
  Pallas kernels: 0 us -> 17.4 us
  local copies, waits for them, and re-layouts: 36.5 us -> 23.3 us
    pallas_call x0 -> x3, Pallas kernels: none -> 17.4 us  [the longest x2 12 us: depthwise(): pl.pallas_call(functools.partial(depthwise_kernel, flipped), grid=(images...]
    reduce_sum x1, other arithmetic: 15.8 us -> 0.27 us  [layer_norm(): centered = convolved - jnp.mean(convolved, axis=-1, keepdims=True)]
    another operation x57 -> x0, local copies, waits for them, and re-layouts: 13.2 us -> none  [the longest x56 13.2 us: kernel_terms(): kernel_rows.append(jnp.stack(kernel_row))]
    convert_element_type x1, other arithmetic: 13.4 us -> 1.19 us  [on_device(): feature_grad = jnp.where(inside_cells, masked_cot + depthwise(grad_padded...]
    ppermute x9, waiting for transfers between devices: 24 us -> 12.6 us  [other_row(): return lax.ppermute(values, 'rows', [(0, 1), (1, 0)])]
    ppermute x22 -> x23, waiting for transfers between devices: 24 us -> 34.3 us  [partner(): return lax.ppermute(values, 'dp', [(i, i ^ bit) for i in range(count)])]
    reduce_sum x4 -> x1, other arithmetic: 10.4 us -> 0.32 us  [kernel_terms(): return jnp.sum(terms, axis=(0, 2)).reshape(span, span, channels)]
    all_gather x1, waiting for transfers between devices: 0.01 us -> 9.63 us  [on_device(): down_full = lax.all_gather(down_weight, 'dp', axis=0, tiled=True)]
  transfers between devices with their start and end apart: 36 -> 37, of which waited for: 13 -> 15; matrix products, arithmetic and copies ran while one was open for 43% -> 26% of each run, Pallas kernels for 0% -> 5%
where the time goes in v3:
time: 231 us; the launch traced here: 230 us
  waiting for transfers between devices  66.5 us (29%)
  starting transfers between devices  47.9 us (21%)
  other arithmetic  38.4 us (17%)
  local copies, waits for them, and re-layouts  23.3 us (10%)
  matrix products  21.4 us (9%)
  Pallas kernels  17.4 us (8%)
  between operations  15.7 us (7%)
    ppermute x23, waiting for transfers between devices, partner(): return lax.ppermute(values, 'dp', [(i, i ^ bit) for i in range(count)])  34.3 us
    ppermute x23, starting transfers between devices, partner(): return lax.ppermute(values, 'dp', [(i, i ^ bit) for i in range(count)])  26.4 us
    add x6, other arithmetic, halved_dp(): return pick(slices, mine, axis) + partner(sent, bit).astype(jnp.float32)  13 us
    ppermute x9, waiting for transfers between devices, other_row(): return lax.ppermute(values, 'rows', [(0, 1), (1, 0)])  12.6 us
    ppermute x9, starting transfers between devices, other_row(): return lax.ppermute(values, 'rows', [(0, 1), (1, 0)])  12.3 us
    pallas_call x2, Pallas kernels, depthwise(): pl.pallas_call(functools.partial(depthwise_kernel, flipped), grid=(images...  12 us
    all_gather x1, waiting for transfers between devices, on_device(): down_full = lax.all_gather(down_weight, 'dp', axis=0, tiled=True)  9.63 us
    unnamed x76, local copies, waits for them, and re-layouts  9.19 us
  transfers between devices with their start and end apart: 37, of which 15 were waited for; matrix products, arithmetic and copies ran while one was open for 26% of the time, Pallas kernels for 5%

profile of v3, /device:TPU:0, one launch (start us, length us, event | category | flops | bytes accessed | tf_op | source)
XLA Modules:
  0.0 230.5 jit_solution(11035726238074927370)
XLA Ops:
  8.2 5.1 %collective-permute-start.2 = (bf16[48,1408]{1,0:T(8,128)(2,1)S(1)}, bf16[48,1408]{1,0:T(8,128)(2,1)S(1)}, u32[]{:S(2)}, u32[]{:S(2)}) collective-permute-start(bf16[48,1408]{1,0:T(8,128)(2,1)S(1)} %constant_dynamic-slice_fusion.4), channel_id=1, source_target_pairs={{0,24},{2,26},{4,28},{6,30},{8,16},{10,18},{12,20},{14,22},{16,8},... | collective-permute-start | bytes 405512 | tf_op jit(solution)/shard_map/ppermute | solution.py:133
  17.2 3.5 %collective-permute-start = (bf16[1,3,32,768]{3,2,1,0:T(8,128)(2,1)S(1)}, bf16[1,3,32,768]{3,2,1,0:T(8,128)(2,1)S(1)}, u32[]{:S(2)}, u32[]{:S(2)}) collective-permute-start(bf16[1,3,32,768]{3,2,1,0:T(8,128)(2,1)S(1)} %get-tuple-element.67), channel_id=1, source_target_pairs={{0,1},{2,3},{4,5},{6,7},{8,9},{10,11},{12,13},{14,15},{16,17},{18,... | collective-permute-start | bytes 442376 | tf_op jit(solution)/shard_map/ppermute | solution.py:20
  25.0 2.8 %collective-permute-done.1 = bf16[1,3,32,768]{3,2,1,0:T(8,128)(2,1)S(1)} collective-permute-done((bf16[1,3,32,768]{3,2,1,0:T(8,128)(2,1)S(1)}, bf16[1,3,32,768]{3,2,1,0:T(8,128)(2,1)S(1)}, u32[]{:S(2)}, u32[]{:S(2)}) %collective-permute-start.1) | collective-permute-done | bytes 147488 | tf_op jit(solution)/shard_map/ppermute | solution.py:23
  33.0 5.9 %shard_map.101 = f32[1,16,32,768]{3,2,1,0:T(8,128)S(1)} custom-call(f32[1,22,38,768]{3,2,1,0:T(8,128)S(1)} %copy-done, f32[7,7,768]{2,1,0:T(8,128)S(1)} %copy-done.2), custom_call_target="tpu_custom_call" | custom-call | flops 38535168 | bytes 2568192 | tf_op jit(solution)/shard_map/pallas_call | solution.py:65
  42.6 9.1 %collective-permute-done.8 = bf16[2,48,2816]{2,1,0:T(8,128)(2,1)} collective-permute-done((bf16[2,48,2816]{2,1,0:T(8,128)(2,1)S(1)}, bf16[2,48,2816]{2,1,0:T(8,128)(2,1)}, u32[]{:S(2)}, u32[]{:S(2)}) %collective-permute-start.8) | collective-permute-done | bytes 540704 | tf_op jit(solution)/shard_map/ppermute | solution.py:133
  56.0 3.5 %collective-permute-done.9 = bf16[4,2,48,2816]{3,2,1,0:T(8,128)(2,1)} collective-permute-done((bf16[4,2,48,2816]{3,2,1,0:T(8,128)(2,1)}, bf16[4,2,48,2816]{3,2,1,0:T(8,128)(2,1)}, u32[]{:S(2)}, u32[]{:S(2)}) %collective-permute-start.9) | collective-permute-done | bytes 2162720 | tf_op jit(solution)/shard_map/ppermute | solution.py:133
  62.0 4.5 %multiply_convert_fusion = (bf16[512,2816]{1,0:T(8,128)(2,1)S(1)}, f32[512,2816]{1,0:T(8,128)}) fusion(bf16[512,768]{1,0:T(8,128)(2,1)S(1)} %bitcast.107, bf16[768,2816]{1,0:T(8,128)(2,1)S(1)} %bitcast.101), kind=kOutput, calls=%fused_computation.9 | convolution fusion | flops 2221801472 | bytes 13762560 | tf_op jit(solution)/shard_map/dot_general | solution.py:270
  69.1 3.3 %copy-done.3 = f32[2816,768]{1,0:T(8,128)} copy-done((f32[2816,768]{1,0:T(8,128)}, f32[2816,768]{1,0:T(8,128)S(1)}, u32[]{:S(2)}) %copy-start.3) | copy-done | bytes 8650776
  74.1 4.6 %collective-permute-done.10 = bf16[4,2,176,768]{3,2,0,1:T(8,128)(2,1)} collective-permute-done((bf16[4,2,176,768]{3,2,0,1:T(8,128)(2,1)}, bf16[4,2,176,768]{3,2,0,1:T(8,128)(2,1)}, u32[]{:S(2)}, u32[]{:S(2)}) %collective-permute-start.10) | collective-permute-done | bytes 2162720 | tf_op jit(solution)/shard_map/ppermute | solution.py:133
  78.7 5.4 %bitcast_add_fusion.1 = f32[4,2,176,768]{3,2,0,1:T(8,128)} fusion(bf16[4,2,176,768]{3,2,0,1:T(8,128)(2,1)} %collective-permute-done.10, f32[4,2,2,176,768]{4,3,2,1,0:T(8,128)} %bitcast.97, s32[]{:T(128)S(6)} %select_n.334), kind=kLoop, calls=%fused_computation.15 | loop fusion | flops 2162688 | bytes 10813444 | tf_op jit(solution)/shard_map/add | solution.py:151
  84.1 9.6 %all-gather.2.cloned.1.call-done = bf16[2816,768]{1,0:T(8,128)(2,1)} async-done(((bf16[176,768]{1,0:T(8,128)(2,1)}), bf16[2816,768]{1,0:T(8,128)(2,1)}) %all-gather.2.cloned.1.call-update) | async-done | bytes 4325392 | tf_op jit(solution)/shard_map/all_gather | solution.py:255
  93.7 2.9 %fusion.32 = (f32[2,2,176,768]{3,2,0,1:T(8,128)S(1)}, f32[2,2,176,768]{3,2,0,1:T(8,128)S(1)}) fusion(f32[4,2,176,768]{3,2,0,1:T(8,128)} %bitcast_add_fusion.1), kind=kLoop, calls=%fused_computation.124 | loop fusion | bytes 8650752 | tf_op jit(solution)/shard_map/slice | solution.py:181
  100.5 5.9 %fusion.5 = bf16[512,2816]{1,0:T(8,128)(2,1)S(1)} fusion(f32[512,2816]{1,0:T(8,128)} %get-tuple-element.84, bf16[512,768]{1,0:T(8,128)(2,1)S(1)} %bitcast.106, bf16[2816,768]{1,0:T(8,128)(2,1)S(1)} %copy-done.33), kind=kOutput, calls=%fused_computation.8 | convolution fusion | flops 2229010432 | bytes 13762560 | tf_op jit(solution)/shard_map/dot_general | solution.py:282
  108.9 3.4 %copy-done.4 = f32[768,2816]{1,0:T(8,128)} copy-done((f32[768,2816]{1,0:T(8,128)}, f32[768,2816]{1,0:T(8,128)S(1)}, u32[]{:S(2)}) %copy-start.4) | copy-done | bytes 8650776
  113.9 3.6 %fusion.35 = (f32[512]{0:T(512)S(1)}, f32[512,768]{1,0:T(8,128)}) fusion(bf16[512,2816]{1,0:T(8,128)(2,1)S(1)} %fusion.5, bf16[768,2816]{1,0:T(8,128)(2,1)S(1)} %bitcast.104), kind=kOutput, calls=%fused_computation.127 | convolution fusion | flops 2214985216 | bytes 8783872 | tf_op jit(solution)/shard_map/dot_general | solution.py:293
  128.3 5.4 %shard_map.102 = f32[1,49,8,768]{3,2,1,0:T(8,128)S(1)} custom-call(f32[1,16,32,768]{3,2,1,0:T(8,128)S(1)} %multiply_select_fusion.grad_ref, f32[1,22,38,768]{3,2,1,0:T(8,128)S(1)} %copy-done.1), custom_call_target="tpu_custom_call" | custom-call | flops 38535168 | bytes 2568192 | tf_op jit(solution)/shard_map/pallas_call | solution.py:102
  140.3 3.0 %collective-permute-start.14 = (bf16[1,3,32,768]{3,2,1,0:T(8,128)(2,1)}, bf16[1,3,32,768]{3,2,1,0:T(8,128)(2,1)S(1)}, u32[]{:S(2)}, u32[]{:S(2)}) collective-permute-start(bf16[1,3,32,768]{3,2,1,0:T(8,128)(2,1)} %get-tuple-element.65), channel_id=1, source_target_pairs={{0,1},{2,3},{4,5},{6,7},{8,9},{10,11},{12,13},{14,15},{16,17},{18,... | collective-permute-start | bytes 442376 | tf_op jit(solution)/shard_map/ppermute | solution.py:20
  146.2 7.1 %collective-permute-done.14 = bf16[1,3,32,768]{3,2,1,0:T(8,128)(2,1)S(1)} collective-permute-done((bf16[1,3,32,768]{3,2,1,0:T(8,128)(2,1)}, bf16[1,3,32,768]{3,2,1,0:T(8,128)(2,1)S(1)}, u32[]{:S(2)}, u32[]{:S(2)}) %collective-permute-start.14) | collective-permute-done | bytes 147488 | tf_op jit(solution)/shard_map/ppermute | solution.py:20
  158.0 3.8 %collective-permute-done.17 = bf16[2,176,384]{2,1,0:T(8,128)(2,1)S(1)} collective-permute-done((bf16[2,176,384]{2,1,0:T(8,128)(2,1)S(1)}, bf16[2,176,384]{2,1,0:T(8,128)(2,1)S(1)}, u32[]{:S(2)}, u32[]{:S(2)}) %collective-permute-start.17) | collective-permute-done | bytes 270368 | tf_op jit(solution)/shard_map/ppermute | solution.py:137
  170.6 6.1 %shard_map.103 = f32[1,16,32,768]{3,2,1,0:T(8,128)S(1)} custom-call(f32[1,22,38,768]{3,2,1,0:T(8,128)S(1)} %pad.9.padded_ref, f32[7,7,768]{2,1,0:T(8,128)S(1)} %copy-done.2), custom_call_target="tpu_custom_call" | custom-call | flops 38535168 | bytes 2568192 | tf_op jit(solution)/shard_map/pallas_call | solution.py:65
  180.8 5.0 %collective-permute-done.24 = bf16[2,48,1408]{2,1,0:T(8,128)(2,1)S(1)} collective-permute-done((bf16[2,48,1408]{2,1,0:T(8,128)(2,1)S(1)}, bf16[2,48,1408]{2,1,0:T(8,128)(2,1)S(1)}, u32[]{:S(2)}, u32[]{:S(2)}) %collective-permute-start.24) | collective-permute-done | bytes 270368 | tf_op jit(solution)/shard_map/ppermute | solution.py:137
  196.9 4.0 %collective-permute-done.27 = bf16[48,1408]{1,0:T(8,128)(2,1)S(1)} collective-permute-done((bf16[48,1408]{1,0:T(8,128)(2,1)S(1)}, bf16[48,1408]{1,0:T(8,128)(2,1)S(1)}, u32[]{:S(2)}, u32[]{:S(2)}) %collective-permute-start.27) | collective-permute-done | bytes 135200 | tf_op jit(solution)/shard_map/ppermute | solution.py:133
  213.2 3.7 %collective-permute-done.33 = f32[7,7,768]{2,1,0:T(8,128)S(1)} collective-permute-done((f32[7,7,768]{2,1,0:T(8,128)S(1)}, f32[7,7,768]{2,1,0:T(8,128)S(1)}, u32[]{:S(2)}, u32[]{:S(2)}) %collective-permute-start.33) | collective-permute-done | bytes 150560 | tf_op jit(solution)/shard_map/ppermute | solution.py:133
  216.9 6.0 %collective-permute-done.34 = f32[7,7,768]{2,1,0:T(8,128)S(1)} collective-permute-done((f32[7,7,768]{2,1,0:T(8,128)S(1)}, f32[7,7,768]{2,1,0:T(8,128)S(1)}, u32[]{:S(2)}, u32[]{:S(2)}) %collective-permute-start.34) | collective-permute-done | bytes 150560 | tf_op jit(solution)/shard_map/ppermute | solution.py:133
  (211 shorter events, 97.6 us)
Async XLA Ops:
  7.2 86.5 %all-gather.2.cloned.1.call-start = ((), (), s32[]{:S(2)}) async-start(), calls=%async_computation | async-start | bytes 4595712 | tf_op jit(solution)/shard_map/all_gather | solution.py:255
  8.2 13.9 %collective-permute-start.2 = (bf16[48,1408]{1,0:T(8,128)(2,1)S(1)}, bf16[48,1408]{1,0:T(8,128)(2,1)S(1)}, u32[]{:S(2)}, u32[]{:S(2)}) collective-permute-start(bf16[48,1408]{1,0:T(8,128)(2,1)S(1)} %constant_dynamic-slice_fusion.4), channel_id=1, source_target_pairs={{0,24},{2,26},{4,28},{6,30},{8,16},{10,18},{12,20},{14,22},{16,8},... | collective-permute-start | bytes 405512 | tf_op jit(solution)/shard_map/ppermute | solution.py:133
  13.3 11.4 %collective-permute-start.3 = (bf16[48,1408]{1,0:T(8,128)(2,1)S(1)}, bf16[48,1408]{1,0:T(8,128)(2,1)S(1)}, u32[]{:S(2)}, u32[]{:S(2)}) collective-permute-start(bf16[48,1408]{1,0:T(8,128)(2,1)S(1)} %constant_dynamic-slice_fusion.4), channel_id=1, source_target_pairs={{0,16},{2,18},{4,20},{6,22},{8,24},{10,26},{12,28},{14,30},{16,0},... | collective-permute-start | bytes 405512 | tf_op jit(solution)/shard_map/ppermute | solution.py:133
  13.3 11.4 %collective-permute-start.4 = (bf16[48,1408]{1,0:T(8,128)(2,1)S(1)}, bf16[48,1408]{1,0:T(8,128)(2,1)S(1)}, u32[]{:S(2)}, u32[]{:S(2)}) collective-permute-start(bf16[48,1408]{1,0:T(8,128)(2,1)S(1)} %constant_dynamic-slice_fusion.4), channel_id=1, source_target_pairs={{0,8},{2,10},{4,12},{6,14},{8,0},{10,2},{12,4},{14,6},{16,24},{18,... | collective-permute-start | bytes 405512 | tf_op jit(solution)/shard_map/ppermute | solution.py:133
  40.0 11.7 %collective-permute-start.8 = (bf16[2,48,2816]{2,1,0:T(8,128)(2,1)S(1)}, bf16[2,48,2816]{2,1,0:T(8,128)(2,1)}, u32[]{:S(2)}, u32[]{:S(2)}) collective-permute-start(bf16[2,48,2816]{2,1,0:T(8,128)(2,1)S(1)} %pad_maximum_fusion.5), channel_id=1, source_target_pairs={{0,4},{2,6},{4,0},{6,2},{8,12},{10,14},{12,8},{14,10},{16,20},{18,... | collective-permute-start | bytes 1622024 | tf_op jit(solution)/shard_map/ppermute | solution.py:133
  40.5 12.5 %collective-permute-start.7 = (bf16[2,2,48,1408]{3,2,0,1:T(8,128)(2,1)}, bf16[2,2,48,1408]{3,2,0,1:T(8,128)(2,1)S(1)}, u32[]{:S(2)}, u32[]{:S(2)}) collective-permute-start(bf16[2,2,48,1408]{3,2,0,1:T(8,128)(2,1)} %pad_maximum_fusion.4), channel_id=1, source_target_pairs={{0,1},{1,0},{2,3},{3,2},{4,5},{5,4},{6,7},{7,6},{8,9},{9,8},{10,11... | collective-permute-start | bytes 1622024 | tf_op jit(solution)/shard_map/ppermute | solution.py:137
  97.6 24.1 %collective-permute-start.13 = (bf16[2,176,768]{2,1,0:T(8,128)(2,1)}, bf16[2,176,768]{2,1,0:T(8,128)(2,1)}, u32[]{:S(2)}, u32[]{:S(2)}) collective-permute-start(bf16[2,176,768]{2,1,0:T(8,128)(2,1)} %fusion.16), channel_id=1, source_target_pairs={{0,4},{2,6},{4,0},{6,2},{8,12},{10,14},{12,8},{14,10},{16,20},{18,... | collective-permute-start | bytes 1622024 | tf_op jit(solution)/shard_map/ppermute | solution.py:133
  99.0 25.3 %collective-permute-start.12 = (bf16[2,2,176,384]{3,2,0,1:T(8,128)(2,1)}, bf16[2,2,176,384]{3,2,0,1:T(8,128)(2,1)}, u32[]{:S(2)}, u32[]{:S(2)}) collective-permute-start(bf16[2,2,176,384]{3,2,0,1:T(8,128)(2,1)} %dynamic-slice_convert_fusion.3), channel_id=1, source_target_pairs={{0,1},{1,0},{2,3},{3,2},{4,5},{5,4},{6,7},{7,6},{8,9},{9,8},{10,11... | collective-permute-start | bytes 1622024 | tf_op jit(solution)/shard_map/ppermute | solution.py:137
  113.8 11.6 %collective-permute-start.11 = (bf16[4,2,48,2816]{3,2,0,1:T(8,128)(2,1)}, bf16[4,2,48,2816]{3,2,0,1:T(8,128)(2,1)}, u32[]{:S(2)}, u32[]{:S(2)}) collective-permute-start(bf16[4,2,48,2816]{3,2,0,1:T(8,128)(2,1)} %fusion.8), channel_id=1, source_target_pairs={{0,2},{2,0},{4,6},{6,4},{8,10},{10,8},{12,14},{14,12},{16,18},{18,... | collective-permute-start | bytes 6488072 | tf_op jit(solution)/shard_map/ppermute | solution.py:133
  135.0 26.9 %collective-permute-start.19 = (bf16[2,48,2816]{2,1,0:T(8,128)(2,1)}, bf16[2,48,2816]{2,1,0:T(8,128)(2,1)}, u32[]{:S(2)}, u32[]{:S(2)}) collective-permute-start(bf16[2,48,2816]{2,1,0:T(8,128)(2,1)} %fusion.17), channel_id=1, source_target_pairs={{0,4},{2,6},{4,0},{6,2},{8,12},{10,14},{12,8},{14,10},{16,20},{18,... | collective-permute-start | bytes 1622024 | tf_op jit(solution)/shard_map/ppermute | solution.py:133
  137.3 25.9 %collective-permute-start.18 = (bf16[2,2,48,1408]{3,2,0,1:T(8,128)(2,1)}, bf16[2,2,48,1408]{3,2,0,1:T(8,128)(2,1)}, u32[]{:S(2)}, u32[]{:S(2)}) collective-permute-start(bf16[2,2,48,1408]{3,2,0,1:T(8,128)(2,1)} %dynamic-slice_convert_fusion.1), channel_id=1, source_target_pairs={{0,1},{1,0},{2,3},{3,2},{4,5},{5,4},{6,7},{7,6},{8,9},{9,8},{10,11... | collective-permute-start | bytes 1622024 | tf_op jit(solution)/shard_map/ppermute | solution.py:137
  138.7 18.1 %collective-permute-start.16 = (bf16[2,176,384]{2,1,0:T(8,128)(2,1)}, bf16[2,176,384]{2,1,0:T(8,128)(2,1)}, u32[]{:S(2)}, u32[]{:S(2)}) collective-permute-start(bf16[2,176,384]{2,1,0:T(8,128)(2,1)} %fusion.18), channel_id=1, source_target_pairs={{0,4},{2,6},{4,0},{6,2},{8,12},{10,14},{12,8},{14,10},{16,20},{18,... | collective-permute-start | bytes 811016 | tf_op jit(solution)/shard_map/ppermute | solution.py:133
  140.3 13.0 %collective-permute-start.14 = (bf16[1,3,32,768]{3,2,1,0:T(8,128)(2,1)}, bf16[1,3,32,768]{3,2,1,0:T(8,128)(2,1)S(1)}, u32[]{:S(2)}, u32[]{:S(2)}) collective-permute-start(bf16[1,3,32,768]{3,2,1,0:T(8,128)(2,1)} %get-tuple-element.65), channel_id=1, source_target_pairs={{0,1},{2,3},{4,5},{6,7},{8,9},{10,11},{12,13},{14,15},{16,17},{18,... | collective-permute-start | bytes 442376 | tf_op jit(solution)/shard_map/ppermute | solution.py:20
  143.3 12.4 %collective-permute-start.15 = (bf16[1,3,32,768]{3,2,1,0:T(8,128)(2,1)}, bf16[1,3,32,768]{3,2,1,0:T(8,128)(2,1)}, u32[]{:S(2)}, u32[]{:S(2)}) collective-permute-start(bf16[1,3,32,768]{3,2,1,0:T(8,128)(2,1)} %get-tuple-element.66), channel_id=1, source_target_pairs={{1,0},{3,2},{5,4},{7,6},{9,8},{11,10},{13,12},{15,14},{17,16},{19,... | collective-permute-start | bytes 442376 | tf_op jit(solution)/shard_map/ppermute | solution.py:23
  164.8 15.9 %collective-permute-start.25 = (f32[7,7,768]{2,1,0:T(8,128)S(1)}, f32[7,7,768]{2,1,0:T(8,128)S(1)}, u32[]{:S(2)}, u32[]{:S(2)}) collective-permute-start(f32[7,7,768]{2,1,0:T(8,128)S(1)} %mul.134), channel_id=1, source_target_pairs={{0,2},{2,0},{4,6},{6,4},{8,10},{10,8},{12,14},{14,12},{16,18},{18,... | collective-permute-start | bytes 451592 | tf_op jit(solution)/shard_map/ppermute | solution.py:133
  164.9 15.8 %collective-permute-start.23 = (bf16[2,48,1408]{2,1,0:T(8,128)(2,1)S(1)}, bf16[2,48,1408]{2,1,0:T(8,128)(2,1)S(1)}, u32[]{:S(2)}, u32[]{:S(2)}) collective-permute-start(bf16[2,48,1408]{2,1,0:T(8,128)(2,1)S(1)} %fusion.19), channel_id=1, source_target_pairs={{0,4},{2,6},{4,0},{6,2},{8,12},{10,14},{12,8},{14,10},{16,20},{18,... | collective-permute-start | bytes 811016 | tf_op jit(solution)/shard_map/ppermute | solution.py:133
  165.8 12.1 %collective-permute-start.20 = (bf16[176,384]{1,0:T(8,128)(2,1)S(1)}, bf16[176,384]{1,0:T(8,128)(2,1)S(1)}, u32[]{:S(2)}, u32[]{:S(2)}) collective-permute-start(bf16[176,384]{1,0:T(8,128)(2,1)S(1)} %get-tuple-element.58), channel_id=1, source_target_pairs={{0,8},{2,10},{4,12},{6,14},{8,0},{10,2},{12,4},{14,6},{16,24},{18,... | collective-permute-start | bytes 405512 | tf_op jit(solution)/shard_map/ppermute | solution.py:133
  167.4 13.2 %collective-permute-start.21 = (bf16[176,384]{1,0:T(8,128)(2,1)S(1)}, bf16[176,384]{1,0:T(8,128)(2,1)S(1)}, u32[]{:S(2)}, u32[]{:S(2)}) collective-permute-start(bf16[176,384]{1,0:T(8,128)(2,1)S(1)} %get-tuple-element.60), channel_id=1, source_target_pairs={{0,16},{2,18},{4,20},{6,22},{8,24},{10,26},{12,28},{14,30},{16,0},... | collective-permute-start | bytes 405512 | tf_op jit(solution)/shard_map/ppermute | solution.py:133
  168.3 12.3 %collective-permute-start.22 = (bf16[176,384]{1,0:T(8,128)(2,1)S(1)}, bf16[176,384]{1,0:T(8,128)(2,1)S(1)}, u32[]{:S(2)}, u32[]{:S(2)}) collective-permute-start(bf16[176,384]{1,0:T(8,128)(2,1)S(1)} %get-tuple-element.59), channel_id=1, source_target_pairs={{0,24},{2,26},{4,28},{6,30},{8,16},{10,18},{12,20},{14,22},{16,8},... | collective-permute-start | bytes 405512 | tf_op jit(solution)/shard_map/ppermute | solution.py:133
  185.9 16.3 %collective-permute-start.31 = (f32[7,7,768]{2,1,0:T(8,128)S(1)}, f32[7,7,768]{2,1,0:T(8,128)S(1)}, u32[]{:S(2)}, u32[]{:S(2)}) collective-permute-start(f32[7,7,768]{2,1,0:T(8,128)S(1)} %add.237), channel_id=1, source_target_pairs={{0,4},{2,6},{4,0},{6,2},{8,12},{10,14},{12,8},{14,10},{16,20},{18,... | collective-permute-start | bytes 451592 | tf_op jit(solution)/shard_map/ppermute | solution.py:133
  187.2 14.1 %collective-permute-start.30 = (bf16[176,384]{1,0:T(8,128)(2,1)S(1)}, bf16[176,384]{1,0:T(8,128)(2,1)S(1)}, u32[]{:S(2)}, u32[]{:S(2)}) collective-permute-start(bf16[176,384]{1,0:T(8,128)(2,1)S(1)} %fusion.24), channel_id=1, source_target_pairs={{0,1},{1,0},{2,3},{3,2},{4,5},{5,4},{6,7},{7,6},{8,9},{9,8},{10,11... | collective-permute-start | bytes 405512 | tf_op jit(solution)/shard_map/ppermute | solution.py:137
  189.6 11.2 %collective-permute-start.27 = (bf16[48,1408]{1,0:T(8,128)(2,1)S(1)}, bf16[48,1408]{1,0:T(8,128)(2,1)S(1)}, u32[]{:S(2)}, u32[]{:S(2)}) collective-permute-start(bf16[48,1408]{1,0:T(8,128)(2,1)S(1)} %get-tuple-element.57), channel_id=1, source_target_pairs={{0,16},{2,18},{4,20},{6,22},{8,24},{10,26},{12,28},{14,30},{16,0},... | collective-permute-start | bytes 405512 | tf_op jit(solution)/shard_map/ppermute | solution.py:133
  209.7 13.1 %collective-permute-start.34 = (f32[7,7,768]{2,1,0:T(8,128)S(1)}, f32[7,7,768]{2,1,0:T(8,128)S(1)}, u32[]{:S(2)}, u32[]{:S(2)}) collective-permute-start(f32[7,7,768]{2,1,0:T(8,128)S(1)} %add.243), channel_id=1, source_target_pairs={{0,16},{2,18},{4,20},{6,22},{8,24},{10,26},{12,28},{14,30},{16,0},... | collective-permute-start | bytes 451592 | tf_op jit(solution)/shard_map/ppermute | solution.py:133
  212.0 10.8 %collective-permute-start.35 = (f32[7,7,768]{2,1,0:T(8,128)S(1)}, f32[7,7,768]{2,1,0:T(8,128)S(1)}, u32[]{:S(2)}, u32[]{:S(2)}) collective-permute-start(f32[7,7,768]{2,1,0:T(8,128)S(1)} %add.243), channel_id=1, source_target_pairs={{0,8},{2,10},{4,12},{6,14},{8,0},{10,2},{12,4},{14,6},{16,24},{18,... | collective-permute-start | bytes 451592 | tf_op jit(solution)/shard_map/ppermute | solution.py:133
  (51 other events, 356.8 us)
Sparse Core Ops, SparseCore 0:
  40.6 53.0 all-gather.1

commit v4 on v3

--- a/solution.py
+++ b/solution.py
@@ -172,13 +172,14 @@
 
 def scatter_core(partial):
     line = lax.axis_size("dp") // 4
+    core = place()[2]
     slices = partial.reshape(line, 2, 2, partial.shape[0] // (4 * line), partial.shape[1])
-    return halved_dp(slices, 2, place()[2], 1)
-
-
-def scatter_first(slices):
-    cut = slices.shape[0] // 2
-    return halved_rows(slices[:cut]), halved_dp(slices[cut:], 1, place()[1], 2)
+    kept = pick(slices, core, 2).astype(jnp.float32)
+    return kept, partner(pick(slices, 1 - core, 2), 1).astype(jnp.float32)
+
+
+def scatter_first(low, high):
+    return halved_rows(low), halved_dp(high, 1, place()[1], 2)
 
 
 def scatter_second(low, high):
@@ -196,6 +197,11 @@
 
 def scatter_last(half):
     return both_rows(half.astype(jnp.bfloat16)).astype(jnp.float32)
+
+
+def sum_rows(slice_terms):
+    sent = slice_terms.astype(jnp.bfloat16)
+    return sent.astype(jnp.float32) + other_row(sent).astype(jnp.float32)
 
 
 def gather_line(weight):
@@ -222,16 +228,10 @@
     return slices.reshape(-1, slices.shape[-1])
 
 
-def summed_line(values):
-    line = lax.axis_size("dp") // 4
-    at = place()[0]
-    pieces = [values] + [partner(values, 4 * step) for step in range(1, line)]
-    bit = 1
-    while bit < line:
-        swap = (at // bit) % 2 == 1
-        pieces = [jnp.where(swap, pieces[j ^ bit], pieces[j]) for j in range(line)]
-        bit *= 2
-    return functools.reduce(jnp.add, pieces)
+def summed_everywhere(terms):
+    flat = terms.reshape(-1, terms.shape[-1]).astype(jnp.bfloat16)
+    everyone = lax.all_gather(flat, ("dp", "rows"), axis=0)
+    return jnp.sum(everyone.astype(jnp.float32), axis=0).reshape(terms.shape)
 
 
 def on_device(features, bucket, kernel, up_weight, down_weight, cotangent):
@@ -252,21 +252,21 @@
     inside_cells = inside[..., None]
     masked = jnp.where(inside_cells, features, jnp.zeros((), features.dtype))
     masked_cot = jnp.where(inside_cells, cotangent, jnp.zeros((), cotangent.dtype))
-    down_full = lax.all_gather(down_weight, "dp", axis=0, tiled=True)
-    up_low, up_high = gather_line(up_weight)
+    up_full = lax.all_gather(up_weight, "dp", axis=0, tiled=True)
+    down_low, down_high = gather_line(down_weight)
     rimmed = padded_2(masked, (("rows", 1),), reach)
     padded = jnp.pad(rimmed, ((0, 0), (0, 0), (reach, reach), (0, 0))).astype(jnp.float32)
-    padded, up_low, up_high = lax.optimization_barrier((padded, up_low, up_high))
-    up_low, up_high = gather_middle(up_low), both_rows(up_high)
+    padded, down_low, down_high = lax.optimization_barrier((padded, down_low, down_high))
+    down_low, down_high = gather_middle(down_low), both_rows(down_high)
     convolved = depthwise(padded, kernel, strip_rows, canvas_cols, False)
-    convolved, up_low, up_high = lax.optimization_barrier((convolved, up_low, up_high))
-    up_low, up_high = both_rows(up_low), gather_middle(up_high)
+    convolved, down_low, down_high = lax.optimization_barrier((convolved, down_low, down_high))
+    down_low, down_high = both_rows(down_low), gather_middle(down_high)
+    down_full = gather_core(down_low, down_high)
     convolved = jnp.where(inside_cells, convolved, 0.0)
     unit_norm, inv_std = layer_norm(convolved)
     normed = unit_norm.astype(jnp.bfloat16)
     tokens = normed.reshape(images * strip_rows * canvas_cols, channels)
     cot_rows = masked_cot.reshape(images * strip_rows * canvas_cols, channels)
-    up_full = gather_core(up_low, up_high)
     pre_act = jnp.dot(tokens, up_full, preferred_element_type=jnp.float32)
     hidden, derivative = gelu_parts(pre_act)
     activation = hidden.astype(jnp.bfloat16)
@@ -275,56 +275,57 @@
             activation, cot_rows, (((0,), (0,)), ((), ())), preferred_element_type=jnp.float32
         )
         * grad_scale
-    )
-    down_part = scatter_core(down_part)
-    down_full, down_part = lax.optimization_barrier((down_full, down_part))
-    down_low, down_high = scatter_first(down_part)
+    ).astype(jnp.bfloat16)
+    down_kept, down_came = scatter_core(down_part)
     grad_act = lax.dot_general(
         cot_rows, down_full, (((1,), (1,)), ((), ())), preferred_element_type=jnp.float32
     )
     grad_pre = (grad_act * derivative).astype(jnp.bfloat16)
+    down_part = down_kept + down_came
+    grad_pre, down_part = lax.optimization_barrier((grad_pre, down_part))
     up_part = (
         lax.dot_general(
             tokens, grad_pre, (((0,), (0,)), ((), ())), preferred_element_type=jnp.float32
         )
         * grad_scale
-    )
-    up_part = scatter_core(up_part)
+    ).astype(jnp.bfloat16)
+    up_kept, up_came = scatter_core(up_part)
+    cut = up_kept.shape[0] // 2
+    up_low, up_high = up_kept[:cut] + up_came[:cut], up_kept[cut:] + up_came[cut:]
     grad_rows = lax.dot_general(
         grad_pre, up_full, (((1,), (1,)), ((), ())), preferred_element_type=jnp.float32
     )
     grad_norm = grad_rows.reshape(features.shape)
     grad_conv = jnp.where(inside_cells, norm_backward(grad_norm, unit_norm, inv_std), 0.0)
-    grad_conv, up_part, down_low, down_high = lax.optimization_barrier(
-        (grad_conv, up_part, down_low, down_high)
-    )
-    down_part = scatter_second(down_low, down_high)
-    up_low, up_high = scatter_first(up_part)
+    grad_conv, up_low, up_high, down_part = lax.optimization_barrier(
+        (grad_conv, up_low, up_high, down_part)
+    )
     grad_rimmed = padded_2(grad_conv.astype(jnp.bfloat16), (("rows", 1),), reach).astype(
         grad_conv.dtype
     )
     kernel_part = kernel_terms(grad_conv, padded, kernel.shape[0]) * grad_scale
-    kernel_part, grad_rimmed, down_part, up_low, up_high = lax.optimization_barrier(
-        (kernel_part, grad_rimmed, down_part, up_low, up_high)
-    )
-    kernel_part = kernel_part + partner(kernel_part, 1)
-    down_half = scatter_line(down_part)
-    up_part = scatter_second(up_low, up_high)
+    down_part = halved_dp(down_part, 1, place()[1], 2)
+    kernel_part, grad_rimmed, up_low, up_high = lax.optimization_barrier(
+        (kernel_part, grad_rimmed, up_low, up_high)
+    )
+    kernel_grad = summed_everywhere(kernel_part)
+    up_low, up_high = scatter_first(up_low, up_high)
     grad_padded = jnp.pad(grad_rimmed, ((0, 0), (0, 0), (reach, reach), (0, 0)))
     feature_grad = jnp.where(
         inside_cells,
         masked_cot + depthwise(grad_padded, kernel, strip_rows, canvas_cols, True),
         0.0,
     ).astype(jnp.bfloat16)
-    feature_grad, activation, down_half, up_part, kernel_part = lax.optimization_barrier(
-        (feature_grad, activation, down_half, up_part, kernel_part)
-    )
-    kernel_part = kernel_part + partner(kernel_part, 2)
-    up_half = scatter_line(up_part)
+    feature_grad, activation, down_part, up_low, up_high = lax.optimization_barrier(
+        (feature_grad, activation, down_part, up_low, up_high)
+    )
+    up_part = scatter_second(up_low, up_high)
+    down_part = scatter_line(down_part)
     branch = jnp.dot(activation, down_full, preferred_element_type=jnp.float32)
     block_out = (masked + branch.reshape(features.shape)).astype(jnp.bfloat16)
-    kernel_grad = summed_line(kernel_part + other_row(kernel_part))
-    down_grad = scatter_last(down_half)
+    block_out, up_part, down_part = lax.optimization_barrier((block_out, up_part, down_part))
+    up_half = scatter_line(up_part)
+    down_grad = sum_rows(down_part)
     up_grad = scatter_last(up_half)
     return (block_out, feature_grad, up_grad, down_grad, kernel_grad)
 

time: 231 us -> 241 us (1.043)
  waiting for transfers between devices: 66.5 us -> 90.7 us
  starting transfers between devices: 47.9 us -> 38.6 us
  other arithmetic: 38.4 us -> 32.8 us
    ppermute x23 -> x17, waiting for transfers between devices: 34.3 us -> 76 us  [partner(): return lax.ppermute(values, 'dp', [(i, i ^ bit) for i in range(count)])]
    add x6 -> x3, other arithmetic: 13 us -> 2.43 us  [halved_dp(): return pick(slices, mine, axis) + partner(sent, bit).astype(jnp.float32)]
    ppermute x2, waiting for transfers between devices: 7.14 us -> 0.01 us  [padded_2(): lax.ppermute(lax.slice_in_dim(block, block.shape[dim] - width, None, axis...]
    ppermute x23 -> x17, starting transfers between devices: 26.4 us -> 19.8 us  [partner(): return lax.ppermute(values, 'dp', [(i, i ^ bit) for i in range(count)])]
    ppermute x9 -> x6, starting transfers between devices: 12.3 us -> 5.78 us  [other_row(): return lax.ppermute(values, 'rows', [(0, 1), (1, 0)])]
    ppermute x9 -> x6, waiting for transfers between devices: 12.6 us -> 6.22 us  [other_row(): return lax.ppermute(values, 'rows', [(0, 1), (1, 0)])]
    dynamic_slice x0 -> x4, local copies, waits for them, and re-layouts: none -> 6.28 us  [pick(): return lax.dynamic_index_in_dim(values, which, axis, keepdims=False)]
    add x4 -> x3, other arithmetic: 0.82 us -> 6.93 us  [the longest x1 4.26 us: on_device(): down_part = down_kept + down_came]
  transfers between devices with their start and end apart: 37 -> 29, of which waited for: 15 -> 10; matrix products, arithmetic and copies ran while one was open for 26% -> 22% of each run, Pallas kernels for 5% -> 5%
where the time goes in v4:
time: 241 us; the launch traced here: 240 us
  waiting for transfers between devices  90.7 us (38%)
  starting transfers between devices  38.6 us (16%)
  other arithmetic  32.8 us (14%)
  local copies, waits for them, and re-layouts  24.2 us (10%)
  matrix products  21 us (9%)
  Pallas kernels  17.2 us (7%)
  between operations  15.4 us (6%)
    ppermute x17, waiting for transfers between devices, partner(): return lax.ppermute(values, 'dp', [(i, i ^ bit) for i in range(count)])  76 us
    ppermute x17, starting transfers between devices, partner(): return lax.ppermute(values, 'dp', [(i, i ^ bit) for i in range(count)])  19.8 us
    pallas_call x2, Pallas kernels, depthwise(): pl.pallas_call(functools.partial(depthwise_kernel, flipped), grid=(images...  11.7 us
    ppermute x2, starting transfers between devices, padded_2(): lax.ppermute(lax.slice_in_dim(block, block.shape[dim] - width, None, axis...  10.4 us
    unnamed x48, local copies, waits for them, and re-layouts  8.34 us
    all_gather x1, waiting for transfers between devices, on_device(): up_full = lax.all_gather(up_weight, 'dp', axis=0, tiled=True)  7.8 us
    dot_general x1, matrix products, on_device(): pre_act = jnp.dot(tokens, up_full, preferred_element_type=jnp.float32)  6.4 us
    dynamic_slice x4, local copies, waits for them, and re-layouts, pick(): return lax.dynamic_index_in_dim(values, which, axis, keepdims=False)  6.28 us
  transfers between devices with their start and end apart: 29, of which 10 were waited for; matrix products, arithmetic and copies ran while one was open for 22% of the time, Pallas kernels for 5%

profile of v4, /device:TPU:0, one launch (start us, length us, event | category | flops | bytes accessed | tf_op | source)
XLA Modules:
  0.0 239.9 jit_solution(4610257512096396498)
XLA Ops:
  8.9 5.1 %collective-permute-start.2 = (bf16[176,384]{1,0:T(8,128)(2,1)S(1)}, bf16[176,384]{1,0:T(8,128)(2,1)S(1)}, u32[]{:S(2)}, u32[]{:S(2)}) collective-permute-start(bf16[176,384]{1,0:T(8,128)(2,1)S(1)} %constant_dynamic-slice_fusion.4), channel_id=1, source_target_pairs={{0,24},{2,26},{4,28},{6,30},{8,16},{10,18},{12,20},{14,22},{16,8},... | collective-permute-start | bytes 405512 | tf_op jit(solution)/shard_map/ppermute | solution.py:133
  19.2 4.6 %collective-permute-start = (bf16[1,3,32,768]{3,2,1,0:T(8,128)(2,1)S(1)}, bf16[1,3,32,768]{3,2,1,0:T(8,128)(2,1)S(1)}, u32[]{:S(2)}, u32[]{:S(2)}) collective-permute-start(bf16[1,3,32,768]{3,2,1,0:T(8,128)(2,1)S(1)} %get-tuple-element.73), channel_id=1, source_target_pairs={{0,1},{2,3},{4,5},{6,7},{8,9},{10,11},{12,13},{14,15},{16,17},{18,... | collective-permute-start | bytes 442376 | tf_op jit(solution)/shard_map/ppermute | solution.py:20
  23.8 3.6 %collective-permute-done.3 = bf16[176,384]{1,0:T(8,128)(2,1)S(1)} collective-permute-done((bf16[176,384]{1,0:T(8,128)(2,1)S(1)}, bf16[176,384]{1,0:T(8,128)(2,1)S(1)}, u32[]{:S(2)}, u32[]{:S(2)}) %collective-permute-start.3) | collective-permute-done | bytes 135200 | tf_op jit(solution)/shard_map/ppermute | solution.py:133
  34.7 5.9 %shard_map.101 = f32[1,16,32,768]{3,2,1,0:T(8,128)S(1)} custom-call(f32[1,22,38,768]{3,2,1,0:T(8,128)S(1)} %copy-done, f32[7,7,768]{2,1,0:T(8,128)S(1)} %copy-done.2), custom_call_target="tpu_custom_call" | custom-call | flops 38535168 | bytes 2568192 | tf_op jit(solution)/shard_map/pallas_call | solution.py:65
  42.2 21.5 %collective-permute-done.8 = bf16[2,176,768]{2,1,0:T(8,128)(2,1)S(1)} collective-permute-done((bf16[2,176,768]{2,1,0:T(8,128)(2,1)S(1)}, bf16[2,176,768]{2,1,0:T(8,128)(2,1)S(1)}, u32[]{:S(2)}, u32[]{:S(2)}) %collective-permute-start.8) | collective-permute-done | bytes 540704 | tf_op jit(solution)/shard_map/ppermute | solution.py:133
  66.6 7.8 %all-gather.3.cloned.1.call-done = bf16[768,2816]{1,0:T(8,128)(2,1)} async-done(((bf16[48,2816]{1,0:T(8,128)(2,1)}), bf16[768,2816]{1,0:T(8,128)(2,1)}) %all-gather.3.cloned.1.call-update) | async-done | bytes 4325392 | tf_op jit(solution)/shard_map/all_gather | solution.py:255
  74.5 6.4 %multiply_convert_fusion.2 = (bf16[512,2816]{1,0:T(8,128)(2,1)S(1)}, f32[512,2816]{1,0:T(8,128)}) fusion(bf16[512,768]{1,0:T(8,128)(2,1)} %bitcast.114, bf16[768,2816]{1,0:T(8,128)(2,1)} %all-gather.3.cloned.1.call-done), kind=kOutput, calls=%fused_computation.9 | convolution fusion | flops 2221801472 | bytes 13762560 | tf_op jit(solution)/shard_map/dot_general | solution.py:270
  89.7 2.6 %slice-done.4 = s8[4194304]{0:T(1024)(128)(4,1)S(1)} async-done(((s8[5767168]{0:T(1024)(128)(4,1)}), s8[4194304]{0:T(1024)(128)(4,1)S(1)}, s32[]{:S(2)}) %slice-start.4) | async-done | bytes 4194328
  93.5 3.9 %fusion.5 = bf16[512,2816]{1,0:T(8,128)(2,1)S(1)} fusion(f32[512,2816]{1,0:T(8,128)S(1)} %bitcast.120, bf16[512,768]{1,0:T(8,128)(2,1)S(1)} %bitcast.113, bf16[2816,768]{1,0:T(8,128)(2,1)S(1)} %bitcast.106), kind=kOutput, calls=%fused_computation.8 | convolution fusion | flops 2229010432 | bytes 13762560 | tf_op jit(solution)/shard_map/dot_general | solution.py:280
  97.4 4.3 %convert_add_fusion = f32[4,2,176,768]{3,2,0,1:T(8,128)} fusion(bf16[4,2,176,768]{3,2,0,1:T(8,128)(2,1)} %collective-permute-done.10, bf16[4,2,1,176,768]{4,3,2,1,0:T(8,128)(2,1)S(1)} %copy-done.4), kind=kLoop, calls=%fused_computation.13 | loop fusion | flops 3244032 | bytes 8650752 | tf_op jit(solution)/shard_map/add | solution.py:284
  107.5 2.5 %fusion.31 = (f32[512]{0:T(512)S(1)}, f32[512,768]{1,0:T(8,128)S(1)}) fusion(bf16[512,2816]{1,0:T(8,128)(2,1)S(1)} %fusion.5, bf16[768,2816]{1,0:T(8,128)(2,1)S(1)} %bitcast.117), kind=kOutput, calls=%fused_computation.118 | convolution fusion | flops 2214985216 | bytes 8783872 | tf_op jit(solution)/shard_map/dot_general | solution.py:295
  117.1 5.4 %shard_map.102 = f32[1,49,8,768]{3,2,1,0:T(8,128)S(1)} custom-call(f32[1,16,32,768]{3,2,1,0:T(8,128)S(1)} %multiply_select_fusion.grad_ref, f32[1,22,38,768]{3,2,1,0:T(8,128)S(1)} %copy-done.1), custom_call_target="tpu_custom_call" | custom-call | flops 38535168 | bytes 2568192 | tf_op jit(solution)/shard_map/pallas_call | solution.py:102
  125.6 5.9 %collective-permute-start.12 = (bf16[1,3,32,768]{3,2,1,0:T(8,128)(2,1)}, bf16[1,3,32,768]{3,2,1,0:T(8,128)(2,1)}, u32[]{:S(2)}, u32[]{:S(2)}) collective-permute-start(bf16[1,3,32,768]{3,2,1,0:T(8,128)(2,1)} %get-tuple-element.71), channel_id=1, source_target_pairs={{0,1},{2,3},{4,5},{6,7},{8,9},{10,11},{12,13},{14,15},{16,17},{18,... | collective-permute-start | bytes 442376 | tf_op jit(solution)/shard_map/ppermute | solution.py:20
  133.5 2.7 %fusion.14 = bf16[4,176,768]{2,1,0:T(8,128)(2,1)} fusion(f32[4,2,176,768]{3,2,0,1:T(8,128)} %convert_add_fusion, s32[]{:T(128)S(6)} %select_n.272), kind=kLoop, calls=%fused_computation.44 | loop fusion | bytes 2162692 | tf_op jit(solution)/shard_map/convert_element_type | solution.py:150
  142.5 5.9 %shard_map.103 = f32[1,16,32,768]{3,2,1,0:T(8,128)S(1)} custom-call(f32[1,22,38,768]{3,2,1,0:T(8,128)S(1)} %pad.9.padded_ref, f32[7,7,768]{2,1,0:T(8,128)S(1)} %copy-done.2), custom_call_target="tpu_custom_call" | custom-call | flops 38535168 | bytes 2568192 | tf_op jit(solution)/shard_map/pallas_call | solution.py:65
  150.3 3.6 %collective-permute-done.15 = bf16[2,2,48,1408]{3,2,0,1:T(8,128)(2,1)S(1)} collective-permute-done((bf16[2,2,48,1408]{3,2,0,1:T(8,128)(2,1)}, bf16[2,2,48,1408]{3,2,0,1:T(8,128)(2,1)S(1)}, u32[]{:S(2)}, u32[]{:S(2)}) %collective-permute-start.15) | collective-permute-done | bytes 540704 | tf_op jit(solution)/shard_map/ppermute | solution.py:137
  155.3 18.7 %collective-permute-done.16 = bf16[2,48,2816]{2,1,0:T(8,128)(2,1)S(1)} collective-permute-done((bf16[2,48,2816]{2,1,0:T(8,128)(2,1)}, bf16[2,48,2816]{2,1,0:T(8,128)(2,1)S(1)}, u32[]{:S(2)}, u32[]{:S(2)}) %collective-permute-start.16) | collective-permute-done | bytes 540704 | tf_op jit(solution)/shard_map/ppermute | solution.py:133
  181.8 3.3 %fusion.7 = bf16[1,16,32,768]{3,2,1,0:T(8,128)(2,1)} fusion(bf16[1,16,32,768]{3,2,1,0:T(8,128)(2,1)S(1)} %copy-done.9, bf16[16,32,2816]{2,1,0:T(8,128)(2,1)S(1)} %bitcast.118, bf16[2816,768,1]{1,0,2:T(8,128)(2,1)S(1)} %bitcast.109), kind=kOutput, calls=%fused_computation.31 | convolution fusion | flops 2215772160 | bytes 8781824 | tf_op jit(solution)/shard_map/dot_general | solution.py:324
  185.2 4.5 %collective-permute-done.21 = bf16[176,768]{1,0:T(8,128)(2,1)S(1)} collective-permute-done((bf16[176,768]{1,0:T(8,128)(2,1)S(1)}, bf16[176,768]{1,0:T(8,128)(2,1)S(1)}, u32[]{:S(2)}, u32[]{:S(2)}) %collective-permute-start.21) | collective-permute-done | bytes 270368 | tf_op jit(solution)/shard_map/ppermute | solution.py:133
  189.7 18.9 %collective-permute-done.20 = bf16[176,768]{1,0:T(8,128)(2,1)S(1)} collective-permute-done((bf16[176,768]{1,0:T(8,128)(2,1)S(1)}, bf16[176,768]{1,0:T(8,128)(2,1)S(1)}, u32[]{:S(2)}, u32[]{:S(2)}) %collective-permute-start.20) | collective-permute-done | bytes 270368 | tf_op jit(solution)/shard_map/ppermute | solution.py:133
  210.4 3.1 %collective-permute-start.22 = (bf16[48,1408]{1,0:T(8,128)(2,1)S(1)}, bf16[48,1408]{1,0:T(8,128)(2,1)S(1)}, u32[]{:S(2)}, u32[]{:S(2)}) collective-permute-start(bf16[48,1408]{1,0:T(8,128)(2,1)S(1)} %get-tuple-element.64), channel_id=1, source_target_pairs={{0,8},{2,10},{4,12},{6,14},{8,0},{10,2},{12,4},{14,6},{16,24},{18,... | collective-permute-start | bytes 405512 | tf_op jit(solution)/shard_map/ppermute | solution.py:133
  215.3 3.2 %collective-permute-done.24 = bf16[48,1408]{1,0:T(8,128)(2,1)S(1)} collective-permute-done((bf16[48,1408]{1,0:T(8,128)(2,1)S(1)}, bf16[48,1408]{1,0:T(8,128)(2,1)S(1)}, u32[]{:S(2)}, u32[]{:S(2)}) %collective-permute-start.24) | collective-permute-done | bytes 135200 | tf_op jit(solution)/shard_map/ppermute | solution.py:133
  218.5 5.6 %collective-permute-done.23 = bf16[48,1408]{1,0:T(8,128)(2,1)S(1)} collective-permute-done((bf16[48,1408]{1,0:T(8,128)(2,1)S(1)}, bf16[48,1408]{1,0:T(8,128)(2,1)S(1)}, u32[]{:S(2)}, u32[]{:S(2)}) %collective-permute-start.23) | collective-permute-done | bytes 135200 | tf_op jit(solution)/shard_map/ppermute | solution.py:133
  226.7 2.6 %collective-permute-done.25 = bf16[48,1408]{1,0:T(8,128)(2,1)S(1)} collective-permute-done((bf16[48,1408]{1,0:T(8,128)(2,1)S(1)}, bf16[48,1408]{1,0:T(8,128)(2,1)S(1)}, u32[]{:S(2)}, u32[]{:S(2)}) %collective-permute-start.25) | collective-permute-done | bytes 135200 | tf_op jit(solution)/shard_map/ppermute | solution.py:137
  (162 shorter events, 73.1 us)
Async XLA Ops:
  7.2 67.3 %all-gather.3.cloned.1.call-start = ((), (), s32[]{:S(2)}) async-start(), calls=%async_computation | async-start | bytes 4595712 | tf_op jit(solution)/shard_map/all_gather | solution.py:255
  7.9 222.2 %all-gather.5.cloned.1.call-start = ((), (), s32[]{:S(2)}) async-start(), calls=%async_computation.1 | async-start | bytes 2838528 | tf_op jit(solution)/shard_map/all_gather | solution.py:233
  8.9 14.9 %collective-permute-start.2 = (bf16[176,384]{1,0:T(8,128)(2,1)S(1)}, bf16[176,384]{1,0:T(8,128)(2,1)S(1)}, u32[]{:S(2)}, u32[]{:S(2)}) collective-permute-start(bf16[176,384]{1,0:T(8,128)(2,1)S(1)} %constant_dynamic-slice_fusion.4), channel_id=1, source_target_pairs={{0,24},{2,26},{4,28},{6,30},{8,16},{10,18},{12,20},{14,22},{16,8},... | collective-permute-start | bytes 405512 | tf_op jit(solution)/shard_map/ppermute | solution.py:133
  14.0 13.4 %collective-permute-start.3 = (bf16[176,384]{1,0:T(8,128)(2,1)S(1)}, bf16[176,384]{1,0:T(8,128)(2,1)S(1)}, u32[]{:S(2)}, u32[]{:S(2)}) collective-permute-start(bf16[176,384]{1,0:T(8,128)(2,1)S(1)} %constant_dynamic-slice_fusion.4), channel_id=1, source_target_pairs={{0,16},{2,18},{4,20},{6,22},{8,24},{10,26},{12,28},{14,30},{16,0},... | collective-permute-start | bytes 405512 | tf_op jit(solution)/shard_map/ppermute | solution.py:133
  14.0 13.4 %collective-permute-start.4 = (bf16[176,384]{1,0:T(8,128)(2,1)S(1)}, bf16[176,384]{1,0:T(8,128)(2,1)S(1)}, u32[]{:S(2)}, u32[]{:S(2)}) collective-permute-start(bf16[176,384]{1,0:T(8,128)(2,1)S(1)} %constant_dynamic-slice_fusion.4), channel_id=1, source_target_pairs={{0,8},{2,10},{4,12},{6,14},{8,0},{10,2},{12,4},{14,6},{16,24},{18,... | collective-permute-start | bytes 405512 | tf_op jit(solution)/shard_map/ppermute | solution.py:133
  17.9 9.8 %collective-permute-start.1 = (bf16[1,3,32,768]{3,2,1,0:T(8,128)(2,1)S(1)}, bf16[1,3,32,768]{3,2,1,0:T(8,128)(2,1)S(1)}, u32[]{:S(2)}, u32[]{:S(2)}) collective-permute-start(bf16[1,3,32,768]{3,2,1,0:T(8,128)(2,1)S(1)} %get-tuple-element.74), channel_id=1, source_target_pairs={{1,0},{3,2},{5,4},{7,6},{9,8},{11,10},{13,12},{15,14},{17,16},{19,... | collective-permute-start | bytes 442376 | tf_op jit(solution)/shard_map/ppermute | solution.py:23
  29.5 11.1 %collective-permute-start.5 = (bf16[2,176,384]{2,1,0:T(8,128)(2,1)S(1)}, bf16[2,176,384]{2,1,0:T(8,128)(2,1)S(1)}, u32[]{:S(2)}, u32[]{:S(2)}) collective-permute-start(bf16[2,176,384]{2,1,0:T(8,128)(2,1)S(1)} %get-tuple-element.30), channel_id=1, source_target_pairs={{0,4},{2,6},{4,0},{6,2},{8,12},{10,14},{12,8},{14,10},{16,20},{18,... | collective-permute-start | bytes 811016 | tf_op jit(solution)/shard_map/ppermute | solution.py:133
  40.9 22.8 %collective-permute-start.8 = (bf16[2,176,768]{2,1,0:T(8,128)(2,1)S(1)}, bf16[2,176,768]{2,1,0:T(8,128)(2,1)S(1)}, u32[]{:S(2)}, u32[]{:S(2)}) collective-permute-start(bf16[2,176,768]{2,1,0:T(8,128)(2,1)S(1)} %pad_maximum_fusion.3), channel_id=1, source_target_pairs={{0,4},{2,6},{4,0},{6,2},{8,12},{10,14},{12,8},{14,10},{16,20},{18,... | collective-permute-start | bytes 1622024 | tf_op jit(solution)/shard_map/ppermute | solution.py:133
  41.1 22.6 %collective-permute-start.7 = (bf16[2,2,176,384]{3,2,0,1:T(8,128)(2,1)S(1)}, bf16[2,2,176,384]{3,2,0,1:T(8,128)(2,1)S(1)}, u32[]{:S(2)}, u32[]{:S(2)}) collective-permute-start(bf16[2,2,176,384]{3,2,0,1:T(8,128)(2,1)S(1)} %pad_maximum_fusion.2), channel_id=1, source_target_pairs={{0,1},{1,0},{2,3},{3,2},{4,5},{5,4},{6,7},{7,6},{8,9},{9,8},{10,11... | collective-permute-start | bytes 1622024 | tf_op jit(solution)/shard_map/ppermute | solution.py:137
  65.5 21.3 %collective-permute-start.9 = (bf16[4,2,176,768]{3,2,0,1:T(8,128)(2,1)}, bf16[4,2,176,768]{3,2,0,1:T(8,128)(2,1)}, u32[]{:S(2)}, u32[]{:S(2)}) collective-permute-start(bf16[4,2,176,768]{3,2,0,1:T(8,128)(2,1)} %maximum_maximum_fusion), channel_id=1, source_target_pairs={{0,2},{2,0},{4,6},{6,4},{8,10},{10,8},{12,14},{14,12},{16,18},{18,... | collective-permute-start | bytes 6488072 | tf_op jit(solution)/shard_map/ppermute | solution.py:133
  86.5 10.8 %collective-permute-start.10 = (bf16[4,2,176,768]{3,2,0,1:T(8,128)(2,1)}, bf16[4,2,176,768]{3,2,0,1:T(8,128)(2,1)}, u32[]{:S(2)}, u32[]{:S(2)}) collective-permute-start(bf16[4,2,176,768]{3,2,0,1:T(8,128)(2,1)} %bitcast.104), channel_id=1, source_target_pairs={{0,2},{2,0},{4,6},{6,4},{8,10},{10,8},{12,14},{14,12},{16,18},{18,... | collective-permute-start | bytes 6488072 | tf_op jit(solution)/shard_map/ppermute | solution.py:133
  124.3 12.4 %collective-permute-start.13 = (bf16[1,3,32,768]{3,2,1,0:T(8,128)(2,1)}, bf16[1,3,32,768]{3,2,1,0:T(8,128)(2,1)}, u32[]{:S(2)}, u32[]{:S(2)}) collective-permute-start(bf16[1,3,32,768]{3,2,1,0:T(8,128)(2,1)} %get-tuple-element.72), channel_id=1, source_target_pairs={{1,0},{3,2},{5,4},{7,6},{9,8},{11,10},{13,12},{15,14},{17,16},{19,... | collective-permute-start | bytes 442376 | tf_op jit(solution)/shard_map/ppermute | solution.py:23
  125.6 11.1 %collective-permute-start.12 = (bf16[1,3,32,768]{3,2,1,0:T(8,128)(2,1)}, bf16[1,3,32,768]{3,2,1,0:T(8,128)(2,1)}, u32[]{:S(2)}, u32[]{:S(2)}) collective-permute-start(bf16[1,3,32,768]{3,2,1,0:T(8,128)(2,1)} %get-tuple-element.71), channel_id=1, source_target_pairs={{0,1},{2,3},{4,5},{6,7},{8,9},{10,11},{12,13},{14,15},{16,17},{18,... | collective-permute-start | bytes 442376 | tf_op jit(solution)/shard_map/ppermute | solution.py:20
  136.1 38.0 %collective-permute-start.14 = (bf16[4,176,768]{2,1,0:T(8,128)(2,1)}, bf16[4,176,768]{2,1,0:T(8,128)(2,1)}, u32[]{:S(2)}, u32[]{:S(2)}) collective-permute-start(bf16[4,176,768]{2,1,0:T(8,128)(2,1)} %fusion.14), channel_id=1, source_target_pairs={{0,4},{2,6},{4,0},{6,2},{8,12},{10,14},{12,8},{14,10},{16,20},{18,... | collective-permute-start | bytes 3244040 | tf_op jit(solution)/shard_map/ppermute | solution.py:133
  140.2 13.8 %collective-permute-start.15 = (bf16[2,2,48,1408]{3,2,0,1:T(8,128)(2,1)}, bf16[2,2,48,1408]{3,2,0,1:T(8,128)(2,1)S(1)}, u32[]{:S(2)}, u32[]{:S(2)}) collective-permute-start(bf16[2,2,48,1408]{3,2,0,1:T(8,128)(2,1)} %dynamic-slice_convert_fusion.2), channel_id=1, source_target_pairs={{0,1},{1,0},{2,3},{3,2},{4,5},{5,4},{6,7},{7,6},{8,9},{9,8},{10,11... | collective-permute-start | bytes 1622024 | tf_op jit(solution)/shard_map/ppermute | solution.py:137
  141.1 32.9 %collective-permute-start.16 = (bf16[2,48,2816]{2,1,0:T(8,128)(2,1)}, bf16[2,48,2816]{2,1,0:T(8,128)(2,1)S(1)}, u32[]{:S(2)}, u32[]{:S(2)}) collective-permute-start(bf16[2,48,2816]{2,1,0:T(8,128)(2,1)} %fusion.16), channel_id=1, source_target_pairs={{0,4},{2,6},{4,0},{6,2},{8,12},{10,14},{12,8},{14,10},{16,20},{18,... | collective-permute-start | bytes 1622024 | tf_op jit(solution)/shard_map/ppermute | solution.py:133
  176.6 32.2 %collective-permute-start.17 = (bf16[2,48,1408]{2,1,0:T(8,128)(2,1)S(1)}, bf16[2,48,1408]{2,1,0:T(8,128)(2,1)S(1)}, u32[]{:S(2)}, u32[]{:S(2)}) collective-permute-start(bf16[2,48,1408]{2,1,0:T(8,128)(2,1)S(1)} %fusion.19), channel_id=1, source_target_pairs={{0,4},{2,6},{4,0},{6,2},{8,12},{10,14},{12,8},{14,10},{16,20},{18,... | collective-permute-start | bytes 811016 | tf_op jit(solution)/shard_map/ppermute | solution.py:133
  177.3 12.4 %collective-permute-start.21 = (bf16[176,768]{1,0:T(8,128)(2,1)S(1)}, bf16[176,768]{1,0:T(8,128)(2,1)S(1)}, u32[]{:S(2)}, u32[]{:S(2)}) collective-permute-start(bf16[176,768]{1,0:T(8,128)(2,1)S(1)} %get-tuple-element.62), channel_id=1, source_target_pairs={{0,24},{2,26},{4,28},{6,30},{8,16},{10,18},{12,20},{14,22},{16,8},... | collective-permute-start | bytes 811016 | tf_op jit(solution)/shard_map/ppermute | solution.py:133
  179.2 29.4 %collective-permute-start.20 = (bf16[176,768]{1,0:T(8,128)(2,1)S(1)}, bf16[176,768]{1,0:T(8,128)(2,1)S(1)}, u32[]{:S(2)}, u32[]{:S(2)}) collective-permute-start(bf16[176,768]{1,0:T(8,128)(2,1)S(1)} %get-tuple-element.63), channel_id=1, source_target_pairs={{0,16},{2,18},{4,20},{6,22},{8,24},{10,26},{12,28},{14,30},{16,0},... | collective-permute-start | bytes 811016 | tf_op jit(solution)/shard_map/ppermute | solution.py:133
  180.1 28.5 %collective-permute-start.19 = (bf16[176,768]{1,0:T(8,128)(2,1)S(1)}, bf16[176,768]{1,0:T(8,128)(2,1)S(1)}, u32[]{:S(2)}, u32[]{:S(2)}) collective-permute-start(bf16[176,768]{1,0:T(8,128)(2,1)S(1)} %get-tuple-element.61), channel_id=1, source_target_pairs={{0,8},{2,10},{4,12},{6,14},{8,0},{10,2},{12,4},{14,6},{16,24},{18,... | collective-permute-start | bytes 811016 | tf_op jit(solution)/shard_map/ppermute | solution.py:133
  209.0 9.5 %collective-permute-start.24 = (bf16[48,1408]{1,0:T(8,128)(2,1)S(1)}, bf16[48,1408]{1,0:T(8,128)(2,1)S(1)}, u32[]{:S(2)}, u32[]{:S(2)}) collective-permute-start(bf16[48,1408]{1,0:T(8,128)(2,1)S(1)} %get-tuple-element.65), channel_id=1, source_target_pairs={{0,24},{2,26},{4,28},{6,30},{8,16},{10,18},{12,20},{14,22},{16,8},... | collective-permute-start | bytes 405512 | tf_op jit(solution)/shard_map/ppermute | solution.py:133
  210.4 13.7 %collective-permute-start.23 = (bf16[48,1408]{1,0:T(8,128)(2,1)S(1)}, bf16[48,1408]{1,0:T(8,128)(2,1)S(1)}, u32[]{:S(2)}, u32[]{:S(2)}) collective-permute-start(bf16[48,1408]{1,0:T(8,128)(2,1)S(1)} %get-tuple-element.66), channel_id=1, source_target_pairs={{0,16},{2,18},{4,20},{6,22},{8,24},{10,26},{12,28},{14,30},{16,0},... | collective-permute-start | bytes 405512 | tf_op jit(solution)/shard_map/ppermute | solution.py:133
  210.4 13.7 %collective-permute-start.22 = (bf16[48,1408]{1,0:T(8,128)(2,1)S(1)}, bf16[48,1408]{1,0:T(8,128)(2,1)S(1)}, u32[]{:S(2)}, u32[]{:S(2)}) collective-permute-start(bf16[48,1408]{1,0:T(8,128)(2,1)S(1)} %get-tuple-element.64), channel_id=1, source_target_pairs={{0,8},{2,10},{4,12},{6,14},{8,0},{10,2},{12,4},{14,6},{16,24},{18,... | collective-permute-start | bytes 405512 | tf_op jit(solution)/shard_map/ppermute | solution.py:133
  213.4 12.4 %collective-permute-start.26 = (bf16[176,768]{1,0:T(8,128)(2,1)S(1)}, bf16[176,768]{1,0:T(8,128)(2,1)S(1)}, u32[]{:S(2)}, u32[]{:S(2)}) collective-permute-start(bf16[176,768]{1,0:T(8,128)(2,1)S(1)} %fusion.18), channel_id=1, source_target_pairs={{0,1},{1,0},{2,3},{3,2},{4,5},{5,4},{6,7},{7,6},{8,9},{9,8},{10,11... | collective-permute-start | bytes 811016 | tf_op jit(solution)/shard_map/ppermute | solution.py:137
  (29 other events, 212.2 us)
Sparse Core Ops, SparseCore 0:
  10.3 64.1 all-gather.2
  150.4 72.5 all-gather.4

commit v5 on v4

--- a/solution.py
+++ b/solution.py
@@ -228,10 +228,16 @@
     return slices.reshape(-1, slices.shape[-1])
 
 
-def summed_everywhere(terms):
-    flat = terms.reshape(-1, terms.shape[-1]).astype(jnp.bfloat16)
-    everyone = lax.all_gather(flat, ("dp", "rows"), axis=0)
-    return jnp.sum(everyone.astype(jnp.float32), axis=0).reshape(terms.shape)
+def summed_line(values):
+    line = lax.axis_size("dp") // 4
+    at = place()[0]
+    pieces = [values] + [partner(values, 4 * step) for step in range(1, line)]
+    bit = 1
+    while bit < line:
+        swap = (at // bit) % 2 == 1
+        pieces = [jnp.where(swap, pieces[j ^ bit], pieces[j]) for j in range(line)]
+        bit *= 2
+    return functools.reduce(jnp.add, pieces)
 
 
 def on_device(features, bucket, kernel, up_weight, down_weight, cotangent):
@@ -297,18 +303,17 @@
     )
     grad_norm = grad_rows.reshape(features.shape)
     grad_conv = jnp.where(inside_cells, norm_backward(grad_norm, unit_norm, inv_std), 0.0)
-    grad_conv, up_low, up_high, down_part = lax.optimization_barrier(
-        (grad_conv, up_low, up_high, down_part)
-    )
+    grad_conv, up_low, up_high = lax.optimization_barrier((grad_conv, up_low, up_high))
     grad_rimmed = padded_2(grad_conv.astype(jnp.bfloat16), (("rows", 1),), reach).astype(
         grad_conv.dtype
     )
     kernel_part = kernel_terms(grad_conv, padded, kernel.shape[0]) * grad_scale
     down_part = halved_dp(down_part, 1, place()[1], 2)
-    kernel_part, grad_rimmed, up_low, up_high = lax.optimization_barrier(
-        (kernel_part, grad_rimmed, up_low, up_high)
-    )
-    kernel_grad = summed_everywhere(kernel_part)
+    kernel_part, grad_rimmed, up_low, up_high, down_part = lax.optimization_barrier(
+        (kernel_part, grad_rimmed, up_low, up_high, down_part)
+    )
+    kernel_part = kernel_part + partner(kernel_part, 1)
+    down_part = scatter_line(down_part)
     up_low, up_high = scatter_first(up_low, up_high)
     grad_padded = jnp.pad(grad_rimmed, ((0, 0), (0, 0), (reach, reach), (0, 0)))
     feature_grad = jnp.where(
@@ -316,14 +321,15 @@
         masked_cot + depthwise(grad_padded, kernel, strip_rows, canvas_cols, True),
         0.0,
     ).astype(jnp.bfloat16)
-    feature_grad, activation, down_part, up_low, up_high = lax.optimization_barrier(
-        (feature_grad, activation, down_part, up_low, up_high)
+    feature_grad, activation, down_part, up_low, up_high, kernel_part = lax.optimization_barrier(
+        (feature_grad, activation, down_part, up_low, up_high, kernel_part)
     )
     up_part = scatter_second(up_low, up_high)
-    down_part = scatter_line(down_part)
+    kernel_part = kernel_part + partner(kernel_part, 2)
     branch = jnp.dot(activation, down_full, preferred_element_type=jnp.float32)
     block_out = (masked + branch.reshape(features.shape)).astype(jnp.bfloat16)
-    block_out, up_part, down_part = lax.optimization_barrier((block_out, up_part, down_part))
+    block_out, up_part, kernel_part = lax.optimization_barrier((block_out, up_part, kernel_part))
+    kernel_grad = summed_line(kernel_part + other_row(kernel_part))
     up_half = scatter_line(up_part)
     down_grad = sum_rows(down_part)
     up_grad = scatter_last(up_half)

time: 241 us -> 249 us (1.033)
  waiting for transfers between devices: 90.7 us -> 107 us
  local copies, waits for them, and re-layouts: 24.2 us -> 19.4 us
  other arithmetic: 32.8 us -> 29.7 us
    ppermute x2, waiting for transfers between devices: 0.01 us -> 7.03 us  [padded_2(): lax.ppermute(lax.slice_in_dim(block, 0, width, axis=dim), axis, backward)]
    ppermute x17 -> x22, waiting for transfers between devices: 76 us -> 82.5 us  [partner(): return lax.ppermute(values, 'dp', [(i, i ^ bit) for i in range(count)])]
    ppermute x17 -> x22, starting transfers between devices: 19.8 us -> 24 us  [partner(): return lax.ppermute(values, 'dp', [(i, i ^ bit) for i in range(count)])]
    ppermute x6 -> x7, waiting for transfers between devices: 6.22 us -> 9.75 us  [other_row(): return lax.ppermute(values, 'rows', [(0, 1), (1, 0)])]
    ppermute x2, starting transfers between devices: 10.4 us -> 7.86 us  [padded_2(): lax.ppermute(lax.slice_in_dim(block, block.shape[dim] - width, None, axis...]
    ppermute x6 -> x7, starting transfers between devices: 5.78 us -> 4.34 us  [other_row(): return lax.ppermute(values, 'rows', [(0, 1), (1, 0)])]
    unnamed x48 -> x54, local copies, waits for them, and re-layouts: 8.34 us -> 8.63 us
  transfers between devices with their start and end apart: 29 -> 34, of which waited for: 10 -> 18; matrix products, arithmetic and copies ran while one was open for 22% -> 18% of each run, Pallas kernels for 5% -> 5%
where the time goes in v5:
time: 249 us; the launch traced here: 248 us
  waiting for transfers between devices  107 us (43%)
  starting transfers between devices  38.8 us (16%)
  other arithmetic  29.7 us (12%)
  matrix products  21 us (8%)
  local copies, waits for them, and re-layouts  19.4 us (8%)
  Pallas kernels  17.4 us (7%)
  between operations  15.5 us (6%)
    ppermute x22, waiting for transfers between devices, partner(): return lax.ppermute(values, 'dp', [(i, i ^ bit) for i in range(count)])  82.5 us
    ppermute x22, starting transfers between devices, partner(): return lax.ppermute(values, 'dp', [(i, i ^ bit) for i in range(count)])  24 us
    pallas_call x2, Pallas kernels, depthwise(): pl.pallas_call(functools.partial(depthwise_kernel, flipped), grid=(images...  12 us
    ppermute x7, waiting for transfers between devices, other_row(): return lax.ppermute(values, 'rows', [(0, 1), (1, 0)])  9.75 us
    unnamed x54, local copies, waits for them, and re-layouts  8.63 us
    ppermute x2, starting transfers between devices, padded_2(): lax.ppermute(lax.slice_in_dim(block, block.shape[dim] - width, None, axis...  7.86 us
    ppermute x2, waiting for transfers between devices, padded_2(): lax.ppermute(lax.slice_in_dim(block, 0, width, axis=dim), axis, backward)  7.03 us
    all_gather x1, waiting for transfers between devices, on_device(): up_full = lax.all_gather(up_weight, 'dp', axis=0, tiled=True)  6.54 us
  transfers between devices with their start and end apart: 34, of which 18 were waited for; matrix products, arithmetic and copies ran while one was open for 18% of the time, Pallas kernels for 5%

profile of v5, /device:TPU:0, one launch (start us, length us, event | category | flops | bytes accessed | tf_op | source)
XLA Modules:
  0.0 248.3 jit_solution(5749563352573658813)
XLA Ops:
  8.8 3.1 %collective-permute-start.4 = (bf16[176,384]{1,0:T(8,128)(2,1)S(1)}, bf16[176,384]{1,0:T(8,128)(2,1)S(1)}, u32[]{:S(2)}, u32[]{:S(2)}) collective-permute-start(bf16[176,384]{1,0:T(8,128)(2,1)S(1)} %constant_dynamic-slice_fusion.4), channel_id=1, source_target_pairs={{0,8},{2,10},{4,12},{6,14},{8,0},{10,2},{12,4},{14,6},{16,24},{18,... | collective-permute-start | bytes 405512 | tf_op jit(solution)/shard_map/ppermute | solution.py:133
  11.9 2.6 %collective-permute-start.3 = (bf16[176,384]{1,0:T(8,128)(2,1)S(1)}, bf16[176,384]{1,0:T(8,128)(2,1)S(1)}, u32[]{:S(2)}, u32[]{:S(2)}) collective-permute-start(bf16[176,384]{1,0:T(8,128)(2,1)S(1)} %constant_dynamic-slice_fusion.4), channel_id=1, source_target_pairs={{0,16},{2,18},{4,20},{6,22},{8,24},{10,26},{12,28},{14,30},{16,0},... | collective-permute-start | bytes 405512 | tf_op jit(solution)/shard_map/ppermute | solution.py:133
  17.8 3.6 %collective-permute-start = (bf16[1,3,32,768]{3,2,1,0:T(8,128)(2,1)S(1)}, bf16[1,3,32,768]{3,2,1,0:T(8,128)(2,1)S(1)}, u32[]{:S(2)}, u32[]{:S(2)}) collective-permute-start(bf16[1,3,32,768]{3,2,1,0:T(8,128)(2,1)S(1)} %get-tuple-element.75), channel_id=1, source_target_pairs={{0,1},{2,3},{4,5},{6,7},{8,9},{10,11},{12,13},{14,15},{16,17},{18,... | collective-permute-start | bytes 442376 | tf_op jit(solution)/shard_map/ppermute | solution.py:20
  25.5 2.9 %collective-permute-done.1 = bf16[1,3,32,768]{3,2,1,0:T(8,128)(2,1)S(1)} collective-permute-done((bf16[1,3,32,768]{3,2,1,0:T(8,128)(2,1)S(1)}, bf16[1,3,32,768]{3,2,1,0:T(8,128)(2,1)S(1)}, u32[]{:S(2)}, u32[]{:S(2)}) %collective-permute-start.1) | collective-permute-done | bytes 147488 | tf_op jit(solution)/shard_map/ppermute | solution.py:23
  33.6 5.9 %shard_map.101 = f32[1,16,32,768]{3,2,1,0:T(8,128)S(1)} custom-call(f32[1,22,38,768]{3,2,1,0:T(8,128)S(1)} %copy-done, f32[7,7,768]{2,1,0:T(8,128)S(1)} %copy-done.2), custom_call_target="tpu_custom_call" | custom-call | flops 38535168 | bytes 2568192 | tf_op jit(solution)/shard_map/pallas_call | solution.py:65
  43.0 8.8 %collective-permute-done.7 = bf16[2,2,176,384]{3,2,0,1:T(8,128)(2,1)S(1)} collective-permute-done((bf16[2,2,176,384]{3,2,0,1:T(8,128)(2,1)S(1)}, bf16[2,2,176,384]{3,2,0,1:T(8,128)(2,1)S(1)}, u32[]{:S(2)}, u32[]{:S(2)}) %collective-permute-start.7) | collective-permute-done | bytes 540704 | tf_op jit(solution)/shard_map/ppermute | solution.py:137
  51.8 12.9 %collective-permute-done.8 = bf16[2,176,768]{2,1,0:T(8,128)(2,1)S(1)} collective-permute-done((bf16[2,176,768]{2,1,0:T(8,128)(2,1)S(1)}, bf16[2,176,768]{2,1,0:T(8,128)(2,1)S(1)}, u32[]{:S(2)}, u32[]{:S(2)}) %collective-permute-start.8) | collective-permute-done | bytes 540704 | tf_op jit(solution)/shard_map/ppermute | solution.py:133
  67.7 6.5 %all-gather.2.cloned.1.call-done = bf16[768,2816]{1,0:T(8,128)(2,1)} async-done(((bf16[48,2816]{1,0:T(8,128)(2,1)}), bf16[768,2816]{1,0:T(8,128)(2,1)}) %all-gather.2.cloned.1.call-update) | async-done | bytes 4325392 | tf_op jit(solution)/shard_map/all_gather | solution.py:261
  74.2 6.4 %multiply_convert_fusion.2 = (bf16[512,2816]{1,0:T(8,128)(2,1)S(1)}, f32[512,2816]{1,0:T(8,128)}) fusion(bf16[512,768]{1,0:T(8,128)(2,1)} %bitcast.116, bf16[768,2816]{1,0:T(8,128)(2,1)} %all-gather.2.cloned.1.call-done), kind=kOutput, calls=%fused_computation.9 | convolution fusion | flops 2221801472 | bytes 13762560 | tf_op jit(solution)/shard_map/dot_general | solution.py:276
  89.4 2.6 %slice-done.6 = s8[4194304]{0:T(1024)(128)(4,1)S(1)} async-done(((s8[5767168]{0:T(1024)(128)(4,1)}), s8[4194304]{0:T(1024)(128)(4,1)S(1)}, s32[]{:S(2)}) %slice-start.6) | async-done | bytes 4194328
  93.3 3.9 %fusion.5 = bf16[512,2816]{1,0:T(8,128)(2,1)S(1)} fusion(f32[512,2816]{1,0:T(8,128)S(1)} %bitcast.122, bf16[512,768]{1,0:T(8,128)(2,1)S(1)} %bitcast.115, bf16[2816,768]{1,0:T(8,128)(2,1)S(1)} %bitcast.108), kind=kOutput, calls=%fused_computation.8 | convolution fusion | flops 2229010432 | bytes 13762560 | tf_op jit(solution)/shard_map/dot_general | solution.py:286
  97.2 4.3 %convert_add_fusion = f32[4,2,176,768]{3,2,0,1:T(8,128)} fusion(bf16[4,2,176,768]{3,2,0,1:T(8,128)(2,1)} %collective-permute-done.10, bf16[4,2,1,176,768]{4,3,2,1,0:T(8,128)(2,1)S(1)} %copy-done.4), kind=kLoop, calls=%fused_computation.12 | loop fusion | flops 3244032 | bytes 8650752 | tf_op jit(solution)/shard_map/add | solution.py:290
  115.0 22.8 %collective-permute-done.14 = bf16[4,176,768]{2,1,0:T(8,128)(2,1)S(1)} collective-permute-done((bf16[4,176,768]{2,1,0:T(8,128)(2,1)S(1)}, bf16[4,176,768]{2,1,0:T(8,128)(2,1)S(1)}, u32[]{:S(2)}, u32[]{:S(2)}) %collective-permute-start.14) | collective-permute-done | bytes 1081376 | tf_op jit(solution)/shard_map/ppermute | solution.py:133
  144.0 5.4 %shard_map.102 = f32[1,49,8,768]{3,2,1,0:T(8,128)S(1)} custom-call(f32[1,16,32,768]{3,2,1,0:T(8,128)S(1)} %multiply_select_fusion.grad_ref, f32[1,22,38,768]{3,2,1,0:T(8,128)S(1)} %copy-done.1), custom_call_target="tpu_custom_call" | custom-call | flops 38535168 | bytes 2568192 | tf_op jit(solution)/shard_map/pallas_call | solution.py:102
  151.1 4.2 %collective-permute-start.12 = (bf16[1,3,32,768]{3,2,1,0:T(8,128)(2,1)}, bf16[1,3,32,768]{3,2,1,0:T(8,128)(2,1)}, u32[]{:S(2)}, u32[]{:S(2)}) collective-permute-start(bf16[1,3,32,768]{3,2,1,0:T(8,128)(2,1)} %get-tuple-element.73), channel_id=1, source_target_pairs={{0,1},{2,3},{4,5},{6,7},{8,9},{10,11},{12,13},{14,15},{16,17},{18,... | collective-permute-start | bytes 442376 | tf_op jit(solution)/shard_map/ppermute | solution.py:20
  158.6 4.1 %collective-permute-done.13 = bf16[1,3,32,768]{3,2,1,0:T(8,128)(2,1)} collective-permute-done((bf16[1,3,32,768]{3,2,1,0:T(8,128)(2,1)}, bf16[1,3,32,768]{3,2,1,0:T(8,128)(2,1)}, u32[]{:S(2)}, u32[]{:S(2)}) %collective-permute-start.13) | collective-permute-done | bytes 147488 | tf_op jit(solution)/shard_map/ppermute | solution.py:23
  164.4 6.1 %shard_map.103 = f32[1,16,32,768]{3,2,1,0:T(8,128)S(1)} custom-call(f32[1,22,38,768]{3,2,1,0:T(8,128)S(1)} %pad.9.padded_ref, f32[7,7,768]{2,1,0:T(8,128)S(1)} %copy-done.2), custom_call_target="tpu_custom_call" | custom-call | flops 38535168 | bytes 2568192 | tf_op jit(solution)/shard_map/pallas_call | solution.py:65
  177.2 3.7 %collective-permute-done.15 = bf16[176,768]{1,0:T(8,128)(2,1)S(1)} collective-permute-done((bf16[176,768]{1,0:T(8,128)(2,1)S(1)}, bf16[176,768]{1,0:T(8,128)(2,1)S(1)}, u32[]{:S(2)}, u32[]{:S(2)}) %collective-permute-start.15) | collective-permute-done | bytes 270368 | tf_op jit(solution)/shard_map/ppermute | solution.py:133
  180.9 7.3 %collective-permute-done.17 = bf16[176,768]{1,0:T(8,128)(2,1)S(1)} collective-permute-done((bf16[176,768]{1,0:T(8,128)(2,1)S(1)}, bf16[176,768]{1,0:T(8,128)(2,1)S(1)}, u32[]{:S(2)}, u32[]{:S(2)}) %collective-permute-start.17) | collective-permute-done | bytes 270368 | tf_op jit(solution)/shard_map/ppermute | solution.py:133
  188.2 11.3 %collective-permute-done.16 = bf16[176,768]{1,0:T(8,128)(2,1)S(1)} collective-permute-done((bf16[176,768]{1,0:T(8,128)(2,1)S(1)}, bf16[176,768]{1,0:T(8,128)(2,1)S(1)}, u32[]{:S(2)}, u32[]{:S(2)}) %collective-permute-start.16) | collective-permute-done | bytes 270368 | tf_op jit(solution)/shard_map/ppermute | solution.py:133
  202.2 3.3 %fusion.7 = bf16[1,16,32,768]{3,2,1,0:T(8,128)(2,1)} fusion(bf16[1,16,32,768]{3,2,1,0:T(8,128)(2,1)S(1)} %copy-done.10, bf16[16,32,2816]{2,1,0:T(8,128)(2,1)S(1)} %bitcast.120, bf16[2816,768,1]{1,0,2:T(8,128)(2,1)S(1)} %bitcast.111), kind=kOutput, calls=%fused_computation.30 | convolution fusion | flops 2215772160 | bytes 8781824 | tf_op jit(solution)/shard_map/dot_general | solution.py:329
  208.3 2.8 %collective-permute-done.21 = bf16[2,48,1408]{2,1,0:T(8,128)(2,1)S(1)} collective-permute-done((bf16[2,48,1408]{2,1,0:T(8,128)(2,1)S(1)}, bf16[2,48,1408]{2,1,0:T(8,128)(2,1)S(1)}, u32[]{:S(2)}, u32[]{:S(2)}) %collective-permute-start.21) | collective-permute-done | bytes 270368 | tf_op jit(solution)/shard_map/ppermute | solution.py:133
  219.8 5.1 %collective-permute-done.25 = bf16[48,1408]{1,0:T(8,128)(2,1)S(1)} collective-permute-done((bf16[48,1408]{1,0:T(8,128)(2,1)S(1)}, bf16[48,1408]{1,0:T(8,128)(2,1)S(1)}, u32[]{:S(2)}, u32[]{:S(2)}) %collective-permute-start.25) | collective-permute-done | bytes 135200 | tf_op jit(solution)/shard_map/ppermute | solution.py:133
  232.7 8.0 %collective-permute-done.31 = f32[7,7,768]{2,1,0:T(8,128)S(1)} collective-permute-done((f32[7,7,768]{2,1,0:T(8,128)S(1)}, f32[7,7,768]{2,1,0:T(8,128)S(1)}, u32[]{:S(2)}, u32[]{:S(2)}) %collective-permute-start.31) | collective-permute-done | bytes 150560 | tf_op jit(solution)/shard_map/ppermute | solution.py:133
  (179 shorter events, 85.2 us)
Async XLA Ops:
  7.2 67.0 %all-gather.2.cloned.1.call-start = ((), (), s32[]{:S(2)}) async-start(), calls=%async_computation | async-start | bytes 4595712 | tf_op jit(solution)/shard_map/all_gather | solution.py:261
  8.8 13.9 %collective-permute-start.4 = (bf16[176,384]{1,0:T(8,128)(2,1)S(1)}, bf16[176,384]{1,0:T(8,128)(2,1)S(1)}, u32[]{:S(2)}, u32[]{:S(2)}) collective-permute-start(bf16[176,384]{1,0:T(8,128)(2,1)S(1)} %constant_dynamic-slice_fusion.4), channel_id=1, source_target_pairs={{0,8},{2,10},{4,12},{6,14},{8,0},{10,2},{12,4},{14,6},{16,24},{18,... | collective-permute-start | bytes 405512 | tf_op jit(solution)/shard_map/ppermute | solution.py:133
  11.9 13.3 %collective-permute-start.3 = (bf16[176,384]{1,0:T(8,128)(2,1)S(1)}, bf16[176,384]{1,0:T(8,128)(2,1)S(1)}, u32[]{:S(2)}, u32[]{:S(2)}) collective-permute-start(bf16[176,384]{1,0:T(8,128)(2,1)S(1)} %constant_dynamic-slice_fusion.4), channel_id=1, source_target_pairs={{0,16},{2,18},{4,20},{6,22},{8,24},{10,26},{12,28},{14,30},{16,0},... | collective-permute-start | bytes 405512 | tf_op jit(solution)/shard_map/ppermute | solution.py:133
  14.5 10.7 %collective-permute-start.2 = (bf16[176,384]{1,0:T(8,128)(2,1)S(1)}, bf16[176,384]{1,0:T(8,128)(2,1)S(1)}, u32[]{:S(2)}, u32[]{:S(2)}) collective-permute-start(bf16[176,384]{1,0:T(8,128)(2,1)S(1)} %constant_dynamic-slice_fusion.4), channel_id=1, source_target_pairs={{0,24},{2,26},{4,28},{6,30},{8,16},{10,18},{12,20},{14,22},{16,8},... | collective-permute-start | bytes 405512 | tf_op jit(solution)/shard_map/ppermute | solution.py:133
  30.3 9.2 %collective-permute-start.5 = (bf16[2,176,384]{2,1,0:T(8,128)(2,1)S(1)}, bf16[2,176,384]{2,1,0:T(8,128)(2,1)S(1)}, u32[]{:S(2)}, u32[]{:S(2)}) collective-permute-start(bf16[2,176,384]{2,1,0:T(8,128)(2,1)S(1)} %get-tuple-element.31), channel_id=1, source_target_pairs={{0,4},{2,6},{4,0},{6,2},{8,12},{10,14},{12,8},{14,10},{16,20},{18,... | collective-permute-start | bytes 811016 | tf_op jit(solution)/shard_map/ppermute | solution.py:133
  39.7 12.0 %collective-permute-start.7 = (bf16[2,2,176,384]{3,2,0,1:T(8,128)(2,1)S(1)}, bf16[2,2,176,384]{3,2,0,1:T(8,128)(2,1)S(1)}, u32[]{:S(2)}, u32[]{:S(2)}) collective-permute-start(bf16[2,2,176,384]{3,2,0,1:T(8,128)(2,1)S(1)} %pad_maximum_fusion.2), channel_id=1, source_target_pairs={{0,1},{1,0},{2,3},{3,2},{4,5},{5,4},{6,7},{7,6},{8,9},{9,8},{10,11... | collective-permute-start | bytes 1622024 | tf_op jit(solution)/shard_map/ppermute | solution.py:137
  41.8 23.0 %collective-permute-start.8 = (bf16[2,176,768]{2,1,0:T(8,128)(2,1)S(1)}, bf16[2,176,768]{2,1,0:T(8,128)(2,1)S(1)}, u32[]{:S(2)}, u32[]{:S(2)}) collective-permute-start(bf16[2,176,768]{2,1,0:T(8,128)(2,1)S(1)} %pad_maximum_fusion.3), channel_id=1, source_target_pairs={{0,4},{2,6},{4,0},{6,2},{8,12},{10,14},{12,8},{14,10},{16,20},{18,... | collective-permute-start | bytes 1622024 | tf_op jit(solution)/shard_map/ppermute | solution.py:133
  66.5 20.1 %collective-permute-start.9 = (bf16[4,2,176,768]{3,2,0,1:T(8,128)(2,1)}, bf16[4,2,176,768]{3,2,0,1:T(8,128)(2,1)}, u32[]{:S(2)}, u32[]{:S(2)}) collective-permute-start(bf16[4,2,176,768]{3,2,0,1:T(8,128)(2,1)} %maximum_maximum_fusion), channel_id=1, source_target_pairs={{0,2},{2,0},{4,6},{6,4},{8,10},{10,8},{12,14},{14,12},{16,18},{18,... | collective-permute-start | bytes 6488072 | tf_op jit(solution)/shard_map/ppermute | solution.py:133
  86.3 10.8 %collective-permute-start.10 = (bf16[4,2,176,768]{3,2,0,1:T(8,128)(2,1)}, bf16[4,2,176,768]{3,2,0,1:T(8,128)(2,1)}, u32[]{:S(2)}, u32[]{:S(2)}) collective-permute-start(bf16[4,2,176,768]{3,2,0,1:T(8,128)(2,1)} %bitcast.104), channel_id=1, source_target_pairs={{0,2},{2,0},{4,6},{6,4},{8,10},{10,8},{12,14},{14,12},{16,18},{18,... | collective-permute-start | bytes 6488072 | tf_op jit(solution)/shard_map/ppermute | solution.py:133
  107.1 32.3 %collective-permute-start.11 = (bf16[4,2,48,2816]{3,2,0,1:T(8,128)(2,1)}, bf16[4,2,48,2816]{3,2,0,1:T(8,128)(2,1)}, u32[]{:S(2)}, u32[]{:S(2)}) collective-permute-start(bf16[4,2,48,2816]{3,2,0,1:T(8,128)(2,1)} %bitcast.103), channel_id=1, source_target_pairs={{0,2},{2,0},{4,6},{6,4},{8,10},{10,8},{12,14},{14,12},{16,18},{18,... | collective-permute-start | bytes 6488072 | tf_op jit(solution)/shard_map/ppermute | solution.py:133
  111.7 26.1 %collective-permute-start.14 = (bf16[4,176,768]{2,1,0:T(8,128)(2,1)S(1)}, bf16[4,176,768]{2,1,0:T(8,128)(2,1)S(1)}, u32[]{:S(2)}, u32[]{:S(2)}) collective-permute-start(bf16[4,176,768]{2,1,0:T(8,128)(2,1)S(1)} %fusion.14), channel_id=1, source_target_pairs={{0,4},{2,6},{4,0},{6,2},{8,12},{10,14},{12,8},{14,10},{16,20},{18,... | collective-permute-start | bytes 3244040 | tf_op jit(solution)/shard_map/ppermute | solution.py:133
  164.1 13.0 %collective-permute-start.20 = (f32[7,7,768]{2,1,0:T(8,128)S(1)}, f32[7,7,768]{2,1,0:T(8,128)S(1)}, u32[]{:S(2)}, u32[]{:S(2)}) collective-permute-start(f32[7,7,768]{2,1,0:T(8,128)S(1)} %mul.126), channel_id=1, source_target_pairs={{0,2},{2,0},{4,6},{6,4},{8,10},{10,8},{12,14},{14,12},{16,18},{18,... | collective-permute-start | bytes 451592 | tf_op jit(solution)/shard_map/ppermute | solution.py:133
  170.7 28.9 %collective-permute-start.19 = (bf16[2,48,2816]{2,1,0:T(8,128)(2,1)S(1)}, bf16[2,48,2816]{2,1,0:T(8,128)(2,1)S(1)}, u32[]{:S(2)}, u32[]{:S(2)}) collective-permute-start(bf16[2,48,2816]{2,1,0:T(8,128)(2,1)S(1)} %fusion.16), channel_id=1, source_target_pairs={{0,4},{2,6},{4,0},{6,2},{8,12},{10,14},{12,8},{14,10},{16,20},{18,... | collective-permute-start | bytes 1622024 | tf_op jit(solution)/shard_map/ppermute | solution.py:133
  172.2 8.7 %collective-permute-start.15 = (bf16[176,768]{1,0:T(8,128)(2,1)S(1)}, bf16[176,768]{1,0:T(8,128)(2,1)S(1)}, u32[]{:S(2)}, u32[]{:S(2)}) collective-permute-start(bf16[176,768]{1,0:T(8,128)(2,1)S(1)} %get-tuple-element.63), channel_id=1, source_target_pairs={{0,8},{2,10},{4,12},{6,14},{8,0},{10,2},{12,4},{14,6},{16,24},{18,... | collective-permute-start | bytes 811016 | tf_op jit(solution)/shard_map/ppermute | solution.py:133
  173.3 15.0 %collective-permute-start.17 = (bf16[176,768]{1,0:T(8,128)(2,1)S(1)}, bf16[176,768]{1,0:T(8,128)(2,1)S(1)}, u32[]{:S(2)}, u32[]{:S(2)}) collective-permute-start(bf16[176,768]{1,0:T(8,128)(2,1)S(1)} %get-tuple-element.64), channel_id=1, source_target_pairs={{0,24},{2,26},{4,28},{6,30},{8,16},{10,18},{12,20},{14,22},{16,8},... | collective-permute-start | bytes 811016 | tf_op jit(solution)/shard_map/ppermute | solution.py:133
  175.0 24.4 %collective-permute-start.16 = (bf16[176,768]{1,0:T(8,128)(2,1)S(1)}, bf16[176,768]{1,0:T(8,128)(2,1)S(1)}, u32[]{:S(2)}, u32[]{:S(2)}) collective-permute-start(bf16[176,768]{1,0:T(8,128)(2,1)S(1)} %get-tuple-element.65), channel_id=1, source_target_pairs={{0,16},{2,18},{4,20},{6,22},{8,24},{10,26},{12,28},{14,30},{16,0},... | collective-permute-start | bytes 811016 | tf_op jit(solution)/shard_map/ppermute | solution.py:133
  177.1 22.7 %collective-permute-start.18 = (bf16[2,2,48,1408]{3,2,0,1:T(8,128)(2,1)S(1)}, bf16[2,2,48,1408]{3,2,0,1:T(8,128)(2,1)S(1)}, u32[]{:S(2)}, u32[]{:S(2)}) collective-permute-start(bf16[2,2,48,1408]{3,2,0,1:T(8,128)(2,1)S(1)} %dynamic-slice_convert_fusion.2), channel_id=1, source_target_pairs={{0,1},{1,0},{2,3},{3,2},{4,5},{5,4},{6,7},{7,6},{8,9},{9,8},{10,11... | collective-permute-start | bytes 1622024 | tf_op jit(solution)/shard_map/ppermute | solution.py:137
  200.9 10.2 %collective-permute-start.21 = (bf16[2,48,1408]{2,1,0:T(8,128)(2,1)S(1)}, bf16[2,48,1408]{2,1,0:T(8,128)(2,1)S(1)}, u32[]{:S(2)}, u32[]{:S(2)}) collective-permute-start(bf16[2,48,1408]{2,1,0:T(8,128)(2,1)S(1)} %fusion.22), channel_id=1, source_target_pairs={{0,4},{2,6},{4,0},{6,2},{8,12},{10,14},{12,8},{14,10},{16,20},{18,... | collective-permute-start | bytes 811016 | tf_op jit(solution)/shard_map/ppermute | solution.py:133
  211.4 8.4 %collective-permute-start.26 = (bf16[48,1408]{1,0:T(8,128)(2,1)S(1)}, bf16[48,1408]{1,0:T(8,128)(2,1)S(1)}, u32[]{:S(2)}, u32[]{:S(2)}) collective-permute-start(bf16[48,1408]{1,0:T(8,128)(2,1)S(1)} %get-tuple-element.67), channel_id=1, source_target_pairs={{0,24},{2,26},{4,28},{6,30},{8,16},{10,18},{12,20},{14,22},{16,8},... | collective-permute-start | bytes 405512 | tf_op jit(solution)/shard_map/ppermute | solution.py:133
  213.0 11.9 %collective-permute-start.25 = (bf16[48,1408]{1,0:T(8,128)(2,1)S(1)}, bf16[48,1408]{1,0:T(8,128)(2,1)S(1)}, u32[]{:S(2)}, u32[]{:S(2)}) collective-permute-start(bf16[48,1408]{1,0:T(8,128)(2,1)S(1)} %get-tuple-element.68), channel_id=1, source_target_pairs={{0,16},{2,18},{4,20},{6,22},{8,24},{10,26},{12,28},{14,30},{16,0},... | collective-permute-start | bytes 405512 | tf_op jit(solution)/shard_map/ppermute | solution.py:133
  214.9 10.2 %collective-permute-start.28 = (bf16[176,768]{1,0:T(8,128)(2,1)S(1)}, bf16[176,768]{1,0:T(8,128)(2,1)S(1)}, u32[]{:S(2)}, u32[]{:S(2)}) collective-permute-start(bf16[176,768]{1,0:T(8,128)(2,1)S(1)} %fusion.18), channel_id=1, source_target_pairs={{0,1},{1,0},{2,3},{3,2},{4,5},{5,4},{6,7},{7,6},{8,9},{9,8},{10,11... | collective-permute-start | bytes 811016 | tf_op jit(solution)/shard_map/ppermute | solution.py:137
  214.9 11.1 %collective-permute-start.29 = (f32[7,7,768]{2,1,0:T(8,128)S(1)}, f32[7,7,768]{2,1,0:T(8,128)S(1)}, u32[]{:S(2)}, u32[]{:S(2)}) collective-permute-start(f32[7,7,768]{2,1,0:T(8,128)S(1)} %add.223), channel_id=1, source_target_pairs={{0,1},{1,0},{2,3},{3,2},{4,5},{5,4},{6,7},{7,6},{8,9},{9,8},{10,11... | collective-permute-start | bytes 451592 | tf_op jit(solution)/shard_map/ppermute | solution.py:137
  226.0 14.7 %collective-permute-start.31 = (f32[7,7,768]{2,1,0:T(8,128)S(1)}, f32[7,7,768]{2,1,0:T(8,128)S(1)}, u32[]{:S(2)}, u32[]{:S(2)}) collective-permute-start(f32[7,7,768]{2,1,0:T(8,128)S(1)} %add.228), channel_id=1, source_target_pairs={{0,16},{2,18},{4,20},{6,22},{8,24},{10,26},{12,28},{14,30},{16,0},... | collective-permute-start | bytes 451592 | tf_op jit(solution)/shard_map/ppermute | solution.py:133
  228.4 12.3 %collective-permute-start.30 = (f32[7,7,768]{2,1,0:T(8,128)S(1)}, f32[7,7,768]{2,1,0:T(8,128)S(1)}, u32[]{:S(2)}, u32[]{:S(2)}) collective-permute-start(f32[7,7,768]{2,1,0:T(8,128)S(1)} %add.228), channel_id=1, source_target_pairs={{0,24},{2,26},{4,28},{6,30},{8,16},{10,18},{12,20},{14,22},{16,8},... | collective-permute-start | bytes 451592 | tf_op jit(solution)/shard_map/ppermute | solution.py:133
  (37 other events, 301.9 us)
Sparse Core Ops, SparseCore 0:
  10.3 63.8 all-gather.1
